TPU v7x, 32 devices: a whole 2x2x4 slice. The times are simulated.
32 devices in a mesh: row: 4 (over x, core), col: 2 (over y), basis: 4 (over z).
Axes of the slice: x: 2, y: 2, z: 4, core: 2. Of those that a mesh axis runs over, the one named last changes fastest.
Arguments:
- block_data: bfloat16 [256, 128, 128], P(('row', 'col', 'basis')), may hold values from -1.1953125 to 1.1953125
- item_pairs: int32 [256, 2], P(('row', 'col', 'basis')), may hold values from 0 to 1023
- dest_slot: int32 [256], P(('row', 'col', 'basis')), may hold values from 0 to 7, as said below
- brick_tag: int32 [256], P(('row', 'col', 'basis')), may hold values from 0 to 7
- centres: float32 [1024, 3, 128], replicated, may hold values from -1.5 to 1.5
- exponents: float32 [1024, 128], replicated, may hold values from 4 to 12
- levels: int32 [64], replicated, may hold values 0 or 1
- cell_pos: int32 [64, 256], P(('row', 'col', 'basis')), may hold values from 0 to 4095, as said below
- corner_refs: int32 [64, 256, 8], P(('row', 'col', 'basis')), may hold values from 0 to 511, as said below
Outputs:
- density: float32 [64, 4096], P(('row', 'col', 'basis'))
Inputs may be any that keep to these rules, and one draw needn't show every extreme that they name: `dest_slot`: on the rows of one device the values are distinct; value v sends the row to brick group v. `cell_pos`: within one brick the cells are distinct, one in each run of 16 consecutive points. `corner_refs`: index v names corner v % 8 of brick v // 8; every index occurs 256 times.
All inputs are finite; a program needn't handle non-finite values.
Results may differ from a plain program's by a relative error of at most 0.0028.
Values sent between devices are 32-bit elements; how exact they have to be, the bound alone decides.
No kernel may reach another device: no remote copies, remote signals or barrier semaphores. Data moves between devices by JAX's collectives and lax.ppermute only.
A program may use at most 64 MiB of HBM per device.

v0:
```python
import jax
import jax.numpy as jnp
from jax import lax
from jax.sharding import PartitionSpec as P

EDGE = 16


coarse_spacing = 0.2


def basis_values(centres, exponents, block_index, level_value, edge_points):
    spacing = coarse_spacing * jnp.exp2(-level_value.astype(jnp.float32))
    coords = (jnp.arange(edge_points, dtype=jnp.float32) - (edge_points - 1) / 2.0) * spacing
    middle = centres[block_index]
    decay_rates = exponents[block_index]
    factor = jnp.exp(
        -decay_rates[None, :, None] * (coords[None, None, :] - middle[:, :, None]) ** 2
    )
    values_grid = (
        factor[0][:, :, None, None] * factor[1][:, None, :, None] * factor[2][:, None, None, :]
    )
    return values_grid.reshape(decay_rates.shape[0], edge_points * edge_points * edge_points)


def pair_density(block_values, pair_index, level_value, centres, exponents, edge_points):
    row_values = basis_values(centres, exponents, pair_index[0], level_value, edge_points)
    col_values = basis_values(centres, exponents, pair_index[1], level_value, edge_points).astype(
        jnp.bfloat16
    )
    product = jnp.dot(block_values, col_values, preferred_element_type=jnp.float32)
    return jnp.sum(row_values * product, axis=0)


def corner_points(edge_points):
    corner_code = jnp.arange(8, dtype=jnp.int32)
    first = corner_code // 4 * (edge_points - 1)
    second = corner_code // 2 % 2 * (edge_points - 1)
    third = corner_code % 2 * (edge_points - 1)
    return (first * edge_points + second) * edge_points + third


def body(
    block_data, item_pairs, dest_slot, brick_tag, centres, exponents, levels, cell_pos, corner_refs
):
    row_count = lax.axis_size("row")
    col_count = lax.axis_size("col")
    group_count = row_count * col_count
    item_count = block_data.shape[0]
    slot_depth = max(1, item_count // group_count)
    slot_count = group_count * slot_depth
    bricks_group = levels.shape[0] // group_count
    point_count = EDGE * EDGE * EDGE
    target = dest_slot // slot_depth * bricks_group + brick_tag
    item_level = levels[target]

    def single(operands):
        return pair_density(operands[0], operands[1], operands[2], centres, exponents, EDGE)

    densities = lax.map(single, (block_data, item_pairs, item_level))
    outgoing = jnp.zeros((slot_count, point_count), jnp.float32).at[dest_slot].set(densities)
    slot_tags = (
        jnp.zeros((slot_count,), jnp.float32).at[dest_slot].set(brick_tag.astype(jnp.float32))
    )
    arrived, arrived_tags = (
        lax.all_to_all(outgoing, ("row", "col"), split_axis=0, concat_axis=0, tiled=True),
        lax.all_to_all(slot_tags, ("row", "col"), split_axis=0, concat_axis=0, tiled=True),
    )
    selector = (
        arrived_tags[None, :] == jnp.arange(bricks_group, dtype=jnp.float32)[:, None]
    ).astype(jnp.float32)
    partial_sum = jnp.dot(selector, arrived, precision=lax.Precision.HIGHEST)
    own_density = lax.psum_scatter(partial_sum, "basis", scatter_dimension=0, tiled=True)
    corner_values = own_density[:, corner_points(EDGE)]
    all_corners = lax.all_gather(
        corner_values, ("row", "col", "basis"), axis=0, tiled=True
    ).reshape(-1)
    corner_mean = jnp.mean(all_corners[corner_refs], axis=-1)
    current = jnp.take_along_axis(own_density, cell_pos, axis=1)
    brick_rows = jnp.arange(own_density.shape[0], dtype=jnp.int32)[:, None]
    return own_density.at[brick_rows, cell_pos].set(0.5 * current + 0.5 * corner_mean)


def solution(mesh):
    return jax.shard_map(
        body,
        mesh=mesh,
        in_specs=(
            P(("row", "col", "basis"), None, None),
            P(("row", "col", "basis"), None),
            P(("row", "col", "basis")),
            P(("row", "col", "basis")),
            P(),
            P(),
            P(),
            P(("row", "col", "basis"), None),
            P(("row", "col", "basis"), None, None),
        ),
        out_specs=P(("row", "col", "basis"), None),
        check_vma=False,
    )
```

profile of v0, /device:TPU:0, one launch (start us, length us, event | category | flops | bytes accessed | tf_op | source)
XLA Modules:
  0.0 337.5 jit_solution(8755111716584597181)
XLA Ops:
  8.6 5.2 %all-to-all-start = ((f32[8,1,1]{2,1,0:T(1,128)}), f32[8,1,1]{2,1,0:T(1,128)S(1)}, u32[]{:S(2)}, u32[]{:S(2)}) async-start(f32[8,1,1]{2,1,0:T(1,128)} %copy.25), calls=%async_computation | async-start | bytes 8192 | tf_op jit(solution)/shard_map/all_to_all | solution.py:67
  13.7 3.8 %copy.26 = f32[1024,3,128]{2,1,0:T(4,128)} copy(f32[1024,3,128]{2,0,1:T(8,128)} %param.15) | data formatting | bytes 3145728 | tf_op jit(solution)/shard_map/while | solution.py:60
  18.3 100.9 %while.13 = (s32[]{:T(128)}, f32[8,4096]{1,0:T(8,128)S(1)}, s32[8,2]{0,1:T(2,128)S(1)}, f32[1024,128]{1,0:T(8,128)}, s32[8]{0:T(128)S(1)}, /*index=5*/f32[1024,3...) while((s32[]{:T(128)}, f32[8,4096]{1,0:T(8,128)S(1)}, ...), condition=%wide.region_3.4_spmd.clone, body=%wide.region_1.3_spmd.sunk.clone | while | flops 136937776 | bytes 11301785 | solution.py:60
  25.5 1.5 broadcast_multiply_fusion.10
  27.0 1.9 copy.40
  38.1 1.5 broadcast_multiply_fusion.10
  39.6 1.9 copy.40
  50.7 1.5 broadcast_multiply_fusion.10
  52.2 1.9 copy.40
  63.3 1.5 broadcast_multiply_fusion.10
  64.8 1.9 copy.40
  75.9 1.5 broadcast_multiply_fusion.10
  77.5 1.9 copy.40
  90.1 1.9 copy.40
  101.2 1.5 broadcast_multiply_fusion.10
  102.7 1.9 copy.40
  115.3 1.9 copy.40
  121.0 4.2 %all-to-all-start.1 = ((f32[8,1,4096]{2,1,0:T(1,128)}), f32[8,1,4096]{2,1,0:T(1,128)S(1)}, u32[]{:S(2)}, u32[]{:S(2)}) async-start(f32[8,1,4096]{2,1,0:T(1,128)} %all_to_all.16), calls=%async_computation.1 | async-start | bytes 262144 | tf_op jit(solution)/shard_map/all_to_all | solution.py:66
  125.4 4.7 %all-to-all-done.1 = f32[8,1,4096]{2,1,0:T(1,128)S(1)} async-done(((f32[8,1,4096]{2,1,0:T(1,128)}), f32[8,1,4096]{2,1,0:T(1,128)S(1)}, u32[]{:S(2)}, u32[]{:S(2)}) %all-to-all-start.1) | async-done | bytes 131104 | tf_op jit(solution)/shard_map/all_to_all | solution.py:66
  132.4 33.2 %all-reduce.3.cloned.1.call-done = f32[8,4096]{1,0:T(8,128)} async-done(((f32[8,4096]{1,0:T(8,128)}), f32[8,4096]{1,0:T(8,128)}) %all-reduce.3.cloned.1.call-update) | async-done | bytes 131088
  167.2 4.8 %gather_fusion.3 = f32[512]{0:T(512)S(1)} fusion(f32[2,4096]{1,0:T(2,128)S(1)} %constant_dynamic-slice_fusion.3, s32[512]{0:T(512)S(1)} %bitcast.95), kind=kCustom, calls=%fused_computation.3 | custom fusion | bytes 8192 | tf_op jit(solution)/shard_map/jit(take_along_axis)/gather | solution.py:79
  172.7 64.9 %all-gather.1 = f32[32,2,8]{2,1,0:T(2,128)S(1)} all-gather(f32[1,2,8]{2,1,0:T(2,128)S(1)} %bitcast.99), channel_id=2, replica_groups=mesh['row'=4,'col'=2,'basis'=4] {'row','col','basis'}, dimensions={0}, use_global_device_ids=true | all-gather | bytes 2112 | tf_op jit(solution)/shard_map/all_gather | solution.py:75
  237.7 25.9 %gather_fusion.2 = f32[4096]{0:T(1024)S(1)} fusion(f32[512]{0:T(512)S(1)} %reshape.245, s32[4096]{0:T(1024)S(1)} %broadcast_clamp_fusion), kind=kCustom, calls=%fused_computation.2 | custom fusion | bytes 49152 | tf_op jit(solution)/shard_map/gather | solution.py:78
  264.0 66.7 %scatter_fusion = f32[2,4096]{1,0:T(2,128)} fusion(f32[2,4096]{1,0:T(2,128)} %copy-done.1, s32[512]{0:T(512)S(1)} %bitcast.94, f32[512]{0:T(512)S(1)} %bitcast.97), kind=kCustom, calls=%fused_computation.6 | custom fusion | bytes 10240 | tf_op jit(solution)/shard_map/scatter | solution.py:81
  (151 shorter events, 49.3 us)
Async XLA Ops:
  6.5 11.0 %copy-start = (s32[64]{0:T(128)S(1)}, s32[64]{0:T(128)}, u32[]{:S(2)}) copy-start(s32[64]{0:T(128)} %param.17) | copy-start | bytes 772
  8.6 112.4 %all-to-all-start = ((f32[8,1,1]{2,1,0:T(1,128)}), f32[8,1,1]{2,1,0:T(1,128)S(1)}, u32[]{:S(2)}, u32[]{:S(2)}) async-start(f32[8,1,1]{2,1,0:T(1,128)} %copy.25), calls=%async_computation | async-start | bytes 8192 | tf_op jit(solution)/shard_map/all_to_all | solution.py:67
  13.7 4.5 %copy-start.2 = (s32[8,2]{0,1:T(2,128)S(1)}, s32[8,2]{0,1:T(2,128)}, u32[]{:S(2)}) copy-start(s32[8,2]{0,1:T(2,128)} %param.12) | copy-start | bytes 196
  18.2 102.4 %copy-start.3 = (s32[2,256,8]{1,2,0:T(8,128)S(1)}, s32[2,256,8]{1,2,0:T(8,128)}, u32[]{:S(2)}) copy-start(s32[2,256,8]{1,2,0:T(8,128)} %param.19) | copy-start | bytes 49156
  18.2 107.0 %copy-start.4 = (s32[2,256]{1,0:T(2,128)S(1)}, s32[2,256]{1,0:T(2,128)}, u32[]{:S(2)}) copy-start(s32[2,256]{1,0:T(2,128)} %param.18) | copy-start | bytes 6148
  18.2 112.9 %copy-start.5 = (u32[32]{0:T(128)S(1)}, u32[32]{0:T(128)}, u32[]{:S(2)}) copy-start(u32[32]{0:T(128)} %constant.186) | copy-start | bytes 388
  121.0 9.2 %all-to-all-start.1 = ((f32[8,1,4096]{2,1,0:T(1,128)}), f32[8,1,4096]{2,1,0:T(1,128)S(1)}, u32[]{:S(2)}, u32[]{:S(2)}) async-start(f32[8,1,4096]{2,1,0:T(1,128)} %all_to_all.16), calls=%async_computation.1 | async-start | bytes 262144 | tf_op jit(solution)/shard_map/all_to_all | solution.py:66
  125.2 40.4 %all-reduce.3.cloned.1.call-start = ((), (), s32[]{:S(2)}) async-start(), calls=%async_computation.2 | async-start | bytes 262144
  166.5 5.5 %copy-start.1 = (f32[2,4096]{1,0:T(2,128)}, f32[2,4096]{1,0:T(2,128)S(1)}, u32[]{:S(2)}) copy-start(f32[2,4096]{1,0:T(2,128)S(1)} %constant_dynamic-slice_fusion.3) | copy-start | bytes 98308
Sparse Core Ops, SparseCore 0:
  131.2 34.3 all-reduce.2
where the time goes:
time: 340 us; the launch traced here: 338 us
  local copies, waits for them, and re-layouts  142 us (42%)
  blocking collectives  64.9 us (19%)
  waiting for transfers between devices  37.9 us (11%)
  loops' own time  35.9 us (11%)
  other arithmetic  22 us (6%)
  between operations  14.3 us (4%)
  matrix products  10.7 us (3%)
  starting transfers between devices  9.45 us (3%)
    scatter x1, local copies, waits for them, and re-layouts, body(): own_density.at[brick_rows, cell_pos].set(0.5 * current + 0.5 * corner_mean)  66.7 us
    all_gather x1, blocking collectives, body(): lax.all_gather(corner_values, ('row', 'col', 'basis'), axis=0, tiled=True)  64.9 us
    another operation x1, loops' own time, body(): densities = lax.map(single, (block_data, item_pairs, item_level))  35.9 us
    unnamed x2, waiting for transfers between devices  33.2 us
    gather x2, local copies, waits for them, and re-layouts, body(): corner_mean = jnp.mean(all_corners[corner_refs], axis=-1)  26.1 us
    mul x16, local copies, waits for them, and re-layouts, basis_values(): factor[0][:, :, None, None] * factor[1][:, None, :, None]  15.4 us
    mul x24, other arithmetic, basis_values(): factor[0][:, :, None, None] * factor[1][:, None, :, None]  12.4 us
    dot_general x8, matrix products, pair_density(): jnp.dot(block_values, col_values, preferred_element_type=jnp.float32)  9.84 us
  transfers between devices with their start and end apart: 3, of which 2 were waited for; matrix products, arithmetic and copies ran while one was open for 21% of the time, Pallas kernels for 0%

commit v1 on v0

v1 whole, which is shorter than its diff:
```python
import functools

import jax
import jax.numpy as jnp
from jax import lax
from jax.experimental import pallas as pl
from jax.experimental.pallas import tpu as pltpu
from jax.sharding import PartitionSpec as P

EDGE = 16
FACE = EDGE * EDGE
LANES = 128
ROWS = EDGE * FACE // LANES
COARSE = 0.2
META = 8
SLOT_ROWS = ROWS + META


def lane_pick(values, index):
    return jnp.take_along_axis(values, index, axis=1, mode="promise_in_bounds")


def iota(shape, axis):
    return lax.broadcasted_iota(jnp.int32, shape, axis)


def axis_factors(coords, middle, decay):
    return jnp.exp(-decay * (coords - middle) ** 2)


def pair_kernel(
    slot_depth,
    bricks_group,
    pairs_ref,
    dest_ref,
    tag_ref,
    levels_ref,
    blocks_ref,
    centres_ref,
    exponents_ref,
    out_ref,
    centre_buf,
    decay_buf,
    corner_buf,
    sems,
):
    items = blocks_ref.shape[0]
    slots = out_ref.shape[0]

    def copies(k, side):
        block = pairs_ref[side, k]
        at = 2 * k + side
        return (
            pltpu.make_async_copy(
                centres_ref.at[:, pl.ds(block, 1), :], centre_buf.at[at], sems.at[0, at]
            ),
            pltpu.make_async_copy(
                exponents_ref.at[pl.ds(block, 1), :], decay_buf.at[at], sems.at[1, at]
            ),
        )

    for k in range(items):
        for side in range(2):
            for copy in copies(k, side):
                copy.start()
    if slots != items:
        out_ref[...] = jnp.zeros_like(out_ref)
    steps = iota((EDGE, LANES), 0).astype(jnp.float32) - (EDGE - 1) / 2.0

    @pl.loop(0, items)
    def _(k):
        for side in range(2):
            for copy in copies(k, side):
                copy.wait()
        slot = dest_ref[k]
        target = slot // slot_depth * bricks_group + tag_ref[k]
        spacing = jnp.where(levels_ref[target] == 1, COARSE * 0.5, COARSE)
        coords = steps * spacing

        def factors(side):
            at = 2 * k + side
            decay = decay_buf[at]
            found = [axis_factors(coords, centre_buf[at, d], decay) for d in range(3)]
            face = jnp.concatenate(
                [found[1][y : y + 1, :] * found[2] for y in range(EDGE)], axis=0
            )
            return found[0], face

        row_x, row_face = factors(0)
        col_x, col_face = factors(1)
        row_x = row_x.T
        row_face = row_face.T
        block = blocks_ref[k]
        for x in range(EDGE):
            col = (col_x[x : x + 1, :] * col_face).astype(jnp.bfloat16)
            product = lax.dot_general(
                block, col, (((1,), (1,)), ((), ())), preferred_element_type=jnp.float32
            )
            dens = jnp.sum(row_x[:, x : x + 1] * row_face * product, axis=0, keepdims=True)
            for half in range(FACE // LANES):
                piece = dens[:, half * LANES : (half + 1) * LANES]
                out_ref[slot, pl.ds(2 * x + half, 1), :] = piece
                if x in (0, EDGE - 1):
                    corner_buf[2 * (x // (EDGE - 1)) + half, pl.ds(k, 1), :] = piece

    shape = (items, LANES)
    lane = iota(shape, 1)
    place = lane % 4
    low = jnp.where(place % 2 == 1, EDGE - 1, 0)
    high = (FACE - EDGE) % LANES + low
    source = jnp.where(place >= 2, high, low)
    found = [lane_pick(corner_buf[n], source) for n in range(4)]
    corner = lane % 8
    first = jnp.where(corner % 4 >= 2, found[1], found[0])
    last = jnp.where(corner % 4 >= 2, found[3], found[2])
    values = jnp.where(corner >= 4, last, first)
    row = iota(shape, 0)
    brick = jnp.zeros(shape, jnp.int32)
    for k in range(items):
        target = dest_ref[k] // slot_depth * bricks_group + tag_ref[k]
        brick = jnp.where(row == k, target, brick)
    meta = jnp.where(lane < 8, values, brick.astype(jnp.float32))
    if slots != items:

        @pl.loop(0, slots)
        def _(s):
            out_ref[s, ROWS:, :] = jnp.where(lane >= LANES - 8, -1.0, meta)

    for k in range(items):
        tag = tag_ref[k].astype(jnp.float32)
        out_ref[dest_ref[k], ROWS:, :] = jnp.where(lane >= LANES - 8, tag, meta)


def group_kernel(bricks_dev, in_ref, out_ref):
    slots = in_ref.shape[0]
    owners = out_ref.shape[0]
    table_rows = out_ref.shape[1] - bricks_dev * ROWS

    out_ref[...] = jnp.zeros_like(out_ref)
    shape = (META, LANES)
    lane = iota(shape, 1)
    index_tag = jnp.full(shape, LANES - 1, jnp.int32)

    def one(s):
        meta = in_ref[s, ROWS:, :]
        tag = jnp.tile(lane_pick(meta, index_tag), (ROWS // META, 1))
        dens = in_ref[s, :ROWS, :]
        for owner in range(owners):
            for b in range(bricks_dev):
                hit = tag == float(owner * bricks_dev + b)
                out_ref[owner, b * ROWS : (b + 1) * ROWS, :] += jnp.where(hit, dens, 0.0)
        values = lane_pick(meta, lane % 8)
        brick = lane_pick(meta, jnp.full(shape, 8, jnp.int32)).astype(jnp.int32)
        values = jnp.where(brick % 16 == lane // 8, values, 0.0)
        line = brick // 16
        for r in range(table_rows):
            part = jnp.sum(jnp.where(line == r, values, 0.0), axis=0, keepdims=True)
            out_ref[0, bricks_dev * ROWS + r : bricks_dev * ROWS + r + 1, :] += part

    if slots <= 8:
        for s in range(slots):
            one(s)
    else:
        pl.loop(0, slots)(one)
    for owner in range(1, owners):
        out_ref[owner, bricks_dev * ROWS :, :] = out_ref[0, bricks_dev * ROWS :, :]


def cell_kernel(in_ref, cells_ref, refs_ref, out_ref):
    owners = in_ref.shape[0]
    bricks_dev, cells = cells_ref.shape
    table_rows = in_ref.shape[1] - bricks_dev * ROWS

    total = in_ref[0]
    for z in range(1, owners):
        total = total + in_ref[z]
    table = total[bricks_dev * ROWS :]
    chunk = (8, LANES)
    refs = [
        [refs_ref[b, :, c * LANES : (c + 1) * LANES] for c in range(cells // LANES)]
        for b in range(bricks_dev)
    ]
    picked = [[jnp.zeros(chunk, jnp.float32) for _ in row] for row in refs]
    for r in range(table_rows):
        line = jnp.broadcast_to(table[r : r + 1, :], chunk)
        for b in range(bricks_dev):
            for c, index in enumerate(refs[b]):
                found = lane_pick(line, index % LANES)
                picked[b][c] = jnp.where(index // LANES == r, found, picked[b][c])
    for b in range(bricks_dev):
        mean = jnp.concatenate(
            [jnp.sum(p, axis=0, keepdims=True) for p in picked[b]], axis=1
        ) * (0.5 / 8.0)
        position = cells_ref[b : b + 1, :]
        high = (position // LANES == iota((ROWS, cells), 0)).astype(jnp.float32)
        here = position % LANES == iota((LANES, cells), 0)

        def spread(values):
            return lax.dot_general(
                high,
                values,
                (((1,), (1,)), ((), ())),
                precision=lax.Precision.HIGHEST,
                preferred_element_type=jnp.float32,
            )

        hit = spread(here.astype(jnp.float32))
        new = spread(jnp.where(here, mean, 0.0))
        own = total[b * ROWS : (b + 1) * ROWS]
        result = jnp.where(hit > 0.5, 0.5 * own + new, own)
        for row in range(ROWS):
            out_ref[b : b + 1, row * LANES : (row + 1) * LANES] = result[row : row + 1, :]


def vmem():
    return pl.BlockSpec(memory_space=pltpu.VMEM)


def smem():
    return pl.BlockSpec(memory_space=pltpu.SMEM)


def body(
    block_data, item_pairs, dest_slot, brick_tag, centres, exponents, levels, cell_pos, corner_refs
):
    groups = lax.axis_size("row") * lax.axis_size("col")
    owners = lax.axis_size("basis")
    items = block_data.shape[0]
    slot_depth = max(1, items // groups)
    slots = groups * slot_depth
    bricks = levels.shape[0]
    bricks_group = bricks // groups
    bricks_dev = bricks_group // owners
    table_rows = -(-bricks * 8 // (8 * LANES)) * 8
    basis = block_data.shape[1]
    params = pltpu.CompilerParams(vmem_limit_bytes=32 * 1024 * 1024)

    outgoing = pl.pallas_call(
        functools.partial(pair_kernel, slot_depth, bricks_group),
        out_shape=jax.ShapeDtypeStruct((slots, SLOT_ROWS, LANES), jnp.float32),
        in_specs=[smem()] * 4 + [vmem()] + [pl.BlockSpec(memory_space=pl.ANY)] * 2,
        out_specs=vmem(),
        scratch_shapes=[
            pltpu.VMEM((2 * items, 3, 1, basis), jnp.float32),
            pltpu.VMEM((2 * items, 1, basis), jnp.float32),
            pltpu.VMEM((4, items, LANES), jnp.float32),
            pltpu.SemaphoreType.DMA((2, 2 * items)),
        ],
        compiler_params=params,
        name="pair_density",
    )(
        item_pairs.T,
        dest_slot,
        brick_tag,
        levels,
        block_data,
        jnp.transpose(centres, (1, 0, 2)),
        exponents,
    )
    arrived = lax.all_to_all(outgoing, ("row", "col"), split_axis=0, concat_axis=0, tiled=True)
    partial = pl.pallas_call(
        functools.partial(group_kernel, bricks_dev),
        out_shape=jax.ShapeDtypeStruct((owners, bricks_dev * ROWS + table_rows, LANES), jnp.float32),
        in_specs=[vmem()],
        out_specs=vmem(),
        compiler_params=params,
        name="group_sum",
    )(arrived)
    parts = lax.all_to_all(partial, "basis", split_axis=0, concat_axis=0, tiled=True)
    return pl.pallas_call(
        cell_kernel,
        out_shape=jax.ShapeDtypeStruct((bricks_dev, EDGE * FACE), jnp.float32),
        in_specs=[vmem()] * 3,
        out_specs=vmem(),
        compiler_params=params,
        name="cells",
    )(parts, cell_pos, jnp.transpose(corner_refs, (0, 2, 1)))


def solution(mesh):
    split = ("row", "col", "basis")
    return jax.shard_map(
        body,
        mesh=mesh,
        in_specs=(
            P(split, None, None),
            P(split, None),
            P(split),
            P(split),
            P(),
            P(),
            P(),
            P(split, None),
            P(split, None, None),
        ),
        out_specs=P(split, None),
        check_vma=False,
    )
```

time: 340 us -> 35.1 us (0.10)
  local copies, waits for them, and re-layouts: 142 us -> 6.05 us
  blocking collectives: 64.9 us -> 21.7 us
  waiting for transfers between devices: 37.9 us -> 0 us
  loops' own time: 35.9 us -> 0 us
  other arithmetic: 22 us -> 0 us
  between operations: 14.3 us -> 0.03 us
  matrix products: 10.7 us -> 0 us
  starting transfers between devices: 9.45 us -> 0 us
  Pallas kernels: 0 us -> 6.98 us
    scatter x3 -> x0, local copies, waits for them, and re-layouts: 68 us -> none  [the longest x1 66.7 us: body(): own_density.at[brick_rows, cell_pos].set(0.5 * current + 0.5 * corner_mean)]
    all_gather x1 -> x0, blocking collectives: 64.9 us -> none  [body(): lax.all_gather(corner_values, ('row', 'col', 'basis'), axis=0, tiled=True)]
    another operation x1 -> x0, loops' own time: 35.9 us -> none  [body(): densities = lax.map(single, (block_data, item_pairs, item_level))]
    unnamed x2 -> x0, waiting for transfers between devices: 33.2 us -> none
    gather x7 -> x0, local copies, waits for them, and re-layouts: 32.2 us -> none  [the longest x2 26.1 us: body(): corner_mean = jnp.mean(all_corners[corner_refs], axis=-1)]
    all_to_all x0 -> x2, blocking collectives: none -> 21.7 us  [the longest x1 11.7 us: body(): lax.all_to_all(partial, 'basis', split_axis=0, concat_axis=0, tiled=True)]
    mul x16 -> x0, local copies, waits for them, and re-layouts: 15.4 us -> none  [basis_values(): factor[0][:, :, None, None] * factor[1][:, None, :, None]]
    mul x32 -> x0, other arithmetic: 12.5 us -> none  [the longest x24 12.4 us: basis_values(): factor[0][:, :, None, None] * factor[1][:, None, :, None]]
  transfers between devices with their start and end apart: 3 -> 0, of which waited for: 2 -> 0; matrix products, arithmetic and copies ran while one was open for 21% -> 0% of each run, Pallas kernels for 0% -> 0%
where the time goes in v1:
time: 35.1 us; the launch traced here: 34.8 us
  blocking collectives  21.7 us (62%)
  Pallas kernels  6.98 us (20%)
  local copies, waits for them, and re-layouts  6.05 us (17%)
    all_to_all x1, blocking collectives, body(): lax.all_to_all(partial, 'basis', split_axis=0, concat_axis=0, tiled=True)  11.7 us
    all_to_all x1, blocking collectives, body(): lax.all_to_all(outgoing, ('row', 'col'), split_axis=0, concat_axis=0, til...  10 us
    unnamed x18, local copies, waits for them, and re-layouts  6.05 us
    pallas_call x1, Pallas kernels, body(): pl.pallas_call(functools.partial(pair_kernel, slot_depth, bricks_group),...  5.4 us
    pallas_call x1, Pallas kernels, body(): pl.pallas_call(cell_kernel, out_shape=jax.ShapeDtypeStruct((bricks_dev, E...  1.33 us

profile of v1, /device:TPU:0, one launch (start us, length us, event | category | flops | bytes accessed | tf_op | source)
XLA Modules:
  0.0 34.8 jit_solution(6489226385006563574)
XLA Ops:
  0.0 0.0 copy-start
  0.0 1.4 %copy-done = f32[1024,3,128]{2,0,1:T(8,128)S(1)} copy-done((f32[1024,3,128]{2,0,1:T(8,128)S(1)}, f32[1024,3,128]{2,0,1:T(8,128)}, u32[]{:S(2)}) %copy-start) | copy-done | bytes 1572888
  1.4 0.0 copy-start.1
  1.4 1.0 %copy-done.1 = f32[1024,128]{1,0:T(8,128)S(1)} copy-done((f32[1024,128]{1,0:T(8,128)S(1)}, f32[1024,128]{1,0:T(8,128)}, u32[]{:S(2)}) %copy-start.1) | copy-done | bytes 524312
  2.5 0.0 copy-start.2
  2.5 0.9 %copy-done.2 = bf16[8,128,128]{2,1,0:T(8,128)(2,1)S(1)} copy-done((bf16[8,128,128]{2,1,0:T(8,128)(2,1)S(1)}, bf16[8,128,128]{2,1,0:T(8,128)(2,1)}, u32[]{:S(2)}) %copy-start.2) | copy-done | bytes 262168
  3.4 0.0 copy-start.5
  3.4 0.7 %copy-done.5 = s32[8,2]{0,1:T(2,128)S(1)} copy-done((s32[8,2]{0,1:T(2,128)S(1)}, s32[8,2]{0,1:T(2,128)}, u32[]{:S(2)}) %copy-start.5) | copy-done | bytes 88
  4.1 0.0 copy-start.6
  4.1 0.7 %copy-done.6 = s32[8]{0:T(128)S(1)} copy-done((s32[8]{0:T(128)S(1)}, s32[8]{0:T(128)}, u32[]{:S(2)}) %copy-start.6) | copy-done | bytes 56
  4.7 0.0 copy-start.7
  4.7 0.7 %copy-done.7 = s32[8]{0:T(128)S(1)} copy-done((s32[8]{0:T(128)S(1)}, s32[8]{0:T(128)}, u32[]{:S(2)}) %copy-start.7) | copy-done | bytes 56
  5.4 0.0 copy-start.8
  5.4 0.7 %copy-done.8 = s32[64]{0:T(128)S(1)} copy-done((s32[64]{0:T(128)S(1)}, s32[64]{0:T(128)}, u32[]{:S(2)}) %copy-start.8) | copy-done | bytes 280
  6.0 0.0 copy-start.3
  6.1 0.0 copy-start.4
  6.1 5.4 %pair_density.1 = f32[8,40,128]{2,1,0:T(8,128)S(1)} custom-call(s32[2,8]{1,0:T(2,128)S(1)} %bitcast.5, s32[8]{0:T(128)S(1)} %copy-done.6, s32[8]{0:T(128)S(1)} %copy-done.7, s32[64]{0:T(128)S(1)} %copy-done.8, bf16[8,128,128]{2,1,0:T(8,128)(2,1)S(1)} %copy-done.2, f32[3,1024,128]{2,1,0:T(8,128)S(1)} %bitcast.3, f32[1024,128]{1,0:T(8,128)S(1)} %copy-done.1), custom_call_target="tpu_custom_call" | custom-call | tf_op jit(solution)/shard_map/pair_density/pallas_call | solution.py:238
  11.5 10.0 %all_to_all.10.in_ref = f32[8,40,128]{2,1,0:T(8,128)S(1)} all-to-all(f32[8,40,128]{2,1,0:T(8,128)S(1)} %pair_density.1), channel_id=1, replica_groups=mesh['row'=4,'col'=2,'basis'=4] {'row','col'}, dimensions={0} | all-to-all | bytes 327680 | tf_op jit(solution)/shard_map/all_to_all | solution.py:260
  21.5 0.3 group_sum.1
  21.7 11.7 %all_to_all.11.in_ref = f32[4,72,128]{2,1,0:T(8,128)S(1)} all-to-all(f32[4,72,128]{2,1,0:T(8,128)S(1)} %group_sum.1), channel_id=1, replica_groups=mesh['row'=4,'col'=2,'basis'=4] {'basis'}, dimensions={0} | all-to-all | bytes 294912 | tf_op jit(solution)/shard_map/all_to_all | solution.py:269
  33.4 0.0 copy-done.3
  33.4 0.0 copy-done.4
  33.4 1.3 %cells.1 = f32[2,4096]{1,0:T(2,128)} custom-call(f32[4,72,128]{2,1,0:T(8,128)S(1)} %all_to_all.11.in_ref, s32[2,256]{1,0:T(2,128)S(1)} %copy-done.4, s32[2,8,256]{2,1,0:T(8,128)S(1)} %bitcast.4), custom_call_target="tpu_custom_call" | custom-call | tf_op jit(solution)/shard_map/cells/pallas_call | solution.py:270
Async XLA Ops:
  0.0 1.4 %copy-start = (f32[1024,3,128]{2,0,1:T(8,128)S(1)}, f32[1024,3,128]{2,0,1:T(8,128)}, u32[]{:S(2)}) copy-start(f32[1024,3,128]{2,0,1:T(8,128)} %param.13) | copy-start | bytes 4718596
  1.4 1.0 %copy-start.1 = (f32[1024,128]{1,0:T(8,128)S(1)}, f32[1024,128]{1,0:T(8,128)}, u32[]{:S(2)}) copy-start(f32[1024,128]{1,0:T(8,128)} %exponents_ref.1) | copy-start | bytes 1572868
  2.5 0.9 %copy-start.2 = (bf16[8,128,128]{2,1,0:T(8,128)(2,1)S(1)}, bf16[8,128,128]{2,1,0:T(8,128)(2,1)}, u32[]{:S(2)}) copy-start(bf16[8,128,128]{2,1,0:T(8,128)(2,1)} %blocks_ref.1) | copy-start | bytes 786436
  3.4 0.7 %copy-start.5 = (s32[8,2]{0,1:T(2,128)S(1)}, s32[8,2]{0,1:T(2,128)}, u32[]{:S(2)}) copy-start(s32[8,2]{0,1:T(2,128)} %param.10) | copy-start | bytes 196
  4.1 0.7 %copy-start.6 = (s32[8]{0:T(128)S(1)}, s32[8]{0:T(128)}, u32[]{:S(2)}) copy-start(s32[8]{0:T(128)} %dest_ref.1) | copy-start | bytes 100
  4.7 0.7 %copy-start.7 = (s32[8]{0:T(128)S(1)}, s32[8]{0:T(128)}, u32[]{:S(2)}) copy-start(s32[8]{0:T(128)} %tag_ref.1) | copy-start | bytes 100
  5.4 0.7 %copy-start.8 = (s32[64]{0:T(128)S(1)}, s32[64]{0:T(128)}, u32[]{:S(2)}) copy-start(s32[64]{0:T(128)} %levels_ref.1) | copy-start | bytes 772
  6.0 27.4 %copy-start.3 = (s32[2,256,8]{1,2,0:T(8,128)S(1)}, s32[2,256,8]{1,2,0:T(8,128)}, u32[]{:S(2)}) copy-start(s32[2,256,8]{1,2,0:T(8,128)} %param.17) | copy-start | bytes 49156
  6.1 27.4 %copy-start.4 = (s32[2,256]{1,0:T(2,128)S(1)}, s32[2,256]{1,0:T(2,128)}, u32[]{:S(2)}) copy-start(s32[2,256]{1,0:T(2,128)} %cells_ref.1) | copy-start | bytes 6148

commit v2 on v1

--- a/solution.py
+++ b/solution.py
@@ -31,21 +31,48 @@
 def pair_kernel(
     slot_depth,
     bricks_group,
+    pairs_hbm,
+    dest_hbm,
+    tag_hbm,
+    levels_hbm,
+    blocks_hbm,
+    centres_ref,
+    exponents_ref,
+    out_ref,
     pairs_ref,
     dest_ref,
     tag_ref,
     levels_ref,
     blocks_ref,
-    centres_ref,
-    exponents_ref,
-    out_ref,
     centre_buf,
     decay_buf,
     corner_buf,
     sems,
+    list_sems,
+    block_sems,
 ):
     items = blocks_ref.shape[0]
     slots = out_ref.shape[0]
+    lists = [
+        pltpu.make_async_copy(source, target, list_sems.at[n])
+        for n, (source, target) in enumerate(
+            (
+                (pairs_hbm, pairs_ref),
+                (dest_hbm, dest_ref),
+                (tag_hbm, tag_ref),
+                (levels_hbm, levels_ref),
+            )
+        )
+    ]
+    for copy in lists:
+        copy.start()
+
+    def block_copy(k):
+        return pltpu.make_async_copy(blocks_hbm.at[k], blocks_ref.at[k], block_sems.at[k])
+
+    for k in range(items):
+        block_copy(k).start()
+    lists[0].wait()
 
     def copies(k, side):
         block = pairs_ref[side, k]
@@ -63,6 +90,8 @@
         for side in range(2):
             for copy in copies(k, side):
                 copy.start()
+    for copy in lists[1:]:
+        copy.wait()
     if slots != items:
         out_ref[...] = jnp.zeros_like(out_ref)
     steps = iota((EDGE, LANES), 0).astype(jnp.float32) - (EDGE - 1) / 2.0
@@ -90,6 +119,7 @@
         col_x, col_face = factors(1)
         row_x = row_x.T
         row_face = row_face.T
+        block_copy(k).wait()
         block = blocks_ref[k]
         for x in range(EDGE):
             col = (col_x[x : x + 1, :] * col_face).astype(jnp.bfloat16)
@@ -216,10 +246,6 @@
     return pl.BlockSpec(memory_space=pltpu.VMEM)
 
 
-def smem():
-    return pl.BlockSpec(memory_space=pltpu.SMEM)
-
-
 def body(
     block_data, item_pairs, dest_slot, brick_tag, centres, exponents, levels, cell_pos, corner_refs
 ):
@@ -238,24 +264,36 @@
     outgoing = pl.pallas_call(
         functools.partial(pair_kernel, slot_depth, bricks_group),
         out_shape=jax.ShapeDtypeStruct((slots, SLOT_ROWS, LANES), jnp.float32),
-        in_specs=[smem()] * 4 + [vmem()] + [pl.BlockSpec(memory_space=pl.ANY)] * 2,
+        in_specs=[pl.BlockSpec(memory_space=pltpu.HBM)] * 7,
         out_specs=vmem(),
         scratch_shapes=[
+            pltpu.SMEM((2, items), jnp.int32),
+            pltpu.SMEM((items,), jnp.int32),
+            pltpu.SMEM((items,), jnp.int32),
+            pltpu.SMEM((bricks,), jnp.int32),
+            pltpu.VMEM(block_data.shape, block_data.dtype),
             pltpu.VMEM((2 * items, 3, 1, basis), jnp.float32),
             pltpu.VMEM((2 * items, 1, basis), jnp.float32),
             pltpu.VMEM((4, items, LANES), jnp.float32),
             pltpu.SemaphoreType.DMA((2, 2 * items)),
+            pltpu.SemaphoreType.DMA((4,)),
+            pltpu.SemaphoreType.DMA((items,)),
         ],
         compiler_params=params,
         name="pair_density",
     )(
-        item_pairs.T,
-        dest_slot,
-        brick_tag,
-        levels,
-        block_data,
-        jnp.transpose(centres, (1, 0, 2)),
-        exponents,
+        *(
+            pltpu.with_memory_space_constraint(operand, pltpu.HBM)
+            for operand in (
+                item_pairs.T,
+                dest_slot,
+                brick_tag,
+                levels,
+                block_data,
+                jnp.transpose(centres, (1, 0, 2)),
+                exponents,
+            )
+        )
     )
     arrived = lax.all_to_all(outgoing, ("row", "col"), split_axis=0, concat_axis=0, tiled=True)
     partial = pl.pallas_call(

time: 35.1 us -> 30.8 us (0.88)
  local copies, waits for them, and re-layouts: 6.05 us -> 0.01 us
  Pallas kernels: 6.98 us -> 8.81 us
    unnamed x18 -> x4, local copies, waits for them, and re-layouts: 6.05 us -> 0.01 us
    pallas_call x1, Pallas kernels: 5.4 us -> 7.23 us  [body(): pl.pallas_call(functools.partial(pair_kernel, slot_depth, bricks_group),...]
where the time goes in v2:
time: 30.8 us; the launch traced here: 30.6 us
  blocking collectives  21.7 us (70%)
  Pallas kernels  8.81 us (29%)
    all_to_all x1, blocking collectives, body(): lax.all_to_all(partial, 'basis', split_axis=0, concat_axis=0, tiled=True)  11.7 us
    all_to_all x1, blocking collectives, body(): lax.all_to_all(outgoing, ('row', 'col'), split_axis=0, concat_axis=0, til...  9.99 us
    pallas_call x1, Pallas kernels, body(): pl.pallas_call(functools.partial(pair_kernel, slot_depth, bricks_group),...  7.23 us
    pallas_call x1, Pallas kernels, body(): pl.pallas_call(cell_kernel, out_shape=jax.ShapeDtypeStruct((bricks_dev, E...  1.33 us

profile of v2, /device:TPU:0, one launch (start us, length us, event | category | flops | bytes accessed | tf_op | source)
XLA Modules:
  0.0 30.6 jit_solution(795577667453280930)
XLA Ops:
  0.0 0.0 copy-start
  0.0 0.0 copy-start.1
  0.0 7.2 %pair_density.1 = f32[8,40,128]{2,1,0:T(8,128)S(1)} custom-call(s32[2,8]{1,0:T(2,128)} %bitcast.5, s32[8]{0:T(128)} %dest_hbm.1, s32[8]{0:T(128)} %tag_hbm.1, s32[64]{0:T(128)} %levels_hbm.1, bf16[8,128,128]{2,1,0:T(8,128)(2,1)} %blocks_hbm.1, f32[3,1024,128]{2,1,0:T(8,128)} %bitcast.4, f32[1024,128]{1,0:T(8,128)} %exponents_ref.1), custom_call_target="tpu_custom_call" | custom-call | tf_op jit(solution)/shard_map/pair_density/pallas_call | solution.py:264
  7.2 10.0 %all_to_all.10.in_ref = f32[8,40,128]{2,1,0:T(8,128)S(1)} all-to-all(f32[8,40,128]{2,1,0:T(8,128)S(1)} %pair_density.1), channel_id=1, replica_groups=mesh['row'=4,'col'=2,'basis'=4] {'row','col'}, dimensions={0} | all-to-all | bytes 327680 | tf_op jit(solution)/shard_map/all_to_all | solution.py:298
  17.2 0.3 group_sum.1
  17.5 11.7 %all_to_all.11.in_ref = f32[4,72,128]{2,1,0:T(8,128)S(1)} all-to-all(f32[4,72,128]{2,1,0:T(8,128)S(1)} %group_sum.1), channel_id=1, replica_groups=mesh['row'=4,'col'=2,'basis'=4] {'basis'}, dimensions={0} | all-to-all | bytes 294912 | tf_op jit(solution)/shard_map/all_to_all | solution.py:307
  29.2 0.0 copy-done
  29.2 0.0 copy-done.1
  29.2 1.3 %cells.1 = f32[2,4096]{1,0:T(2,128)} custom-call(f32[4,72,128]{2,1,0:T(8,128)S(1)} %all_to_all.11.in_ref, s32[2,256]{1,0:T(2,128)S(1)} %copy-done.1, s32[2,8,256]{2,1,0:T(8,128)S(1)} %bitcast.3), custom_call_target="tpu_custom_call" | custom-call | tf_op jit(solution)/shard_map/cells/pallas_call | solution.py:308
Async XLA Ops:
  0.0 29.2 %copy-start = (s32[2,256,8]{1,2,0:T(8,128)S(1)}, s32[2,256,8]{1,2,0:T(8,128)}, u32[]{:S(2)}) copy-start(s32[2,256,8]{1,2,0:T(8,128)} %param.17) | copy-start | bytes 49156
  0.0 29.2 %copy-start.1 = (s32[2,256]{1,0:T(2,128)S(1)}, s32[2,256]{1,0:T(2,128)}, u32[]{:S(2)}) copy-start(s32[2,256]{1,0:T(2,128)} %cells_ref.1) | copy-start | bytes 6148

commit v3 on v2

--- a/solution.py
+++ b/solution.py
@@ -38,19 +38,25 @@
     blocks_hbm,
     centres_ref,
     exponents_ref,
-    out_ref,
-    pairs_ref,
-    dest_ref,
-    tag_ref,
-    levels_ref,
-    blocks_ref,
-    centre_buf,
-    decay_buf,
-    corner_buf,
-    sems,
-    list_sems,
-    block_sems,
+    *refs,
 ):
+    count = len(refs) - 12
+    outs = refs[:count]
+    (
+        out_ref,
+        pairs_ref,
+        dest_ref,
+        tag_ref,
+        levels_ref,
+        blocks_ref,
+        centre_buf,
+        decay_buf,
+        corner_buf,
+        sems,
+        list_sems,
+        block_sems,
+    ) = refs[count:]
+    me = lax.axis_index("row") * lax.axis_size("col") + lax.axis_index("col")
     items = blocks_ref.shape[0]
     slots = out_ref.shape[0]
     lists = [
@@ -94,6 +100,12 @@
         copy.wait()
     if slots != items:
         out_ref[...] = jnp.zeros_like(out_ref)
+
+    def slot_of(k):
+        slot = dest_ref[k]
+        shift = lax.rem(slot // slot_depth - me + count, count)
+        return shift * slot_depth + lax.rem(slot, slot_depth)
+
     steps = iota((EDGE, LANES), 0).astype(jnp.float32) - (EDGE - 1) / 2.0
 
     @pl.loop(0, items)
@@ -101,8 +113,8 @@
         for side in range(2):
             for copy in copies(k, side):
                 copy.wait()
-        slot = dest_ref[k]
-        target = slot // slot_depth * bricks_group + tag_ref[k]
+        slot = slot_of(k)
+        target = dest_ref[k] // slot_depth * bricks_group + tag_ref[k]
         spacing = jnp.where(levels_ref[target] == 1, COARSE * 0.5, COARSE)
         coords = steps * spacing
 
@@ -158,52 +170,53 @@
 
     for k in range(items):
         tag = tag_ref[k].astype(jnp.float32)
-        out_ref[dest_ref[k], ROWS:, :] = jnp.where(lane >= LANES - 8, tag, meta)
-
-
-def group_kernel(bricks_dev, in_ref, out_ref):
-    slots = in_ref.shape[0]
-    owners = out_ref.shape[0]
-    table_rows = out_ref.shape[1] - bricks_dev * ROWS
-
-    out_ref[...] = jnp.zeros_like(out_ref)
+        out_ref[slot_of(k), ROWS:, :] = jnp.where(lane >= LANES - 8, tag, meta)
+    for d, out in enumerate(outs):
+        out[...] = out_ref[d * slot_depth : (d + 1) * slot_depth]
+
+
+def group_kernel(bricks_dev, count, *refs):
+    ins, outs = refs[:count], refs[count:]
+    owners = len(outs)
+    me = lax.axis_index("basis")
+    table_rows = outs[0].shape[0] - bricks_dev * ROWS
     shape = (META, LANES)
     lane = iota(shape, 1)
     index_tag = jnp.full(shape, LANES - 1, jnp.int32)
-
-    def one(s):
-        meta = in_ref[s, ROWS:, :]
-        tag = jnp.tile(lane_pick(meta, index_tag), (ROWS // META, 1))
-        dens = in_ref[s, :ROWS, :]
-        for owner in range(owners):
-            for b in range(bricks_dev):
-                hit = tag == float(owner * bricks_dev + b)
-                out_ref[owner, b * ROWS : (b + 1) * ROWS, :] += jnp.where(hit, dens, 0.0)
+    sums = [jnp.zeros((bricks_dev * ROWS, LANES), jnp.float32) for _ in outs]
+    slots = [(ref, s) for ref in ins for s in range(ref.shape[0])]
+    for b in range(bricks_dev):
+        for d in range(owners):
+            brick = (lax.rem(me + d, owners) * bricks_dev + b).astype(jnp.float32)
+            total = jnp.zeros((ROWS, LANES), jnp.float32)
+            for ref, s in slots:
+                tag = lane_pick(ref[s, ROWS:, :], index_tag)
+                hit = jnp.tile(tag, (ROWS // META, 1)) == brick
+                total = total + jnp.where(hit, ref[s, :ROWS, :], 0.0)
+            outs[d][b * ROWS : (b + 1) * ROWS, :] = total
+    lines = [jnp.zeros((1, LANES), jnp.float32) for _ in range(table_rows)]
+    for ref, s in slots:
+        meta = ref[s, ROWS:, :]
         values = lane_pick(meta, lane % 8)
         brick = lane_pick(meta, jnp.full(shape, 8, jnp.int32)).astype(jnp.int32)
         values = jnp.where(brick % 16 == lane // 8, values, 0.0)
         line = brick // 16
         for r in range(table_rows):
             part = jnp.sum(jnp.where(line == r, values, 0.0), axis=0, keepdims=True)
-            out_ref[0, bricks_dev * ROWS + r : bricks_dev * ROWS + r + 1, :] += part
-
-    if slots <= 8:
-        for s in range(slots):
-            one(s)
-    else:
-        pl.loop(0, slots)(one)
-    for owner in range(1, owners):
-        out_ref[owner, bricks_dev * ROWS :, :] = out_ref[0, bricks_dev * ROWS :, :]
-
-
-def cell_kernel(in_ref, cells_ref, refs_ref, out_ref):
-    owners = in_ref.shape[0]
+            lines[r] = lines[r] + part
+    table = jnp.concatenate(lines, axis=0)
+    for out in outs:
+        out[bricks_dev * ROWS :, :] = table
+
+
+def cell_kernel(*refs):
+    *ins, cells_ref, refs_ref, out_ref = refs
     bricks_dev, cells = cells_ref.shape
-    table_rows = in_ref.shape[1] - bricks_dev * ROWS
-
-    total = in_ref[0]
-    for z in range(1, owners):
-        total = total + in_ref[z]
+    table_rows = ins[0].shape[0] - bricks_dev * ROWS
+
+    total = ins[0][...]
+    for part in ins[1:]:
+        total = total + part[...]
     table = total[bricks_dev * ROWS :]
     chunk = (8, LANES)
     refs = [
@@ -242,6 +255,14 @@
             out_ref[b : b + 1, row * LANES : (row + 1) * LANES] = result[row : row + 1, :]
 
 
+def shifted(pieces, axes):
+    count = len(pieces)
+    return [
+        lax.ppermute(piece, axes, [(i, (i + d) % count) for i in range(count)]) if d else piece
+        for d, piece in enumerate(pieces)
+    ]
+
+
 def vmem():
     return pl.BlockSpec(memory_space=pltpu.VMEM)
 
@@ -263,10 +284,11 @@
 
     outgoing = pl.pallas_call(
         functools.partial(pair_kernel, slot_depth, bricks_group),
-        out_shape=jax.ShapeDtypeStruct((slots, SLOT_ROWS, LANES), jnp.float32),
+        out_shape=[jax.ShapeDtypeStruct((slot_depth, SLOT_ROWS, LANES), jnp.float32)] * groups,
         in_specs=[pl.BlockSpec(memory_space=pltpu.HBM)] * 7,
-        out_specs=vmem(),
+        out_specs=[vmem()] * groups,
         scratch_shapes=[
+            pltpu.VMEM((slots, SLOT_ROWS, LANES), jnp.float32),
             pltpu.SMEM((2, items), jnp.int32),
             pltpu.SMEM((items,), jnp.int32),
             pltpu.SMEM((items,), jnp.int32),
@@ -295,24 +317,25 @@
             )
         )
     )
-    arrived = lax.all_to_all(outgoing, ("row", "col"), split_axis=0, concat_axis=0, tiled=True)
+    arrived = shifted(outgoing, ("row", "col"))
     partial = pl.pallas_call(
-        functools.partial(group_kernel, bricks_dev),
-        out_shape=jax.ShapeDtypeStruct((owners, bricks_dev * ROWS + table_rows, LANES), jnp.float32),
-        in_specs=[vmem()],
-        out_specs=vmem(),
+        functools.partial(group_kernel, bricks_dev, groups),
+        out_shape=[jax.ShapeDtypeStruct((bricks_dev * ROWS + table_rows, LANES), jnp.float32)]
+        * owners,
+        in_specs=[vmem()] * groups,
+        out_specs=[vmem()] * owners,
         compiler_params=params,
         name="group_sum",
-    )(arrived)
-    parts = lax.all_to_all(partial, "basis", split_axis=0, concat_axis=0, tiled=True)
+    )(*arrived)
+    parts = shifted(partial, "basis")
     return pl.pallas_call(
         cell_kernel,
         out_shape=jax.ShapeDtypeStruct((bricks_dev, EDGE * FACE), jnp.float32),
-        in_specs=[vmem()] * 3,
+        in_specs=[vmem()] * (owners + 2),
         out_specs=vmem(),
         compiler_params=params,
         name="cells",
-    )(parts, cell_pos, jnp.transpose(corner_refs, (0, 2, 1)))
+    )(*parts, cell_pos, jnp.transpose(corner_refs, (0, 2, 1)))
 
 
 def solution(mesh):

time: 30.8 us -> 29.4 us (0.955)
  blocking collectives: 21.7 us -> 0 us
  starting transfers between devices: 0 us -> 14.1 us
  waiting for transfers between devices: 0 us -> 6.22 us
    all_to_all x2 -> x0, blocking collectives: 21.7 us -> none  [the longest x1 11.7 us: body(): lax.all_to_all(partial, 'basis', split_axis=0, concat_axis=0, tiled=True)]
    ppermute x0 -> x10, starting transfers between devices: none -> 14.1 us  [shifted(): lax.ppermute(piece, axes, [(i, (i + d) % count) for i in range(count)])]
    ppermute x0 -> x10, waiting for transfers between devices: none -> 6.22 us  [shifted(): lax.ppermute(piece, axes, [(i, (i + d) % count) for i in range(count)])]
  transfers between devices with their start and end apart: 0 -> 10, of which waited for: 0 -> 6; matrix products, arithmetic and copies ran while one was open for 0% -> 0% of each run, Pallas kernels for 0% -> 0%
where the time goes in v3:
time: 29.4 us; the launch traced here: 29.2 us
  starting transfers between devices  14.1 us (48%)
  Pallas kernels  8.83 us (30%)
  waiting for transfers between devices  6.22 us (21%)
    ppermute x10, starting transfers between devices, shifted(): lax.ppermute(piece, axes, [(i, (i + d) % count) for i in range(count)])  14.1 us
    pallas_call x1, Pallas kernels, body(): pl.pallas_call(functools.partial(pair_kernel, slot_depth, bricks_group),...  7.24 us
    ppermute x10, waiting for transfers between devices, shifted(): lax.ppermute(piece, axes, [(i, (i + d) % count) for i in range(count)])  6.22 us
    pallas_call x1, Pallas kernels, body(): pl.pallas_call(cell_kernel, out_shape=jax.ShapeDtypeStruct((bricks_dev, E...  1.33 us
  transfers between devices with their start and end apart: 10, of which 6 were waited for; matrix products, arithmetic and copies ran while one was open for 0% of the time, Pallas kernels for 0%

profile of v3, /device:TPU:0, one launch (start us, length us, event | category | flops | bytes accessed | tf_op | source)
XLA Modules:
  0.0 29.2 jit_solution(4416604719627496590)
XLA Ops:
  0.0 7.2 %pair_density.1 = (f32[1,40,128]{2,1,0:T(8,128)S(1)}, f32[1,40,128]{2,1,0:T(8,128)S(1)}, f32[1,40,128]{2,1,0:T(8,128)S(1)}, f32[1,40,128]{2,1,0:T(8,128)S(1)}, f...) custom-call(s32[2,8]{1,0:T(2,128)} %bitcast.5, ...), custom_call_target="tpu_custom_call" | custom-call | tf_op jit(solution)/shard_map/pair_density/pallas_call | solution.py:285
  7.3 3.0 %collective-permute-start = (f32[1,40,128]{2,1,0:T(8,128)S(1)}, f32[1,40,128]{2,1,0:T(8,128)S(1)}, u32[]{:S(2)}, u32[]{:S(2)}) collective-permute-start(f32[1,40,128]{2,1,0:T(8,128)S(1)} %get-tuple-element.18), channel_id=1, source_target_pairs={{0,4},{4,8},{8,12},{12,16},{16,20},{20,24},{24,28},{28,0},{1,5},{5... | collective-permute-start | bytes 61448 | tf_op jit(solution)/shard_map/ppermute | solution.py:261
  10.3 0.0 collective-permute-start.1
  10.3 1.3 %collective-permute-start.2 = (f32[1,40,128]{2,1,0:T(8,128)S(1)}, f32[1,40,128]{2,1,0:T(8,128)S(1)}, u32[]{:S(2)}, u32[]{:S(2)}) collective-permute-start(f32[1,40,128]{2,1,0:T(8,128)S(1)} %get-tuple-element.20), channel_id=1, source_target_pairs={{0,12},{4,16},{8,20},{12,24},{16,28},{20,0},{24,4},{28,8},{1,13},{... | collective-permute-start | bytes 61448 | tf_op jit(solution)/shard_map/ppermute | solution.py:261
  11.6 0.5 %collective-permute-start.3 = (f32[1,40,128]{2,1,0:T(8,128)S(1)}, f32[1,40,128]{2,1,0:T(8,128)S(1)}, u32[]{:S(2)}, u32[]{:S(2)}) collective-permute-start(f32[1,40,128]{2,1,0:T(8,128)S(1)} %get-tuple-element.21), channel_id=1, source_target_pairs={{0,16},{4,20},{8,24},{12,28},{16,0},{20,4},{24,8},{28,12},{1,17},{... | collective-permute-start | bytes 61448 | tf_op jit(solution)/shard_map/ppermute | solution.py:261
  12.1 2.6 %collective-permute-start.4 = (f32[1,40,128]{2,1,0:T(8,128)S(1)}, f32[1,40,128]{2,1,0:T(8,128)S(1)}, u32[]{:S(2)}, u32[]{:S(2)}) collective-permute-start(f32[1,40,128]{2,1,0:T(8,128)S(1)} %get-tuple-element.22), channel_id=1, source_target_pairs={{0,20},{4,24},{8,28},{12,0},{16,4},{20,8},{24,12},{28,16},{1,21},{... | collective-permute-start | bytes 61448 | tf_op jit(solution)/shard_map/ppermute | solution.py:261
  14.7 0.0 collective-permute-done.refs_1_
  14.7 0.9 %collective-permute-start.5 = (f32[1,40,128]{2,1,0:T(8,128)S(1)}, f32[1,40,128]{2,1,0:T(8,128)S(1)}, u32[]{:S(2)}, u32[]{:S(2)}) collective-permute-start(f32[1,40,128]{2,1,0:T(8,128)S(1)} %get-tuple-element.23), channel_id=1, source_target_pairs={{0,24},{4,28},{8,0},{12,4},{16,8},{20,12},{24,16},{28,20},{1,25},{... | collective-permute-start | bytes 61448 | tf_op jit(solution)/shard_map/ppermute | solution.py:261
  15.6 0.0 collective-permute-done.1.refs_2_
  15.6 0.2 collective-permute-start.6
  15.8 0.0 collective-permute-done.2.refs_3_
  15.8 0.0 collective-permute-done.3.refs_4_
  15.8 0.4 %collective-permute-done.4.refs_5_ = f32[1,40,128]{2,1,0:T(8,128)S(1)} collective-permute-done((f32[1,40,128]{2,1,0:T(8,128)S(1)}, f32[1,40,128]{2,1,0:T(8,128)S(1)}, u32[]{:S(2)}, u32[]{:S(2)}) %collective-permute-start.4) | collective-permute-done | bytes 20512 | tf_op jit(solution)/shard_map/ppermute | solution.py:261
  16.2 0.9 %collective-permute-done.5.refs_6_ = f32[1,40,128]{2,1,0:T(8,128)S(1)} collective-permute-done((f32[1,40,128]{2,1,0:T(8,128)S(1)}, f32[1,40,128]{2,1,0:T(8,128)S(1)}, u32[]{:S(2)}, u32[]{:S(2)}) %collective-permute-start.5) | collective-permute-done | bytes 20512 | tf_op jit(solution)/shard_map/ppermute | solution.py:261
  17.1 2.3 %collective-permute-done.6.refs_7_ = f32[1,40,128]{2,1,0:T(8,128)S(1)} collective-permute-done((f32[1,40,128]{2,1,0:T(8,128)S(1)}, f32[1,40,128]{2,1,0:T(8,128)S(1)}, u32[]{:S(2)}, u32[]{:S(2)}) %collective-permute-start.6) | collective-permute-done | bytes 20512 | tf_op jit(solution)/shard_map/ppermute | solution.py:261
  19.4 0.3 group_sum.1
  19.7 1.6 %collective-permute-start.7 = (f32[72,128]{1,0:T(8,128)S(1)}, f32[72,128]{1,0:T(8,128)S(1)}, u32[]{:S(2)}, u32[]{:S(2)}) collective-permute-start(f32[72,128]{1,0:T(8,128)S(1)} %get-tuple-element.26), channel_id=1, source_target_pairs={{0,1},{1,2},{2,3},{3,0},{4,5},{5,6},{6,7},{7,4},{8,9},{9,10},{10,1... | collective-permute-start | bytes 110600 | tf_op jit(solution)/shard_map/ppermute | solution.py:261
  21.3 2.6 %collective-permute-start.8 = (f32[72,128]{1,0:T(8,128)S(1)}, f32[72,128]{1,0:T(8,128)S(1)}, u32[]{:S(2)}, u32[]{:S(2)}) collective-permute-start(f32[72,128]{1,0:T(8,128)S(1)} %get-tuple-element.27), channel_id=1, source_target_pairs={{0,2},{1,3},{2,0},{3,1},{4,6},{5,7},{6,4},{7,5},{8,10},{9,11},{10,... | collective-permute-start | bytes 110600 | tf_op jit(solution)/shard_map/ppermute | solution.py:261
  23.9 1.4 %collective-permute-start.9 = (f32[72,128]{1,0:T(8,128)S(1)}, f32[72,128]{1,0:T(8,128)S(1)}, u32[]{:S(2)}, u32[]{:S(2)}) collective-permute-start(f32[72,128]{1,0:T(8,128)S(1)} %get-tuple-element.28), channel_id=1, source_target_pairs={{0,3},{1,0},{2,1},{3,2},{4,7},{5,4},{6,5},{7,6},{8,11},{9,8},{10,9... | collective-permute-start | bytes 110600 | tf_op jit(solution)/shard_map/ppermute | solution.py:261
  25.2 0.2 collective-permute-done.7.refs_1_
  25.5 0.7 %collective-permute-done.8.refs_2_ = f32[72,128]{1,0:T(8,128)S(1)} collective-permute-done((f32[72,128]{1,0:T(8,128)S(1)}, f32[72,128]{1,0:T(8,128)S(1)}, u32[]{:S(2)}, u32[]{:S(2)}) %collective-permute-start.8) | collective-permute-done | bytes 36896 | tf_op jit(solution)/shard_map/ppermute | solution.py:261
  26.2 1.7 %collective-permute-done.9.refs_3_ = f32[72,128]{1,0:T(8,128)S(1)} collective-permute-done((f32[72,128]{1,0:T(8,128)S(1)}, f32[72,128]{1,0:T(8,128)S(1)}, u32[]{:S(2)}, u32[]{:S(2)}) %collective-permute-start.9) | collective-permute-done | bytes 36896 | tf_op jit(solution)/shard_map/ppermute | solution.py:261
  27.8 0.0 copy-done.1
  27.8 1.3 %cells.1 = f32[2,4096]{1,0:T(2,128)} custom-call(f32[72,128]{1,0:T(8,128)S(1)} %get-tuple-element.25.refs_0_, f32[72,128]{1,0:T(8,128)S(1)} %collective-permute-done.7.refs_1_, f32[72,128]{1,0:T(8,128)S(1)} %collective-permute-done.8.refs_2_, f32[72,128]{1,0:T(8,128)S(1)} %collective-permute-done.9.refs_3_, s32[2,256]{1,0:T(2,128)S(1)} %copy-done.1, ...), custom_call_target="tpu_custom_call" | custom-call | tf_op jit(solution)/shard_map/cells/pallas_call | solution.py:331
  (3 shorter events, 0.0 us)
Async XLA Ops:
  0.0 27.8 %copy-start = (s32[2,256,8]{1,2,0:T(8,128)S(1)}, s32[2,256,8]{1,2,0:T(8,128)}, u32[]{:S(2)}) copy-start(s32[2,256,8]{1,2,0:T(8,128)} %param.17) | copy-start | bytes 49156
  0.0 27.8 %copy-start.1 = (s32[2,256]{1,0:T(2,128)S(1)}, s32[2,256]{1,0:T(2,128)}, u32[]{:S(2)}) copy-start(s32[2,256]{1,0:T(2,128)} %refs_4_.1) | copy-start | bytes 6148
  7.3 7.5 %collective-permute-start = (f32[1,40,128]{2,1,0:T(8,128)S(1)}, f32[1,40,128]{2,1,0:T(8,128)S(1)}, u32[]{:S(2)}, u32[]{:S(2)}) collective-permute-start(f32[1,40,128]{2,1,0:T(8,128)S(1)} %get-tuple-element.18), channel_id=1, source_target_pairs={{0,4},{4,8},{8,12},{12,16},{16,20},{20,24},{24,28},{28,0},{1,5},{5... | collective-permute-start | bytes 61448 | tf_op jit(solution)/shard_map/ppermute | solution.py:261
  10.3 5.3 %collective-permute-start.1 = (f32[1,40,128]{2,1,0:T(8,128)S(1)}, f32[1,40,128]{2,1,0:T(8,128)S(1)}, u32[]{:S(2)}, u32[]{:S(2)}) collective-permute-start(f32[1,40,128]{2,1,0:T(8,128)S(1)} %get-tuple-element.19), channel_id=1, source_target_pairs={{0,8},{4,12},{8,16},{12,20},{16,24},{20,28},{24,0},{28,4},{1,9},{5... | collective-permute-start | bytes 61448 | tf_op jit(solution)/shard_map/ppermute | solution.py:261
  10.3 5.5 %collective-permute-start.2 = (f32[1,40,128]{2,1,0:T(8,128)S(1)}, f32[1,40,128]{2,1,0:T(8,128)S(1)}, u32[]{:S(2)}, u32[]{:S(2)}) collective-permute-start(f32[1,40,128]{2,1,0:T(8,128)S(1)} %get-tuple-element.20), channel_id=1, source_target_pairs={{0,12},{4,16},{8,20},{12,24},{16,28},{20,0},{24,4},{28,8},{1,13},{... | collective-permute-start | bytes 61448 | tf_op jit(solution)/shard_map/ppermute | solution.py:261
  11.6 4.2 %collective-permute-start.3 = (f32[1,40,128]{2,1,0:T(8,128)S(1)}, f32[1,40,128]{2,1,0:T(8,128)S(1)}, u32[]{:S(2)}, u32[]{:S(2)}) collective-permute-start(f32[1,40,128]{2,1,0:T(8,128)S(1)} %get-tuple-element.21), channel_id=1, source_target_pairs={{0,16},{4,20},{8,24},{12,28},{16,0},{20,4},{24,8},{28,12},{1,17},{... | collective-permute-start | bytes 61448 | tf_op jit(solution)/shard_map/ppermute | solution.py:261
  12.1 4.1 %collective-permute-start.4 = (f32[1,40,128]{2,1,0:T(8,128)S(1)}, f32[1,40,128]{2,1,0:T(8,128)S(1)}, u32[]{:S(2)}, u32[]{:S(2)}) collective-permute-start(f32[1,40,128]{2,1,0:T(8,128)S(1)} %get-tuple-element.22), channel_id=1, source_target_pairs={{0,20},{4,24},{8,28},{12,0},{16,4},{20,8},{24,12},{28,16},{1,21},{... | collective-permute-start | bytes 61448 | tf_op jit(solution)/shard_map/ppermute | solution.py:261
  14.7 2.4 %collective-permute-start.5 = (f32[1,40,128]{2,1,0:T(8,128)S(1)}, f32[1,40,128]{2,1,0:T(8,128)S(1)}, u32[]{:S(2)}, u32[]{:S(2)}) collective-permute-start(f32[1,40,128]{2,1,0:T(8,128)S(1)} %get-tuple-element.23), channel_id=1, source_target_pairs={{0,24},{4,28},{8,0},{12,4},{16,8},{20,12},{24,16},{28,20},{1,25},{... | collective-permute-start | bytes 61448 | tf_op jit(solution)/shard_map/ppermute | solution.py:261
  15.6 3.8 %collective-permute-start.6 = (f32[1,40,128]{2,1,0:T(8,128)S(1)}, f32[1,40,128]{2,1,0:T(8,128)S(1)}, u32[]{:S(2)}, u32[]{:S(2)}) collective-permute-start(f32[1,40,128]{2,1,0:T(8,128)S(1)} %get-tuple-element.24), channel_id=1, source_target_pairs={{0,28},{4,0},{8,4},{12,8},{16,12},{20,16},{24,20},{28,24},{1,29},{... | collective-permute-start | bytes 61448 | tf_op jit(solution)/shard_map/ppermute | solution.py:261
  19.7 5.8 %collective-permute-start.7 = (f32[72,128]{1,0:T(8,128)S(1)}, f32[72,128]{1,0:T(8,128)S(1)}, u32[]{:S(2)}, u32[]{:S(2)}) collective-permute-start(f32[72,128]{1,0:T(8,128)S(1)} %get-tuple-element.26), channel_id=1, source_target_pairs={{0,1},{1,2},{2,3},{3,0},{4,5},{5,6},{6,7},{7,4},{8,9},{9,10},{10,1... | collective-permute-start | bytes 110600 | tf_op jit(solution)/shard_map/ppermute | solution.py:261
  21.3 4.9 %collective-permute-start.8 = (f32[72,128]{1,0:T(8,128)S(1)}, f32[72,128]{1,0:T(8,128)S(1)}, u32[]{:S(2)}, u32[]{:S(2)}) collective-permute-start(f32[72,128]{1,0:T(8,128)S(1)} %get-tuple-element.27), channel_id=1, source_target_pairs={{0,2},{1,3},{2,0},{3,1},{4,6},{5,7},{6,4},{7,5},{8,10},{9,11},{10,... | collective-permute-start | bytes 110600 | tf_op jit(solution)/shard_map/ppermute | solution.py:261
  23.9 4.0 %collective-permute-start.9 = (f32[72,128]{1,0:T(8,128)S(1)}, f32[72,128]{1,0:T(8,128)S(1)}, u32[]{:S(2)}, u32[]{:S(2)}) collective-permute-start(f32[72,128]{1,0:T(8,128)S(1)} %get-tuple-element.28), channel_id=1, source_target_pairs={{0,3},{1,0},{2,1},{3,2},{4,7},{5,4},{6,5},{7,6},{8,11},{9,8},{10,9... | collective-permute-start | bytes 110600 | tf_op jit(solution)/shard_map/ppermute | solution.py:261

commit v4 on v2

--- a/solution.py
+++ b/solution.py
@@ -161,49 +161,46 @@
         out_ref[dest_ref[k], ROWS:, :] = jnp.where(lane >= LANES - 8, tag, meta)
 
 
-def group_kernel(bricks_dev, in_ref, out_ref):
-    slots = in_ref.shape[0]
-    owners = out_ref.shape[0]
-    table_rows = out_ref.shape[1] - bricks_dev * ROWS
-
-    out_ref[...] = jnp.zeros_like(out_ref)
+def group_kernel(bricks_dev, in_ref, *outs):
+    owners = len(outs)
+    me = lax.axis_index("basis")
+    table_rows = outs[0].shape[0] - bricks_dev * ROWS
     shape = (META, LANES)
     lane = iota(shape, 1)
     index_tag = jnp.full(shape, LANES - 1, jnp.int32)
-
-    def one(s):
+    slots = range(in_ref.shape[0])
+    for b in range(bricks_dev):
+        for d in range(owners):
+            brick = (partner(me, d, owners) * bricks_dev + b).astype(jnp.float32)
+            total = jnp.zeros((ROWS, LANES), jnp.float32)
+            for s in slots:
+                tag = lane_pick(in_ref[s, ROWS:, :], index_tag)
+                hit = jnp.tile(tag, (ROWS // META, 1)) == brick
+                total = total + jnp.where(hit, in_ref[s, :ROWS, :], 0.0)
+            outs[d][b * ROWS : (b + 1) * ROWS, :] = total
+    lines = [jnp.zeros((1, LANES), jnp.float32) for _ in range(table_rows)]
+    for s in slots:
         meta = in_ref[s, ROWS:, :]
-        tag = jnp.tile(lane_pick(meta, index_tag), (ROWS // META, 1))
-        dens = in_ref[s, :ROWS, :]
-        for owner in range(owners):
-            for b in range(bricks_dev):
-                hit = tag == float(owner * bricks_dev + b)
-                out_ref[owner, b * ROWS : (b + 1) * ROWS, :] += jnp.where(hit, dens, 0.0)
         values = lane_pick(meta, lane % 8)
         brick = lane_pick(meta, jnp.full(shape, 8, jnp.int32)).astype(jnp.int32)
         values = jnp.where(brick % 16 == lane // 8, values, 0.0)
         line = brick // 16
         for r in range(table_rows):
             part = jnp.sum(jnp.where(line == r, values, 0.0), axis=0, keepdims=True)
-            out_ref[0, bricks_dev * ROWS + r : bricks_dev * ROWS + r + 1, :] += part
-
-    if slots <= 8:
-        for s in range(slots):
-            one(s)
-    else:
-        pl.loop(0, slots)(one)
-    for owner in range(1, owners):
-        out_ref[owner, bricks_dev * ROWS :, :] = out_ref[0, bricks_dev * ROWS :, :]
-
-
-def cell_kernel(in_ref, cells_ref, refs_ref, out_ref):
-    owners = in_ref.shape[0]
+            lines[r] = lines[r] + part
+    table = jnp.concatenate(lines, axis=0)
+    for out in outs:
+        out[bricks_dev * ROWS :, :] = table
+
+
+def cell_kernel(*refs):
+    *ins, cells_ref, refs_ref, out_ref = refs
     bricks_dev, cells = cells_ref.shape
-    table_rows = in_ref.shape[1] - bricks_dev * ROWS
-
-    total = in_ref[0]
-    for z in range(1, owners):
-        total = total + in_ref[z]
+    table_rows = ins[0].shape[0] - bricks_dev * ROWS
+
+    total = ins[0][...]
+    for part in ins[1:]:
+        total = total + part[...]
     table = total[bricks_dev * ROWS :]
     chunk = (8, LANES)
     refs = [
@@ -240,6 +237,21 @@
         result = jnp.where(hit > 0.5, 0.5 * own + new, own)
         for row in range(ROWS):
             out_ref[b : b + 1, row * LANES : (row + 1) * LANES] = result[row : row + 1, :]
+
+
+def partner(index, shift, count):
+    if count & (count - 1) == 0:
+        return index ^ shift
+    return (index + shift) % count
+
+
+def shifted(pieces, axes):
+    count = len(pieces)
+    moved = list(pieces)
+    for d in range(count - 1, 0, -1):
+        pairs = [(i, partner(i, d, count)) for i in range(count)]
+        moved[d] = lax.ppermute(pieces[d], axes, pairs)
+    return moved
 
 
 def vmem():
@@ -298,21 +310,22 @@
     arrived = lax.all_to_all(outgoing, ("row", "col"), split_axis=0, concat_axis=0, tiled=True)
     partial = pl.pallas_call(
         functools.partial(group_kernel, bricks_dev),
-        out_shape=jax.ShapeDtypeStruct((owners, bricks_dev * ROWS + table_rows, LANES), jnp.float32),
+        out_shape=[jax.ShapeDtypeStruct((bricks_dev * ROWS + table_rows, LANES), jnp.float32)]
+        * owners,
         in_specs=[vmem()],
-        out_specs=vmem(),
+        out_specs=[vmem()] * owners,
         compiler_params=params,
         name="group_sum",
     )(arrived)
-    parts = lax.all_to_all(partial, "basis", split_axis=0, concat_axis=0, tiled=True)
+    parts = shifted(partial, "basis")
     return pl.pallas_call(
         cell_kernel,
         out_shape=jax.ShapeDtypeStruct((bricks_dev, EDGE * FACE), jnp.float32),
-        in_specs=[vmem()] * 3,
+        in_specs=[vmem()] * (owners + 2),
         out_specs=vmem(),
         compiler_params=params,
         name="cells",
-    )(parts, cell_pos, jnp.transpose(corner_refs, (0, 2, 1)))
+    )(*parts, cell_pos, jnp.transpose(corner_refs, (0, 2, 1)))
 
 
 def solution(mesh):

time: 30.8 us -> 29.1 us (0.945)
  blocking collectives: 21.7 us -> 9.99 us
  waiting for transfers between devices: 0 us -> 5.55 us
  starting transfers between devices: 0 us -> 4.45 us
    all_to_all x1 -> x0, blocking collectives: 11.7 us -> none  [body(): lax.all_to_all(partial, 'basis', split_axis=0, concat_axis=0, tiled=True)]
    ppermute x0 -> x3, waiting for transfers between devices: none -> 5.55 us  [shifted(): moved[d] = lax.ppermute(pieces[d], axes, pairs)]
    ppermute x0 -> x3, starting transfers between devices: none -> 4.45 us  [shifted(): moved[d] = lax.ppermute(pieces[d], axes, pairs)]
  transfers between devices with their start and end apart: 0 -> 3, of which waited for: 0 -> 2; matrix products, arithmetic and copies ran while one was open for 0% -> 0% of each run, Pallas kernels for 0% -> 0%
where the time goes in v4:
time: 29.1 us; the launch traced here: 28.8 us
  blocking collectives  9.99 us (34%)
  Pallas kernels  8.81 us (30%)
  waiting for transfers between devices  5.55 us (19%)
  starting transfers between devices  4.45 us (15%)
    all_to_all x1, blocking collectives, body(): lax.all_to_all(outgoing, ('row', 'col'), split_axis=0, concat_axis=0, til...  9.99 us
    pallas_call x1, Pallas kernels, body(): pl.pallas_call(functools.partial(pair_kernel, slot_depth, bricks_group),...  7.23 us
    ppermute x3, waiting for transfers between devices, shifted(): moved[d] = lax.ppermute(pieces[d], axes, pairs)  5.55 us
    ppermute x3, starting transfers between devices, shifted(): moved[d] = lax.ppermute(pieces[d], axes, pairs)  4.45 us
    pallas_call x1, Pallas kernels, body(): pl.pallas_call(cell_kernel, out_shape=jax.ShapeDtypeStruct((bricks_dev, E...  1.33 us
  transfers between devices with their start and end apart: 3, of which 2 were waited for; matrix products, arithmetic and copies ran while one was open for 0% of the time, Pallas kernels for 0%

profile of v4, /device:TPU:0, one launch (start us, length us, event | category | flops | bytes accessed | tf_op | source)
XLA Modules:
  0.0 28.8 jit_solution(11628660350296928277)
XLA Ops:
  0.0 0.0 copy-start
  0.0 0.0 copy-start.1
  0.0 7.2 %pair_density.1 = f32[8,40,128]{2,1,0:T(8,128)S(1)} custom-call(s32[2,8]{1,0:T(2,128)} %bitcast.5, s32[8]{0:T(128)} %dest_hbm.1, s32[8]{0:T(128)} %tag_hbm.1, s32[64]{0:T(128)} %levels_hbm.1, bf16[8,128,128]{2,1,0:T(8,128)(2,1)} %blocks_hbm.1, f32[3,1024,128]{2,1,0:T(8,128)} %bitcast.4, f32[1024,128]{1,0:T(8,128)} %exponents_ref.1), custom_call_target="tpu_custom_call" | custom-call | tf_op jit(solution)/shard_map/pair_density/pallas_call | solution.py:276
  7.2 10.0 %all_to_all.5.in_ref = f32[8,40,128]{2,1,0:T(8,128)S(1)} all-to-all(f32[8,40,128]{2,1,0:T(8,128)S(1)} %pair_density.1), channel_id=1, replica_groups=mesh['row'=4,'col'=2,'basis'=4] {'row','col'}, dimensions={0} | all-to-all | bytes 327680 | tf_op jit(solution)/shard_map/all_to_all | solution.py:310
  17.2 0.3 group_sum.1
  17.5 1.7 %collective-permute-start = (f32[72,128]{1,0:T(8,128)S(1)}, f32[72,128]{1,0:T(8,128)S(1)}, u32[]{:S(2)}, u32[]{:S(2)}) collective-permute-start(f32[72,128]{1,0:T(8,128)S(1)} %get-tuple-element.10), channel_id=1, source_target_pairs={{0,1},{1,0},{2,3},{3,2},{4,5},{5,4},{6,7},{7,6},{8,9},{9,8},{10,11... | collective-permute-start | bytes 110600 | tf_op jit(solution)/shard_map/ppermute | solution.py:253
  19.2 2.6 %collective-permute-start.1 = (f32[72,128]{1,0:T(8,128)S(1)}, f32[72,128]{1,0:T(8,128)S(1)}, u32[]{:S(2)}, u32[]{:S(2)}) collective-permute-start(f32[72,128]{1,0:T(8,128)S(1)} %get-tuple-element.11), channel_id=1, source_target_pairs={{0,2},{1,3},{2,0},{3,1},{4,6},{5,7},{6,4},{7,5},{8,10},{9,11},{10,... | collective-permute-start | bytes 110600 | tf_op jit(solution)/shard_map/ppermute | solution.py:253
  21.7 0.2 collective-permute-start.2
  21.9 0.0 collective-permute-done.refs_1_
  21.9 2.8 %collective-permute-done.1.refs_2_ = f32[72,128]{1,0:T(8,128)S(1)} collective-permute-done((f32[72,128]{1,0:T(8,128)S(1)}, f32[72,128]{1,0:T(8,128)S(1)}, u32[]{:S(2)}, u32[]{:S(2)}) %collective-permute-start.1) | collective-permute-done | bytes 36896 | tf_op jit(solution)/shard_map/ppermute | solution.py:253
  24.7 2.8 %collective-permute-done.2.refs_3_ = f32[72,128]{1,0:T(8,128)S(1)} collective-permute-done((f32[72,128]{1,0:T(8,128)S(1)}, f32[72,128]{1,0:T(8,128)S(1)}, u32[]{:S(2)}, u32[]{:S(2)}) %collective-permute-start.2) | collective-permute-done | bytes 36896 | tf_op jit(solution)/shard_map/ppermute | solution.py:253
  27.5 0.0 copy-done
  27.5 0.0 copy-done.1
  27.5 1.3 %cells.1 = f32[2,4096]{1,0:T(2,128)} custom-call(f32[72,128]{1,0:T(8,128)S(1)} %get-tuple-element.9.refs_0_, f32[72,128]{1,0:T(8,128)S(1)} %collective-permute-done.refs_1_, f32[72,128]{1,0:T(8,128)S(1)} %collective-permute-done.1.refs_2_, f32[72,128]{1,0:T(8,128)S(1)} %collective-permute-done.2.refs_3_, s32[2,256]{1,0:T(2,128)S(1)} %copy-done.1, ...), custom_call_target="tpu_custom_call" | custom-call | tf_op jit(solution)/shard_map/cells/pallas_call | solution.py:321
Async XLA Ops:
  0.0 27.5 %copy-start = (s32[2,256,8]{1,2,0:T(8,128)S(1)}, s32[2,256,8]{1,2,0:T(8,128)}, u32[]{:S(2)}) copy-start(s32[2,256,8]{1,2,0:T(8,128)} %param.17) | copy-start | bytes 49156
  0.0 27.5 %copy-start.1 = (s32[2,256]{1,0:T(2,128)S(1)}, s32[2,256]{1,0:T(2,128)}, u32[]{:S(2)}) copy-start(s32[2,256]{1,0:T(2,128)} %refs_4_.1) | copy-start | bytes 6148
  17.5 4.5 %collective-permute-start = (f32[72,128]{1,0:T(8,128)S(1)}, f32[72,128]{1,0:T(8,128)S(1)}, u32[]{:S(2)}, u32[]{:S(2)}) collective-permute-start(f32[72,128]{1,0:T(8,128)S(1)} %get-tuple-element.10), channel_id=1, source_target_pairs={{0,1},{1,0},{2,3},{3,2},{4,5},{5,4},{6,7},{7,6},{8,9},{9,8},{10,11... | collective-permute-start | bytes 110600 | tf_op jit(solution)/shard_map/ppermute | solution.py:253
  19.2 5.6 %collective-permute-start.1 = (f32[72,128]{1,0:T(8,128)S(1)}, f32[72,128]{1,0:T(8,128)S(1)}, u32[]{:S(2)}, u32[]{:S(2)}) collective-permute-start(f32[72,128]{1,0:T(8,128)S(1)} %get-tuple-element.11), channel_id=1, source_target_pairs={{0,2},{1,3},{2,0},{3,1},{4,6},{5,7},{6,4},{7,5},{8,10},{9,11},{10,... | collective-permute-start | bytes 110600 | tf_op jit(solution)/shard_map/ppermute | solution.py:253
  21.7 5.8 %collective-permute-start.2 = (f32[72,128]{1,0:T(8,128)S(1)}, f32[72,128]{1,0:T(8,128)S(1)}, u32[]{:S(2)}, u32[]{:S(2)}) collective-permute-start(f32[72,128]{1,0:T(8,128)S(1)} %get-tuple-element.12), channel_id=1, source_target_pairs={{0,3},{1,2},{2,1},{3,0},{4,7},{5,6},{6,5},{7,4},{8,11},{9,10},{10,... | collective-permute-start | bytes 110600 | tf_op jit(solution)/shard_map/ppermute | solution.py:253

commit v5 on v4

--- a/solution.py
+++ b/solution.py
@@ -96,11 +96,13 @@
         out_ref[...] = jnp.zeros_like(out_ref)
     steps = iota((EDGE, LANES), 0).astype(jnp.float32) - (EDGE - 1) / 2.0
 
-    @pl.loop(0, items)
-    def _(k):
+    for k in range(items):
         for side in range(2):
             for copy in copies(k, side):
                 copy.wait()
+        block_copy(k).wait()
+
+    def one(k):
         slot = dest_ref[k]
         target = slot // slot_depth * bricks_group + tag_ref[k]
         spacing = jnp.where(levels_ref[target] == 1, COARSE * 0.5, COARSE)
@@ -119,7 +121,6 @@
         col_x, col_face = factors(1)
         row_x = row_x.T
         row_face = row_face.T
-        block_copy(k).wait()
         block = blocks_ref[k]
         for x in range(EDGE):
             col = (col_x[x : x + 1, :] * col_face).astype(jnp.bfloat16)
@@ -132,6 +133,9 @@
                 out_ref[slot, pl.ds(2 * x + half, 1), :] = piece
                 if x in (0, EDGE - 1):
                     corner_buf[2 * (x // (EDGE - 1)) + half, pl.ds(k, 1), :] = piece
+
+    for k in range(items):
+        one(k)
 
     shape = (items, LANES)
     lane = iota(shape, 1)

time: 29.1 us -> 28.2 us (0.969)
  Pallas kernels: 8.81 us -> 7.89 us
    pallas_call x1, Pallas kernels: 7.23 us -> 6.3 us  [body(): pl.pallas_call(functools.partial(pair_kernel, slot_depth, bricks_group),...]
where the time goes in v5:
time: 28.2 us; the launch traced here: 27.9 us
  blocking collectives  10 us (35%)
  Pallas kernels  7.89 us (28%)
  waiting for transfers between devices  5.53 us (20%)
  starting transfers between devices  4.45 us (16%)
    all_to_all x1, blocking collectives, body(): lax.all_to_all(outgoing, ('row', 'col'), split_axis=0, concat_axis=0, til...  10 us
    pallas_call x1, Pallas kernels, body(): pl.pallas_call(functools.partial(pair_kernel, slot_depth, bricks_group),...  6.3 us
    ppermute x3, waiting for transfers between devices, shifted(): moved[d] = lax.ppermute(pieces[d], axes, pairs)  5.53 us
    ppermute x3, starting transfers between devices, shifted(): moved[d] = lax.ppermute(pieces[d], axes, pairs)  4.45 us
    pallas_call x1, Pallas kernels, body(): pl.pallas_call(cell_kernel, out_shape=jax.ShapeDtypeStruct((bricks_dev, E...  1.33 us
  transfers between devices with their start and end apart: 3, of which 2 were waited for; matrix products, arithmetic and copies ran while one was open for 0% of the time, Pallas kernels for 0%

profile of v5, /device:TPU:0, one launch (start us, length us, event | category | flops | bytes accessed | tf_op | source)
XLA Modules:
  0.0 27.9 jit_solution(14849794198816565332)
XLA Ops:
  0.0 0.0 copy-start
  0.0 0.0 copy-start.1
  0.0 6.3 %pair_density.1 = f32[8,40,128]{2,1,0:T(8,128)S(1)} custom-call(s32[2,8]{1,0:T(2,128)} %bitcast.5, s32[8]{0:T(128)} %dest_hbm.1, s32[8]{0:T(128)} %tag_hbm.1, s32[64]{0:T(128)} %levels_hbm.1, bf16[8,128,128]{2,1,0:T(8,128)(2,1)} %blocks_hbm.1, f32[3,1024,128]{2,1,0:T(8,128)} %bitcast.4, f32[1024,128]{1,0:T(8,128)} %exponents_ref.1), custom_call_target="tpu_custom_call" | custom-call | tf_op jit(solution)/shard_map/pair_density/pallas_call | solution.py:280
  6.3 10.0 %all_to_all.5.in_ref = f32[8,40,128]{2,1,0:T(8,128)S(1)} all-to-all(f32[8,40,128]{2,1,0:T(8,128)S(1)} %pair_density.1), channel_id=1, replica_groups=mesh['row'=4,'col'=2,'basis'=4] {'row','col'}, dimensions={0} | all-to-all | bytes 327680 | tf_op jit(solution)/shard_map/all_to_all | solution.py:314
  16.3 0.3 group_sum.1
  16.6 1.6 %collective-permute-start = (f32[72,128]{1,0:T(8,128)S(1)}, f32[72,128]{1,0:T(8,128)S(1)}, u32[]{:S(2)}, u32[]{:S(2)}) collective-permute-start(f32[72,128]{1,0:T(8,128)S(1)} %get-tuple-element.10), channel_id=1, source_target_pairs={{0,1},{1,0},{2,3},{3,2},{4,5},{5,4},{6,7},{7,6},{8,9},{9,8},{10,11... | collective-permute-start | bytes 110600 | tf_op jit(solution)/shard_map/ppermute | solution.py:257
  18.2 2.6 %collective-permute-start.1 = (f32[72,128]{1,0:T(8,128)S(1)}, f32[72,128]{1,0:T(8,128)S(1)}, u32[]{:S(2)}, u32[]{:S(2)}) collective-permute-start(f32[72,128]{1,0:T(8,128)S(1)} %get-tuple-element.11), channel_id=1, source_target_pairs={{0,2},{1,3},{2,0},{3,1},{4,6},{5,7},{6,4},{7,5},{8,10},{9,11},{10,... | collective-permute-start | bytes 110600 | tf_op jit(solution)/shard_map/ppermute | solution.py:257
  20.8 0.2 collective-permute-start.2
  21.0 0.0 collective-permute-done.refs_1_
  21.0 2.8 %collective-permute-done.1.refs_2_ = f32[72,128]{1,0:T(8,128)S(1)} collective-permute-done((f32[72,128]{1,0:T(8,128)S(1)}, f32[72,128]{1,0:T(8,128)S(1)}, u32[]{:S(2)}, u32[]{:S(2)}) %collective-permute-start.1) | collective-permute-done | bytes 36896 | tf_op jit(solution)/shard_map/ppermute | solution.py:257
  23.8 2.8 %collective-permute-done.2.refs_3_ = f32[72,128]{1,0:T(8,128)S(1)} collective-permute-done((f32[72,128]{1,0:T(8,128)S(1)}, f32[72,128]{1,0:T(8,128)S(1)}, u32[]{:S(2)}, u32[]{:S(2)}) %collective-permute-start.2) | collective-permute-done | bytes 36896 | tf_op jit(solution)/shard_map/ppermute | solution.py:257
  26.6 0.0 copy-done
  26.6 0.0 copy-done.1
  26.6 1.3 %cells.1 = f32[2,4096]{1,0:T(2,128)} custom-call(f32[72,128]{1,0:T(8,128)S(1)} %get-tuple-element.9.refs_0_, f32[72,128]{1,0:T(8,128)S(1)} %collective-permute-done.refs_1_, f32[72,128]{1,0:T(8,128)S(1)} %collective-permute-done.1.refs_2_, f32[72,128]{1,0:T(8,128)S(1)} %collective-permute-done.2.refs_3_, s32[2,256]{1,0:T(2,128)S(1)} %copy-done.1, ...), custom_call_target="tpu_custom_call" | custom-call | tf_op jit(solution)/shard_map/cells/pallas_call | solution.py:325
Async XLA Ops:
  0.0 26.6 %copy-start = (s32[2,256,8]{1,2,0:T(8,128)S(1)}, s32[2,256,8]{1,2,0:T(8,128)}, u32[]{:S(2)}) copy-start(s32[2,256,8]{1,2,0:T(8,128)} %param.17) | copy-start | bytes 49156
  0.0 26.6 %copy-start.1 = (s32[2,256]{1,0:T(2,128)S(1)}, s32[2,256]{1,0:T(2,128)}, u32[]{:S(2)}) copy-start(s32[2,256]{1,0:T(2,128)} %refs_4_.1) | copy-start | bytes 6148
  16.6 4.5 %collective-permute-start = (f32[72,128]{1,0:T(8,128)S(1)}, f32[72,128]{1,0:T(8,128)S(1)}, u32[]{:S(2)}, u32[]{:S(2)}) collective-permute-start(f32[72,128]{1,0:T(8,128)S(1)} %get-tuple-element.10), channel_id=1, source_target_pairs={{0,1},{1,0},{2,3},{3,2},{4,5},{5,4},{6,7},{7,6},{8,9},{9,8},{10,11... | collective-permute-start | bytes 110600 | tf_op jit(solution)/shard_map/ppermute | solution.py:257
  18.2 5.6 %collective-permute-start.1 = (f32[72,128]{1,0:T(8,128)S(1)}, f32[72,128]{1,0:T(8,128)S(1)}, u32[]{:S(2)}, u32[]{:S(2)}) collective-permute-start(f32[72,128]{1,0:T(8,128)S(1)} %get-tuple-element.11), channel_id=1, source_target_pairs={{0,2},{1,3},{2,0},{3,1},{4,6},{5,7},{6,4},{7,5},{8,10},{9,11},{10,... | collective-permute-start | bytes 110600 | tf_op jit(solution)/shard_map/ppermute | solution.py:257
  20.8 5.8 %collective-permute-start.2 = (f32[72,128]{1,0:T(8,128)S(1)}, f32[72,128]{1,0:T(8,128)S(1)}, u32[]{:S(2)}, u32[]{:S(2)}) collective-permute-start(f32[72,128]{1,0:T(8,128)S(1)} %get-tuple-element.12), channel_id=1, source_target_pairs={{0,3},{1,2},{2,1},{3,0},{4,7},{5,6},{6,5},{7,4},{8,11},{9,10},{10,... | collective-permute-start | bytes 110600 | tf_op jit(solution)/shard_map/ppermute | solution.py:257

commit v6 on v5

--- a/solution.py
+++ b/solution.py
@@ -12,8 +12,7 @@
 LANES = 128
 ROWS = EDGE * FACE // LANES
 COARSE = 0.2
-META = 8
-SLOT_ROWS = ROWS + META
+TILE = 8
 
 
 def lane_pick(values, index):
@@ -30,6 +29,7 @@
 
 def pair_kernel(
     slot_depth,
+    width,
     bricks_group,
     pairs_hbm,
     dest_hbm,
@@ -52,7 +52,8 @@
     block_sems,
 ):
     items = blocks_ref.shape[0]
-    slots = out_ref.shape[0]
+    part_rows = ROWS // width
+    chunks = out_ref.shape[0] // (part_rows + 1)
     lists = [
         pltpu.make_async_copy(source, target, list_sems.at[n])
         for n, (source, target) in enumerate(
@@ -92,8 +93,14 @@
                 copy.start()
     for copy in lists[1:]:
         copy.wait()
-    if slots != items:
+    if chunks != items * width:
         out_ref[...] = jnp.zeros_like(out_ref)
+
+    def first_row(k, part):
+        slot = dest_ref[k]
+        chunk = (slot // slot_depth * width + part) * slot_depth + lax.rem(slot, slot_depth)
+        return chunk * (part_rows + 1)
+
     steps = iota((EDGE, LANES), 0).astype(jnp.float32) - (EDGE - 1) / 2.0
 
     for k in range(items):
@@ -103,8 +110,7 @@
         block_copy(k).wait()
 
     def one(k):
-        slot = dest_ref[k]
-        target = slot // slot_depth * bricks_group + tag_ref[k]
+        target = dest_ref[k] // slot_depth * bricks_group + tag_ref[k]
         spacing = jnp.where(levels_ref[target] == 1, COARSE * 0.5, COARSE)
         coords = steps * spacing
 
@@ -130,7 +136,8 @@
             dens = jnp.sum(row_x[:, x : x + 1] * row_face * product, axis=0, keepdims=True)
             for half in range(FACE // LANES):
                 piece = dens[:, half * LANES : (half + 1) * LANES]
-                out_ref[slot, pl.ds(2 * x + half, 1), :] = piece
+                part, row = divmod(2 * x + half, part_rows)
+                out_ref[pl.ds(first_row(k, part) + row, 1), :] = piece
                 if x in (0, EDGE - 1):
                     corner_buf[2 * (x // (EDGE - 1)) + half, pl.ds(k, 1), :] = piece
 
@@ -153,59 +160,84 @@
     for k in range(items):
         target = dest_ref[k] // slot_depth * bricks_group + tag_ref[k]
         brick = jnp.where(row == k, target, brick)
-    meta = jnp.where(lane < 8, values, brick.astype(jnp.float32))
-    if slots != items:
-
-        @pl.loop(0, slots)
-        def _(s):
-            out_ref[s, ROWS:, :] = jnp.where(lane >= LANES - 8, -1.0, meta)
-
-    for k in range(items):
-        tag = tag_ref[k].astype(jnp.float32)
-        out_ref[dest_ref[k], ROWS:, :] = jnp.where(lane >= LANES - 8, tag, meta)
-
-
-def group_kernel(bricks_dev, in_ref, *outs):
+    placed = jnp.where(lane // 8 == row, values, 0.0)
+    placed = jnp.where(lane == 8 * items + row, brick.astype(jnp.float32), placed)
+    meta = jnp.sum(placed, axis=0, keepdims=True)
+    last_lane = iota((1, LANES), 1) == LANES - 1
+    if chunks != items * width:
+
+        @pl.loop(0, chunks)
+        def _(n):
+            out_ref[pl.ds(n * (part_rows + 1) + part_rows, 1), :] = jnp.where(
+                last_lane, -1.0, meta
+            )
+
+    for k in range(items):
+        tagged = jnp.where(last_lane, tag_ref[k].astype(jnp.float32), meta)
+        for part in range(width):
+            out_ref[pl.ds(first_row(k, part) + part_rows, 1), :] = tagged
+
+
+def group_kernel(items, bricks_dev, width, in_ref, *outs):
     owners = len(outs)
     me = lax.axis_index("basis")
-    table_rows = outs[0].shape[0] - bricks_dev * ROWS
-    shape = (META, LANES)
+    part_rows = ROWS // width
+    chunks = in_ref.shape[0] // (part_rows + 1)
+    meta = [
+        in_ref[n * (part_rows + 1) + part_rows : (n + 1) * (part_rows + 1), :]
+        for n in range(chunks)
+    ]
+    tags = [
+        jnp.broadcast_to(line[:, LANES - 1 :], (part_rows, LANES)) for line in meta
+    ]
+    for d in range(owners):
+        for b in range(bricks_dev):
+            brick = (owner_of(me, d, owners, width) * bricks_dev + b).astype(jnp.float32)
+            total = jnp.zeros((part_rows, LANES), jnp.float32)
+            for n in range(chunks):
+                dens = in_ref[n * (part_rows + 1) : n * (part_rows + 1) + part_rows, :]
+                total = total + jnp.where(tags[n] == brick, dens, 0.0)
+            outs[d][b * part_rows : (b + 1) * part_rows, :] = total
+    table_rows = outs[0].shape[0] - bricks_dev * part_rows
+    shape = (TILE, LANES)
     lane = iota(shape, 1)
-    index_tag = jnp.full(shape, LANES - 1, jnp.int32)
-    slots = range(in_ref.shape[0])
-    for b in range(bricks_dev):
-        for d in range(owners):
-            brick = (partner(me, d, owners) * bricks_dev + b).astype(jnp.float32)
-            total = jnp.zeros((ROWS, LANES), jnp.float32)
-            for s in slots:
-                tag = lane_pick(in_ref[s, ROWS:, :], index_tag)
-                hit = jnp.tile(tag, (ROWS // META, 1)) == brick
-                total = total + jnp.where(hit, in_ref[s, :ROWS, :], 0.0)
-            outs[d][b * ROWS : (b + 1) * ROWS, :] = total
-    lines = [jnp.zeros((1, LANES), jnp.float32) for _ in range(table_rows)]
-    for s in slots:
-        meta = in_ref[s, ROWS:, :]
-        values = lane_pick(meta, lane % 8)
-        brick = lane_pick(meta, jnp.full(shape, 8, jnp.int32)).astype(jnp.int32)
-        values = jnp.where(brick % 16 == lane // 8, values, 0.0)
-        line = brick // 16
-        for r in range(table_rows):
-            part = jnp.sum(jnp.where(line == r, values, 0.0), axis=0, keepdims=True)
-            lines[r] = lines[r] + part
-    table = jnp.concatenate(lines, axis=0)
-    for out in outs:
-        out[bricks_dev * ROWS :, :] = table
-
-
-def cell_kernel(*refs):
+    lines = [jnp.zeros(shape, jnp.float32) for _ in range(table_rows)]
+    for first in range(0, chunks, TILE):
+        block = jnp.concatenate(meta[first : first + TILE], axis=0)
+        for k in range(items):
+            values = lane_pick(block, 8 * k + lane % 8)
+            brick = lane_pick(block, jnp.full(shape, 8 * items + k, jnp.int32)).astype(jnp.int32)
+            values = jnp.where(brick % 16 == lane // 8, values, 0.0)
+            for r in range(table_rows):
+                lines[r] = lines[r] + jnp.where(brick // 16 == r, values, 0.0)
+    table = jnp.concatenate([jnp.sum(line, axis=0, keepdims=True) for line in lines], axis=0)
+    for out in outs[::width]:
+        out[bricks_dev * part_rows :, :] = table
+
+
+def cell_kernel(width, *refs):
     *ins, cells_ref, refs_ref, out_ref = refs
     bricks_dev, cells = cells_ref.shape
-    table_rows = ins[0].shape[0] - bricks_dev * ROWS
-
-    total = ins[0][...]
-    for part in ins[1:]:
-        total = total + part[...]
-    table = total[bricks_dev * ROWS :]
+    part_rows = ROWS // width
+    table_rows = ins[0].shape[0] - bricks_dev * part_rows
+    mine = lax.axis_index("basis") % width
+
+    totals = []
+    for offset in range(width):
+        total = ins[offset][...]
+        for part in ins[offset + width :: width]:
+            total = total + part[...]
+        totals.append(total)
+    table = totals[0][bricks_dev * part_rows :]
+
+    def own_points(b):
+        halves = [total[b * part_rows : (b + 1) * part_rows] for total in totals]
+        if width == 1:
+            return halves[0]
+        straight = jnp.concatenate(halves, axis=0)
+        crossed = jnp.concatenate(halves[::-1], axis=0)
+        return jnp.where(mine == 0, straight, crossed)
+
     chunk = (8, LANES)
     refs = [
         [refs_ref[b, :, c * LANES : (c + 1) * LANES] for c in range(cells // LANES)]
@@ -237,24 +269,26 @@
 
         hit = spread(here.astype(jnp.float32))
         new = spread(jnp.where(here, mean, 0.0))
-        own = total[b * ROWS : (b + 1) * ROWS]
+        own = own_points(b)
         result = jnp.where(hit > 0.5, 0.5 * own + new, own)
         for row in range(ROWS):
             out_ref[b : b + 1, row * LANES : (row + 1) * LANES] = result[row : row + 1, :]
 
 
-def partner(index, shift, count):
-    if count & (count - 1) == 0:
-        return index ^ shift
-    return (index + shift) % count
-
-
-def shifted(pieces, axes):
-    count = len(pieces)
+def owner_of(index, shift, owners, width):
+    sets = owners // width
+    pair, side = index // width, index % width
+    jump, turn = divmod(shift, width)
+    pair = pair ^ jump if sets & (sets - 1) == 0 else (pair + jump) % sets
+    return pair * width + (side ^ turn)
+
+
+def shifted(pieces, axis, width):
+    owners = len(pieces)
     moved = list(pieces)
-    for d in range(count - 1, 0, -1):
-        pairs = [(i, partner(i, d, count)) for i in range(count)]
-        moved[d] = lax.ppermute(pieces[d], axes, pairs)
+    for d in range(owners - 1, 0, -1):
+        pairs = [(i, owner_of(i, d, owners, width)) for i in range(owners)]
+        moved[d] = lax.ppermute(pieces[d], axis, pairs)
     return moved
 
 
@@ -275,11 +309,14 @@
     bricks_dev = bricks_group // owners
     table_rows = -(-bricks * 8 // (8 * LANES)) * 8
     basis = block_data.shape[1]
+    width = 2 if owners % 2 == 0 else 1
+    part_rows = ROWS // width
+    chunks = slots * width
     params = pltpu.CompilerParams(vmem_limit_bytes=32 * 1024 * 1024)
 
     outgoing = pl.pallas_call(
-        functools.partial(pair_kernel, slot_depth, bricks_group),
-        out_shape=jax.ShapeDtypeStruct((slots, SLOT_ROWS, LANES), jnp.float32),
+        functools.partial(pair_kernel, slot_depth, width, bricks_group),
+        out_shape=jax.ShapeDtypeStruct((chunks * (part_rows + 1), LANES), jnp.float32),
         in_specs=[pl.BlockSpec(memory_space=pltpu.HBM)] * 7,
         out_specs=vmem(),
         scratch_shapes=[
@@ -311,19 +348,34 @@
             )
         )
     )
-    arrived = lax.all_to_all(outgoing, ("row", "col"), split_axis=0, concat_axis=0, tiled=True)
+    sets = [
+        [g * owners + first + side for g in range(groups) for side in range(width)]
+        for first in range(0, owners, width)
+    ]
+    arrived = lax.all_to_all(
+        outgoing.reshape(chunks, 1, (part_rows + 1) * LANES),
+        ("row", "col", "basis"),
+        split_axis=0,
+        concat_axis=0,
+        tiled=True,
+        axis_index_groups=sets,
+    ).reshape(outgoing.shape)
     partial = pl.pallas_call(
-        functools.partial(group_kernel, bricks_dev),
-        out_shape=[jax.ShapeDtypeStruct((bricks_dev * ROWS + table_rows, LANES), jnp.float32)]
-        * owners,
+        functools.partial(group_kernel, items, bricks_dev, width),
+        out_shape=[
+            jax.ShapeDtypeStruct(
+                (bricks_dev * part_rows + (0 if d % width else table_rows), LANES), jnp.float32
+            )
+            for d in range(owners)
+        ],
         in_specs=[vmem()],
         out_specs=[vmem()] * owners,
         compiler_params=params,
         name="group_sum",
     )(arrived)
-    parts = shifted(partial, "basis")
+    parts = shifted(partial, "basis", width)
     return pl.pallas_call(
-        cell_kernel,
+        functools.partial(cell_kernel, width),
         out_shape=jax.ShapeDtypeStruct((bricks_dev, EDGE * FACE), jnp.float32),
         in_specs=[vmem()] * (owners + 2),
         out_specs=vmem(),

time: 28.2 us -> 29.2 us (1.035)
  blocking collectives: 10 us -> 12 us
  waiting for transfers between devices: 5.53 us -> 4.49 us
    all_to_all x1, blocking collectives: 10 us -> 12 us  [body(): lax.all_to_all(outgoing.reshape(chunks, 1, (part_rows + 1) * LANES), ('ro...]
    ppermute x3, waiting for transfers between devices: 5.53 us -> 4.49 us  [shifted(): moved[d] = lax.ppermute(pieces[d], axis, pairs)]
where the time goes in v6:
time: 29.2 us; the launch traced here: 28.9 us
  blocking collectives  12 us (41%)
  Pallas kernels  7.9 us (27%)
  waiting for transfers between devices  4.49 us (15%)
  starting transfers between devices  4.45 us (15%)
    all_to_all x1, blocking collectives, body(): lax.all_to_all(outgoing.reshape(chunks, 1, (part_rows + 1) * LANES), ('ro...  12 us
    pallas_call x1, Pallas kernels, body(): pl.pallas_call(functools.partial(pair_kernel, slot_depth, width, bricks_g...  6.27 us
    ppermute x3, waiting for transfers between devices, shifted(): moved[d] = lax.ppermute(pieces[d], axis, pairs)  4.49 us
    ppermute x3, starting transfers between devices, shifted(): moved[d] = lax.ppermute(pieces[d], axis, pairs)  4.45 us
    pallas_call x1, Pallas kernels, body(): pl.pallas_call(functools.partial(cell_kernel, width), out_shape=jax.Shape...  1.33 us
  transfers between devices with their start and end apart: 3, of which 2 were waited for; matrix products, arithmetic and copies ran while one was open for 0% of the time, Pallas kernels for 0%

profile of v6, /device:TPU:0, one launch (start us, length us, event | category | flops | bytes accessed | tf_op | source)
XLA Modules:
  0.0 28.9 jit_solution(912270643563586534)
XLA Ops:
  0.0 0.0 copy-start
  0.0 0.0 copy-start.1
  0.0 6.3 %pair_density.1 = f32[272,128]{1,0:T(8,128)S(1)} custom-call(s32[2,8]{1,0:T(2,128)} %bitcast.9, s32[8]{0:T(128)} %dest_hbm.1, s32[8]{0:T(128)} %tag_hbm.1, s32[64]{0:T(128)} %levels_hbm.1, bf16[8,128,128]{2,1,0:T(8,128)(2,1)} %blocks_hbm.1, f32[3,1024,128]{2,1,0:T(8,128)} %bitcast.8, f32[1024,128]{1,0:T(8,128)} %exponents_ref.1), custom_call_target="tpu_custom_call" | custom-call | tf_op jit(solution)/shard_map/pair_density/pallas_call | solution.py:317
  6.3 12.0 %all_to_all.5 = f32[16,1,2176]{2,1,0:T(1,128)S(1)} all-to-all(f32[16,1,2176]{2,1,0:T(1,128)S(1)} %bitcast.5), channel_id=1, replica_groups={{0,1,4,5,8,9,12,13,16,17,20,21,24,25,28,29},{2,3,6,7,10,11,14,15,18,19,..., dimensions={0} | all-to-all | bytes 278528 | tf_op jit(solution)/shard_map/all_to_all | solution.py:355
  18.3 0.3 %group_sum.1 = (f32[40,128]{1,0:T(8,128)S(1)}, f32[32,128]{1,0:T(8,128)S(1)}, f32[40,128]{1,0:T(8,128)S(1)}, f32[32,128]{1,0:T(8,128)S(1)}) custom-call(f32[272,128]{1,0:T(8,128)S(1)} %bitcast.6), custom_call_target="tpu_custom_call" | custom-call | tf_op jit(solution)/shard_map/group_sum/pallas_call | solution.py:363
  18.6 2.7 %collective-permute-start.1 = (f32[40,128]{1,0:T(8,128)S(1)}, f32[40,128]{1,0:T(8,128)S(1)}, u32[]{:S(2)}, u32[]{:S(2)}) collective-permute-start(f32[40,128]{1,0:T(8,128)S(1)} %get-tuple-element.11), channel_id=1, source_target_pairs={{0,2},{1,3},{2,0},{3,1},{4,6},{5,7},{6,4},{7,5},{8,10},{9,11},{10,... | collective-permute-start | bytes 61448 | tf_op jit(solution)/shard_map/ppermute | solution.py:291
  21.3 0.7 %collective-permute-start = (f32[32,128]{1,0:T(8,128)S(1)}, f32[32,128]{1,0:T(8,128)S(1)}, u32[]{:S(2)}, u32[]{:S(2)}) collective-permute-start(f32[32,128]{1,0:T(8,128)S(1)} %get-tuple-element.10), channel_id=1, source_target_pairs={{0,1},{1,0},{2,3},{3,2},{4,5},{5,4},{6,7},{7,6},{8,9},{9,8},{10,11... | collective-permute-start | bytes 49160 | tf_op jit(solution)/shard_map/ppermute | solution.py:291
  22.0 1.0 %collective-permute-start.2 = (f32[32,128]{1,0:T(8,128)S(1)}, f32[32,128]{1,0:T(8,128)S(1)}, u32[]{:S(2)}, u32[]{:S(2)}) collective-permute-start(f32[32,128]{1,0:T(8,128)S(1)} %get-tuple-element.12), channel_id=1, source_target_pairs={{0,3},{1,2},{2,1},{3,0},{4,7},{5,6},{6,5},{7,4},{8,11},{9,10},{10,... | collective-permute-start | bytes 49160 | tf_op jit(solution)/shard_map/ppermute | solution.py:291
  23.1 1.9 %collective-permute-done.refs_1_ = f32[32,128]{1,0:T(8,128)S(1)} collective-permute-done((f32[32,128]{1,0:T(8,128)S(1)}, f32[32,128]{1,0:T(8,128)S(1)}, u32[]{:S(2)}, u32[]{:S(2)}) %collective-permute-start) | collective-permute-done | bytes 16416 | tf_op jit(solution)/shard_map/ppermute | solution.py:291
  25.0 2.5 %collective-permute-done.2.refs_3_ = f32[32,128]{1,0:T(8,128)S(1)} collective-permute-done((f32[32,128]{1,0:T(8,128)S(1)}, f32[32,128]{1,0:T(8,128)S(1)}, u32[]{:S(2)}, u32[]{:S(2)}) %collective-permute-start.2) | collective-permute-done | bytes 16416 | tf_op jit(solution)/shard_map/ppermute | solution.py:291
  27.6 0.0 collective-permute-done.1.refs_2_
  27.6 0.0 copy-done
  27.6 0.0 copy-done.1
  27.6 1.3 %cells.1 = f32[2,4096]{1,0:T(2,128)} custom-call(f32[40,128]{1,0:T(8,128)S(1)} %get-tuple-element.9.refs_0_, f32[32,128]{1,0:T(8,128)S(1)} %collective-permute-done.refs_1_, f32[40,128]{1,0:T(8,128)S(1)} %collective-permute-done.1.refs_2_, f32[32,128]{1,0:T(8,128)S(1)} %collective-permute-done.2.refs_3_, s32[2,256]{1,0:T(2,128)S(1)} %copy-done.1, ...), custom_call_target="tpu_custom_call" | custom-call | tf_op jit(solution)/shard_map/cells/pallas_call | solution.py:377
Async XLA Ops:
  0.0 27.6 %copy-start = (s32[2,256,8]{1,2,0:T(8,128)S(1)}, s32[2,256,8]{1,2,0:T(8,128)}, u32[]{:S(2)}) copy-start(s32[2,256,8]{1,2,0:T(8,128)} %param.17) | copy-start | bytes 49156
  0.0 27.6 %copy-start.1 = (s32[2,256]{1,0:T(2,128)S(1)}, s32[2,256]{1,0:T(2,128)}, u32[]{:S(2)}) copy-start(s32[2,256]{1,0:T(2,128)} %refs_4_.1) | copy-start | bytes 6148
  18.6 8.9 %collective-permute-start.1 = (f32[40,128]{1,0:T(8,128)S(1)}, f32[40,128]{1,0:T(8,128)S(1)}, u32[]{:S(2)}, u32[]{:S(2)}) collective-permute-start(f32[40,128]{1,0:T(8,128)S(1)} %get-tuple-element.11), channel_id=1, source_target_pairs={{0,2},{1,3},{2,0},{3,1},{4,6},{5,7},{6,4},{7,5},{8,10},{9,11},{10,... | collective-permute-start | bytes 61448 | tf_op jit(solution)/shard_map/ppermute | solution.py:291
  21.3 3.7 %collective-permute-start = (f32[32,128]{1,0:T(8,128)S(1)}, f32[32,128]{1,0:T(8,128)S(1)}, u32[]{:S(2)}, u32[]{:S(2)}) collective-permute-start(f32[32,128]{1,0:T(8,128)S(1)} %get-tuple-element.10), channel_id=1, source_target_pairs={{0,1},{1,0},{2,3},{3,2},{4,5},{5,4},{6,7},{7,6},{8,9},{9,8},{10,11... | collective-permute-start | bytes 49160 | tf_op jit(solution)/shard_map/ppermute | solution.py:291
  22.0 5.5 %collective-permute-start.2 = (f32[32,128]{1,0:T(8,128)S(1)}, f32[32,128]{1,0:T(8,128)S(1)}, u32[]{:S(2)}, u32[]{:S(2)}) collective-permute-start(f32[32,128]{1,0:T(8,128)S(1)} %get-tuple-element.12), channel_id=1, source_target_pairs={{0,3},{1,2},{2,1},{3,0},{4,7},{5,6},{6,5},{7,4},{8,11},{9,10},{10,... | collective-permute-start | bytes 49160 | tf_op jit(solution)/shard_map/ppermute | solution.py:291

commit v7 on v6

--- a/solution.py
+++ b/solution.py
@@ -178,8 +178,7 @@
             out_ref[pl.ds(first_row(k, part) + part_rows, 1), :] = tagged
 
 
-def group_kernel(items, bricks_dev, width, in_ref, *outs):
-    owners = len(outs)
+def group_kernel(items, bricks_dev, width, owners, shifts, in_ref, *outs):
     me = lax.axis_index("basis")
     part_rows = ROWS // width
     chunks = in_ref.shape[0] // (part_rows + 1)
@@ -197,7 +196,9 @@
             for n in range(chunks):
                 dens = in_ref[n * (part_rows + 1) : n * (part_rows + 1) + part_rows, :]
                 total = total + jnp.where(tags[n] == brick, dens, 0.0)
-            outs[d][b * part_rows : (b + 1) * part_rows, :] = total
+            for out, shift in zip(outs, shifts):
+                if shift == d:
+                    out[b * part_rows : (b + 1) * part_rows, :] = total
     table_rows = outs[0].shape[0] - bricks_dev * part_rows
     shape = (TILE, LANES)
     lane = iota(shape, 1)
@@ -211,8 +212,9 @@
             for r in range(table_rows):
                 lines[r] = lines[r] + jnp.where(brick // 16 == r, values, 0.0)
     table = jnp.concatenate([jnp.sum(line, axis=0, keepdims=True) for line in lines], axis=0)
-    for out in outs[::width]:
-        out[bricks_dev * part_rows :, :] = table
+    for out, shift in zip(outs, shifts):
+        if shift % width == 0:
+            out[bricks_dev * part_rows :, :] = table
 
 
 def cell_kernel(width, *refs):
@@ -283,13 +285,15 @@
     return pair * width + (side ^ turn)
 
 
-def shifted(pieces, axis, width):
-    owners = len(pieces)
-    moved = list(pieces)
-    for d in range(owners - 1, 0, -1):
-        pairs = [(i, owner_of(i, d, owners, width)) for i in range(owners)]
-        moved[d] = lax.ppermute(pieces[d], axis, pairs)
-    return moved
+def exchanges(owners, width):
+    if width > 1 or owners & (owners - 1) or owners > 8:
+        return [
+            (d, [(i, owner_of(i, d, owners, width)) for i in range(owners)])
+            for d in range(1, owners)
+        ]
+    return [
+        (low ^ high, [(low, high), (high, low)]) for high in range(1, owners) for low in range(high)
+    ]
 
 
 def vmem():
@@ -309,7 +313,7 @@
     bricks_dev = bricks_group // owners
     table_rows = -(-bricks * 8 // (8 * LANES)) * 8
     basis = block_data.shape[1]
-    width = 2 if owners % 2 == 0 else 1
+    width = 1
     part_rows = ROWS // width
     chunks = slots * width
     params = pltpu.CompilerParams(vmem_limit_bytes=32 * 1024 * 1024)
@@ -360,24 +364,28 @@
         tiled=True,
         axis_index_groups=sets,
     ).reshape(outgoing.shape)
+    moves = exchanges(owners, width)
+    shifts = [0] + [d for d, _ in moves]
     partial = pl.pallas_call(
-        functools.partial(group_kernel, items, bricks_dev, width),
+        functools.partial(group_kernel, items, bricks_dev, width, owners, shifts),
         out_shape=[
             jax.ShapeDtypeStruct(
                 (bricks_dev * part_rows + (0 if d % width else table_rows), LANES), jnp.float32
             )
-            for d in range(owners)
+            for d in shifts
         ],
         in_specs=[vmem()],
-        out_specs=[vmem()] * owners,
+        out_specs=[vmem()] * len(shifts),
         compiler_params=params,
         name="group_sum",
     )(arrived)
-    parts = shifted(partial, "basis", width)
+    parts = [partial[0]] + [
+        lax.ppermute(piece, "basis", pairs) for piece, (_, pairs) in zip(partial[1:], moves)
+    ]
     return pl.pallas_call(
         functools.partial(cell_kernel, width),
         out_shape=jax.ShapeDtypeStruct((bricks_dev, EDGE * FACE), jnp.float32),
-        in_specs=[vmem()] * (owners + 2),
+        in_specs=[vmem()] * (len(parts) + 2),
         out_specs=vmem(),
         compiler_params=params,
         name="cells",

time: 29.2 us -> 34.7 us (1.19)
  the two profiles are of different devices: /device:TPU:0 before, /device:TPU:24 now
where the time goes in v7:
time: 34.7 us; the launch traced here: 34.3 us
  starting transfers between devices  14 us (40%)
  blocking collectives  8.48 us (24%)
  Pallas kernels  7.79 us (22%)
  waiting for transfers between devices  3.9 us (11%)
    ppermute x6, starting transfers between devices, body(): lax.ppermute(piece, 'basis', pairs)  14 us
    all_to_all x1, blocking collectives, body(): lax.all_to_all(outgoing.reshape(chunks, 1, (part_rows + 1) * LANES), ('ro...  8.48 us
    pallas_call x1, Pallas kernels, body(): pl.pallas_call(functools.partial(pair_kernel, slot_depth, width, bricks_g...  6.23 us
    ppermute x6, waiting for transfers between devices, body(): lax.ppermute(piece, 'basis', pairs)  3.9 us
    pallas_call x1, Pallas kernels, body(): pl.pallas_call(functools.partial(cell_kernel, width), out_shape=jax.Shape...  1.34 us
  transfers between devices with their start and end apart: 6, of which 2 were waited for; matrix products, arithmetic and copies ran while one was open for 0% of the time, Pallas kernels for 0%

profile of v7, /device:TPU:24, one launch (start us, length us, event | category | flops | bytes accessed | tf_op | source)
XLA Modules:
  0.0 34.3 jit_solution(13272782663681479008)
XLA Ops:
  0.0 0.0 copy-start
  0.0 0.0 copy-start.1
  0.0 6.2 %pair_density.1 = f32[264,128]{1,0:T(8,128)S(1)} custom-call(s32[2,8]{1,0:T(2,128)} %bitcast.9, s32[8]{0:T(128)} %dest_hbm.1, s32[8]{0:T(128)} %tag_hbm.1, s32[64]{0:T(128)} %levels_hbm.1, bf16[8,128,128]{2,1,0:T(8,128)(2,1)} %blocks_hbm.1, f32[3,1024,128]{2,1,0:T(8,128)} %bitcast.8, f32[1024,128]{1,0:T(8,128)} %exponents_ref.1), custom_call_target="tpu_custom_call" | custom-call | tf_op jit(solution)/shard_map/pair_density/pallas_call | solution.py:321
  6.2 8.5 %all_to_all.5 = f32[8,1,4224]{2,1,0:T(1,128)S(1)} all-to-all(f32[8,1,4224]{2,1,0:T(1,128)S(1)} %bitcast.5), channel_id=1, replica_groups={{0,4,8,12,16,20,24,28},{1,5,9,13,17,21,25,29},{2,6,10,14,18,22,26,30},{..., dimensions={0} | all-to-all | bytes 270336 | tf_op jit(solution)/shard_map/all_to_all | solution.py:359
  14.7 0.2 group_sum.1
  15.0 0.7 %collective-permute-start = (f32[72,128]{1,0:T(8,128)S(1)}, f32[72,128]{1,0:T(8,128)S(1)}, u32[]{:S(2)}, u32[]{:S(2)}) collective-permute-start(f32[72,128]{1,0:T(8,128)S(1)} %get-tuple-element.13), channel_id=1, source_target_pairs={{0,1},{1,0},{4,5},{5,4},{8,9},{9,8},{12,13},{13,12},{16,17},{17,16... | collective-permute-start | bytes 110600 | tf_op jit(solution)/shard_map/ppermute | solution.py:383
  15.6 0.7 %collective-permute-start.1 = (f32[72,128]{1,0:T(8,128)S(1)}, f32[72,128]{1,0:T(8,128)S(1)}, u32[]{:S(2)}, u32[]{:S(2)}) collective-permute-start(f32[72,128]{1,0:T(8,128)S(1)} %get-tuple-element.14), channel_id=1, source_target_pairs={{0,2},{2,0},{4,6},{6,4},{8,10},{10,8},{12,14},{14,12},{16,18},{18,... | collective-permute-start | bytes 110600 | tf_op jit(solution)/shard_map/ppermute | solution.py:383
  16.3 0.7 %collective-permute-start.2 = (f32[72,128]{1,0:T(8,128)S(1)}, f32[72,128]{1,0:T(8,128)S(1)}, u32[]{:S(2)}, u32[]{:S(2)}) collective-permute-start(f32[72,128]{1,0:T(8,128)S(1)} %get-tuple-element.15), channel_id=1, source_target_pairs={{1,2},{2,1},{5,6},{6,5},{9,10},{10,9},{13,14},{14,13},{17,18},{18,... | collective-permute-start | bytes 110600 | tf_op jit(solution)/shard_map/ppermute | solution.py:383
  17.0 6.2 %collective-permute-start.3 = (f32[72,128]{1,0:T(8,128)S(1)}, f32[72,128]{1,0:T(8,128)S(1)}, u32[]{:S(2)}, u32[]{:S(2)}) collective-permute-start(f32[72,128]{1,0:T(8,128)S(1)} %get-tuple-element.16), channel_id=1, source_target_pairs={{0,3},{3,0},{4,7},{7,4},{8,11},{11,8},{12,15},{15,12},{16,19},{19,... | collective-permute-start | bytes 110600 | tf_op jit(solution)/shard_map/ppermute | solution.py:383
  23.2 3.9 %collective-permute-start.4 = (f32[72,128]{1,0:T(8,128)S(1)}, f32[72,128]{1,0:T(8,128)S(1)}, u32[]{:S(2)}, u32[]{:S(2)}) collective-permute-start(f32[72,128]{1,0:T(8,128)S(1)} %get-tuple-element.17), channel_id=1, source_target_pairs={{1,3},{3,1},{5,7},{7,5},{9,11},{11,9},{13,15},{15,13},{17,19},{19,... | collective-permute-start | bytes 110600 | tf_op jit(solution)/shard_map/ppermute | solution.py:383
  27.1 0.0 collective-permute-done.refs_1_
  27.1 1.9 %collective-permute-start.5 = (f32[72,128]{1,0:T(8,128)S(1)}, f32[72,128]{1,0:T(8,128)S(1)}, u32[]{:S(2)}, u32[]{:S(2)}) collective-permute-start(f32[72,128]{1,0:T(8,128)S(1)} %get-tuple-element.18), channel_id=1, source_target_pairs={{2,3},{3,2},{6,7},{7,6},{10,11},{11,10},{14,15},{15,14},{18,19},{1... | collective-permute-start | bytes 110600 | tf_op jit(solution)/shard_map/ppermute | solution.py:383
  29.1 0.0 collective-permute-done.1.refs_2_
  29.1 0.0 collective-permute-done.2.refs_3_
  29.1 0.0 collective-permute-done.3.refs_4_
  29.1 0.9 %collective-permute-done.4.refs_5_ = f32[72,128]{1,0:T(8,128)S(1)} collective-permute-done((f32[72,128]{1,0:T(8,128)S(1)}, f32[72,128]{1,0:T(8,128)S(1)}, u32[]{:S(2)}, u32[]{:S(2)}) %collective-permute-start.4) | collective-permute-done | bytes 36896 | tf_op jit(solution)/shard_map/ppermute | solution.py:383
  29.9 3.0 %collective-permute-done.5.refs_6_ = f32[72,128]{1,0:T(8,128)S(1)} collective-permute-done((f32[72,128]{1,0:T(8,128)S(1)}, f32[72,128]{1,0:T(8,128)S(1)}, u32[]{:S(2)}, u32[]{:S(2)}) %collective-permute-start.5) | collective-permute-done | bytes 36896 | tf_op jit(solution)/shard_map/ppermute | solution.py:383
  33.0 0.0 copy-done
  33.0 0.0 copy-done.1
  33.0 1.3 %cells.1 = f32[2,4096]{1,0:T(2,128)} custom-call(f32[72,128]{1,0:T(8,128)S(1)} %get-tuple-element.12.refs_0_, f32[72,128]{1,0:T(8,128)S(1)} %collective-permute-done.refs_1_, f32[72,128]{1,0:T(8,128)S(1)} %collective-permute-done.1.refs_2_, f32[72,128]{1,0:T(8,128)S(1)} %collective-permute-done.2.refs_3_, f32[72,128]{1,0:T(8,128)S(1)} %collective-permute-done.3.refs_4_, ...), custom_call_target="tpu_custom_call" | custom-call | tf_op jit(solution)/shard_map/cells/pallas_call | solution.py:385
Async XLA Ops:
  0.0 33.0 %copy-start = (s32[2,256,8]{1,2,0:T(8,128)S(1)}, s32[2,256,8]{1,2,0:T(8,128)}, u32[]{:S(2)}) copy-start(s32[2,256,8]{1,2,0:T(8,128)} %param.17) | copy-start | bytes 49156
  0.0 33.0 %copy-start.1 = (s32[2,256]{1,0:T(2,128)S(1)}, s32[2,256]{1,0:T(2,128)}, u32[]{:S(2)}) copy-start(s32[2,256]{1,0:T(2,128)} %refs_7_.1) | copy-start | bytes 6148
  15.0 12.2 %collective-permute-start = (f32[72,128]{1,0:T(8,128)S(1)}, f32[72,128]{1,0:T(8,128)S(1)}, u32[]{:S(2)}, u32[]{:S(2)}) collective-permute-start(f32[72,128]{1,0:T(8,128)S(1)} %get-tuple-element.13), channel_id=1, source_target_pairs={{0,1},{1,0},{4,5},{5,4},{8,9},{9,8},{12,13},{13,12},{16,17},{17,16... | collective-permute-start | bytes 110600 | tf_op jit(solution)/shard_map/ppermute | solution.py:383
  15.6 13.4 %collective-permute-start.1 = (f32[72,128]{1,0:T(8,128)S(1)}, f32[72,128]{1,0:T(8,128)S(1)}, u32[]{:S(2)}, u32[]{:S(2)}) collective-permute-start(f32[72,128]{1,0:T(8,128)S(1)} %get-tuple-element.14), channel_id=1, source_target_pairs={{0,2},{2,0},{4,6},{6,4},{8,10},{10,8},{12,14},{14,12},{16,18},{18,... | collective-permute-start | bytes 110600 | tf_op jit(solution)/shard_map/ppermute | solution.py:383
  16.3 12.8 %collective-permute-start.2 = (f32[72,128]{1,0:T(8,128)S(1)}, f32[72,128]{1,0:T(8,128)S(1)}, u32[]{:S(2)}, u32[]{:S(2)}) collective-permute-start(f32[72,128]{1,0:T(8,128)S(1)} %get-tuple-element.15), channel_id=1, source_target_pairs={{1,2},{2,1},{5,6},{6,5},{9,10},{10,9},{13,14},{14,13},{17,18},{18,... | collective-permute-start | bytes 110600 | tf_op jit(solution)/shard_map/ppermute | solution.py:383
  17.0 12.1 %collective-permute-start.3 = (f32[72,128]{1,0:T(8,128)S(1)}, f32[72,128]{1,0:T(8,128)S(1)}, u32[]{:S(2)}, u32[]{:S(2)}) collective-permute-start(f32[72,128]{1,0:T(8,128)S(1)} %get-tuple-element.16), channel_id=1, source_target_pairs={{0,3},{3,0},{4,7},{7,4},{8,11},{11,8},{12,15},{15,12},{16,19},{19,... | collective-permute-start | bytes 110600 | tf_op jit(solution)/shard_map/ppermute | solution.py:383
  23.2 6.8 %collective-permute-start.4 = (f32[72,128]{1,0:T(8,128)S(1)}, f32[72,128]{1,0:T(8,128)S(1)}, u32[]{:S(2)}, u32[]{:S(2)}) collective-permute-start(f32[72,128]{1,0:T(8,128)S(1)} %get-tuple-element.17), channel_id=1, source_target_pairs={{1,3},{3,1},{5,7},{7,5},{9,11},{11,9},{13,15},{15,13},{17,19},{19,... | collective-permute-start | bytes 110600 | tf_op jit(solution)/shard_map/ppermute | solution.py:383
  27.1 5.9 %collective-permute-start.5 = (f32[72,128]{1,0:T(8,128)S(1)}, f32[72,128]{1,0:T(8,128)S(1)}, u32[]{:S(2)}, u32[]{:S(2)}) collective-permute-start(f32[72,128]{1,0:T(8,128)S(1)} %get-tuple-element.18), channel_id=1, source_target_pairs={{2,3},{3,2},{6,7},{7,6},{10,11},{11,10},{14,15},{15,14},{18,19},{1... | collective-permute-start | bytes 110600 | tf_op jit(solution)/shard_map/ppermute | solution.py:383

commit v8 on v7

--- a/solution.py
+++ b/solution.py
@@ -10,6 +10,7 @@
 EDGE = 16
 FACE = EDGE * EDGE
 LANES = 128
+SHIFT = 7
 ROWS = EDGE * FACE // LANES
 COARSE = 0.2
 TILE = 8
@@ -141,8 +142,12 @@
                 if x in (0, EDGE - 1):
                     corner_buf[2 * (x // (EDGE - 1)) + half, pl.ds(k, 1), :] = piece
 
-    for k in range(items):
-        one(k)
+    unroll = 4 if items % 4 == 0 else 1
+
+    @pl.loop(0, items // unroll)
+    def _(step):
+        for n in range(unroll):
+            one(step * unroll + n)
 
     shape = (items, LANES)
     lane = iota(shape, 1)
@@ -206,28 +211,44 @@
     for first in range(0, chunks, TILE):
         block = jnp.concatenate(meta[first : first + TILE], axis=0)
         for k in range(items):
-            values = lane_pick(block, 8 * k + lane % 8)
+            values = lane_pick(block, 8 * k + (lane & 7))
             brick = lane_pick(block, jnp.full(shape, 8 * items + k, jnp.int32)).astype(jnp.int32)
-            values = jnp.where(brick % 16 == lane // 8, values, 0.0)
+            values = jnp.where((brick & 15) == lane >> 3, values, 0.0)
             for r in range(table_rows):
-                lines[r] = lines[r] + jnp.where(brick // 16 == r, values, 0.0)
+                lines[r] = lines[r] + jnp.where(brick >> 4 == r, values, 0.0)
     table = jnp.concatenate([jnp.sum(line, axis=0, keepdims=True) for line in lines], axis=0)
     for out, shift in zip(outs, shifts):
         if shift % width == 0:
             out[bricks_dev * part_rows :, :] = table
 
 
-def cell_kernel(width, *refs):
-    *ins, cells_ref, refs_ref, out_ref = refs
+def map_kernel(cells_ref, out_ref):
     bricks_dev, cells = cells_ref.shape
+    cell = (iota((LANES, cells), 1) + 1).astype(jnp.float32)
+    for b in range(bricks_dev):
+        position = cells_ref[b : b + 1, :]
+        high = position >> SHIFT == iota((ROWS, cells), 0)
+        low = (position & (LANES - 1)) == iota((LANES, cells), 0)
+        found = lax.dot_general(
+            high.astype(jnp.float32).astype(jnp.bfloat16),
+            jnp.where(low, cell, 0.0).astype(jnp.bfloat16),
+            (((1,), (1,)), ((), ())),
+            preferred_element_type=jnp.float32,
+        )
+        out_ref[b] = found.astype(jnp.int32) - 1
+
+
+def cell_kernel(width, shifts, *refs):
+    *ins, map_ref, refs_ref, out_ref = refs
+    bricks_dev, _, cells = refs_ref.shape
     part_rows = ROWS // width
-    table_rows = ins[0].shape[0] - bricks_dev * part_rows
     mine = lax.axis_index("basis") % width
 
     totals = []
     for offset in range(width):
-        total = ins[offset][...]
-        for part in ins[offset + width :: width]:
+        parts = [part for part, shift in zip(ins, shifts) if shift % width == offset]
+        total = parts[0][...]
+        for part in parts[1:]:
             total = total + part[...]
         totals.append(total)
     table = totals[0][bricks_dev * part_rows :]
@@ -240,39 +261,28 @@
         crossed = jnp.concatenate(halves[::-1], axis=0)
         return jnp.where(mine == 0, straight, crossed)
 
-    chunk = (8, LANES)
+    chunk = (TILE, LANES)
+    tiles = cells // LANES
     refs = [
-        [refs_ref[b, :, c * LANES : (c + 1) * LANES] for c in range(cells // LANES)]
+        [refs_ref[b, :, c * LANES : (c + 1) * LANES] for c in range(tiles)]
         for b in range(bricks_dev)
     ]
     picked = [[jnp.zeros(chunk, jnp.float32) for _ in row] for row in refs]
-    for r in range(table_rows):
+    for r in range(table.shape[0]):
         line = jnp.broadcast_to(table[r : r + 1, :], chunk)
         for b in range(bricks_dev):
             for c, index in enumerate(refs[b]):
-                found = lane_pick(line, index % LANES)
-                picked[b][c] = jnp.where(index // LANES == r, found, picked[b][c])
+                found = lane_pick(line, (index & (LANES - 1)))
+                picked[b][c] = jnp.where(index >> SHIFT == r, found, picked[b][c])
     for b in range(bricks_dev):
-        mean = jnp.concatenate(
-            [jnp.sum(p, axis=0, keepdims=True) for p in picked[b]], axis=1
-        ) * (0.5 / 8.0)
-        position = cells_ref[b : b + 1, :]
-        high = (position // LANES == iota((ROWS, cells), 0)).astype(jnp.float32)
-        here = position % LANES == iota((LANES, cells), 0)
-
-        def spread(values):
-            return lax.dot_general(
-                high,
-                values,
-                (((1,), (1,)), ((), ())),
-                precision=lax.Precision.HIGHEST,
-                preferred_element_type=jnp.float32,
-            )
-
-        hit = spread(here.astype(jnp.float32))
-        new = spread(jnp.where(here, mean, 0.0))
+        cell = map_ref[b]
+        mean = jnp.zeros((ROWS, LANES), jnp.float32)
+        for c in range(tiles):
+            line = jnp.sum(picked[b][c], axis=0, keepdims=True) * (0.5 / 8.0)
+            found = lane_pick(jnp.broadcast_to(line, (ROWS, LANES)), (cell & (LANES - 1)))
+            mean = jnp.where(cell >> SHIFT == c, found, mean)
         own = own_points(b)
-        result = jnp.where(hit > 0.5, 0.5 * own + new, own)
+        result = jnp.where(cell >= 0, 0.5 * own + mean, own)
         for row in range(ROWS):
             out_ref[b : b + 1, row * LANES : (row + 1) * LANES] = result[row : row + 1, :]
 
@@ -286,13 +296,9 @@
 
 
 def exchanges(owners, width):
-    if width > 1 or owners & (owners - 1) or owners > 8:
-        return [
-            (d, [(i, owner_of(i, d, owners, width)) for i in range(owners)])
-            for d in range(1, owners)
-        ]
     return [
-        (low ^ high, [(low, high), (high, low)]) for high in range(1, owners) for low in range(high)
+        (d, [(i, owner_of(i, d, owners, width)) for i in range(owners)])
+        for d in range(owners - 1, 0, -1)
     ]
 
 
@@ -382,14 +388,23 @@
     parts = [partial[0]] + [
         lax.ppermute(piece, "basis", pairs) for piece, (_, pairs) in zip(partial[1:], moves)
     ]
+    cell_map = pl.pallas_call(
+        map_kernel,
+        out_shape=jax.ShapeDtypeStruct((bricks_dev, ROWS, LANES), jnp.int32),
+        in_specs=[vmem()],
+        out_specs=vmem(),
+        compiler_params=params,
+        cost_estimate=pl.CostEstimate(flops=4_000_000, bytes_accessed=200_000, transcendentals=0),
+        name="cell_map",
+    )(cell_pos)
     return pl.pallas_call(
-        functools.partial(cell_kernel, width),
+        functools.partial(cell_kernel, width, shifts),
         out_shape=jax.ShapeDtypeStruct((bricks_dev, EDGE * FACE), jnp.float32),
         in_specs=[vmem()] * (len(parts) + 2),
         out_specs=vmem(),
         compiler_params=params,
         name="cells",
-    )(*parts, cell_pos, jnp.transpose(corner_refs, (0, 2, 1)))
+    )(*parts, cell_map, jnp.transpose(corner_refs, (0, 2, 1)))
 
 
 def solution(mesh):

time: 34.7 us -> 26.2 us (0.76)
  the two profiles are of different devices: /device:TPU:24 before, /device:TPU:0 now
where the time goes in v8:
time: 26.2 us; the launch traced here: 26 us
  blocking collectives  9.93 us (38%)
  Pallas kernels  7.63 us (29%)
  starting transfers between devices  4.45 us (17%)
  waiting for transfers between devices  3.92 us (15%)
    all_to_all x1, blocking collectives, body(): lax.all_to_all(outgoing.reshape(chunks, 1, (part_rows + 1) * LANES), ('ro...  9.93 us
    pallas_call x1, Pallas kernels, body(): pl.pallas_call(functools.partial(pair_kernel, slot_depth, width, bricks_g...  6.4 us
    ppermute x3, starting transfers between devices, body(): lax.ppermute(piece, 'basis', pairs)  4.45 us
    ppermute x3, waiting for transfers between devices, body(): lax.ppermute(piece, 'basis', pairs)  3.92 us
    pallas_call x1, Pallas kernels, body(): pl.pallas_call(functools.partial(cell_kernel, width, shifts), out_shape=j...  0.88 us
  transfers between devices with their start and end apart: 3, of which 2 were waited for; matrix products, arithmetic and copies ran while one was open for 0% of the time, Pallas kernels for 1%

profile of v8, /device:TPU:0, one launch (start us, length us, event | category | flops | bytes accessed | tf_op | source)
XLA Modules:
  0.0 26.0 jit_solution(3910690015029780243)
XLA Ops:
  0.0 0.0 copy-start.1
  0.0 0.0 copy-start
  0.0 6.4 %pair_density.1 = f32[264,128]{1,0:T(8,128)S(1)} custom-call(s32[2,8]{1,0:T(2,128)} %bitcast.9, s32[8]{0:T(128)} %dest_hbm.1, s32[8]{0:T(128)} %tag_hbm.1, s32[64]{0:T(128)} %levels_hbm.1, bf16[8,128,128]{2,1,0:T(8,128)(2,1)} %blocks_hbm.1, f32[3,1024,128]{2,1,0:T(8,128)} %bitcast.8, f32[1024,128]{1,0:T(8,128)} %exponents_ref.1), custom_call_target="tpu_custom_call" | custom-call | tf_op jit(solution)/shard_map/pair_density/pallas_call | solution.py:327
  6.4 9.9 %all_to_all.5 = f32[8,1,4224]{2,1,0:T(1,128)S(1)} all-to-all(f32[8,1,4224]{2,1,0:T(1,128)S(1)} %bitcast.5), channel_id=1, replica_groups={{0,4,8,12,16,20,24,28},{1,5,9,13,17,21,25,29},{2,6,10,14,18,22,26,30},{..., dimensions={0} | all-to-all | bytes 270336 | tf_op jit(solution)/shard_map/all_to_all | solution.py:365
  16.3 0.2 group_sum.1
  16.5 3.7 %collective-permute-start = (f32[72,128]{1,0:T(8,128)S(1)}, f32[72,128]{1,0:T(8,128)S(1)}, u32[]{:S(2)}, u32[]{:S(2)}) collective-permute-start(f32[72,128]{1,0:T(8,128)S(1)} %get-tuple-element.10), channel_id=1, source_target_pairs={{0,3},{1,2},{2,1},{3,0},{4,7},{5,6},{6,5},{7,4},{8,11},{9,10},{10,... | collective-permute-start | bytes 110600 | tf_op jit(solution)/shard_map/ppermute | solution.py:389
  20.2 0.0 collective-permute-start.1
  20.2 0.8 %collective-permute-start.2 = (f32[72,128]{1,0:T(8,128)S(1)}, f32[72,128]{1,0:T(8,128)S(1)}, u32[]{:S(2)}, u32[]{:S(2)}) collective-permute-start(f32[72,128]{1,0:T(8,128)S(1)} %get-tuple-element.12), channel_id=1, source_target_pairs={{0,1},{1,0},{2,3},{3,2},{4,5},{5,4},{6,7},{7,6},{8,9},{9,8},{10,11... | collective-permute-start | bytes 110600 | tf_op jit(solution)/shard_map/ppermute | solution.py:389
  21.0 0.0 copy-done.1
  21.0 0.1 cell_map.1.refs_4_
  21.2 1.2 %collective-permute-done.refs_1_ = f32[72,128]{1,0:T(8,128)S(1)} collective-permute-done((f32[72,128]{1,0:T(8,128)S(1)}, f32[72,128]{1,0:T(8,128)S(1)}, u32[]{:S(2)}, u32[]{:S(2)}) %collective-permute-start) | collective-permute-done | bytes 36896 | tf_op jit(solution)/shard_map/ppermute | solution.py:389
  22.4 2.7 %collective-permute-done.1.refs_2_ = f32[72,128]{1,0:T(8,128)S(1)} collective-permute-done((f32[72,128]{1,0:T(8,128)S(1)}, f32[72,128]{1,0:T(8,128)S(1)}, u32[]{:S(2)}, u32[]{:S(2)}) %collective-permute-start.1) | collective-permute-done | bytes 36896 | tf_op jit(solution)/shard_map/ppermute | solution.py:389
  25.1 0.0 collective-permute-done.2.refs_3_
  25.1 0.0 copy-done
  25.1 0.9 %cells.1 = f32[2,4096]{1,0:T(2,128)} custom-call(f32[72,128]{1,0:T(8,128)S(1)} %get-tuple-element.9.refs_0_, f32[72,128]{1,0:T(8,128)S(1)} %collective-permute-done.refs_1_, f32[72,128]{1,0:T(8,128)S(1)} %collective-permute-done.1.refs_2_, f32[72,128]{1,0:T(8,128)S(1)} %collective-permute-done.2.refs_3_, s32[2,32,128]{2,1,0:T(8,128)S(1)} %cell_map.1.refs_4_, ...), custom_call_target="tpu_custom_call" | custom-call | tf_op jit(solution)/shard_map/cells/pallas_call | solution.py:400
Async XLA Ops:
  0.0 21.0 %copy-start.1 = (s32[2,256]{1,0:T(2,128)S(1)}, s32[2,256]{1,0:T(2,128)}, u32[]{:S(2)}) copy-start(s32[2,256]{1,0:T(2,128)} %cells_ref.1) | copy-start | bytes 6148
  0.0 25.1 %copy-start = (s32[2,256,8]{1,2,0:T(8,128)S(1)}, s32[2,256,8]{1,2,0:T(8,128)}, u32[]{:S(2)}) copy-start(s32[2,256,8]{1,2,0:T(8,128)} %param.17) | copy-start | bytes 49156
  16.5 5.8 %collective-permute-start = (f32[72,128]{1,0:T(8,128)S(1)}, f32[72,128]{1,0:T(8,128)S(1)}, u32[]{:S(2)}, u32[]{:S(2)}) collective-permute-start(f32[72,128]{1,0:T(8,128)S(1)} %get-tuple-element.10), channel_id=1, source_target_pairs={{0,3},{1,2},{2,1},{3,0},{4,7},{5,6},{6,5},{7,4},{8,11},{9,10},{10,... | collective-permute-start | bytes 110600 | tf_op jit(solution)/shard_map/ppermute | solution.py:389
  20.2 4.9 %collective-permute-start.1 = (f32[72,128]{1,0:T(8,128)S(1)}, f32[72,128]{1,0:T(8,128)S(1)}, u32[]{:S(2)}, u32[]{:S(2)}) collective-permute-start(f32[72,128]{1,0:T(8,128)S(1)} %get-tuple-element.11), channel_id=1, source_target_pairs={{0,2},{1,3},{2,0},{3,1},{4,6},{5,7},{6,4},{7,5},{8,10},{9,11},{10,... | collective-permute-start | bytes 110600 | tf_op jit(solution)/shard_map/ppermute | solution.py:389
  20.2 4.9 %collective-permute-start.2 = (f32[72,128]{1,0:T(8,128)S(1)}, f32[72,128]{1,0:T(8,128)S(1)}, u32[]{:S(2)}, u32[]{:S(2)}) collective-permute-start(f32[72,128]{1,0:T(8,128)S(1)} %get-tuple-element.12), channel_id=1, source_target_pairs={{0,1},{1,0},{2,3},{3,2},{4,5},{5,4},{6,7},{7,6},{8,9},{9,8},{10,11... | collective-permute-start | bytes 110600 | tf_op jit(solution)/shard_map/ppermute | solution.py:389

commit v9 on v8

--- a/solution.py
+++ b/solution.py
@@ -217,9 +217,8 @@
             for r in range(table_rows):
                 lines[r] = lines[r] + jnp.where(brick >> 4 == r, values, 0.0)
     table = jnp.concatenate([jnp.sum(line, axis=0, keepdims=True) for line in lines], axis=0)
-    for out, shift in zip(outs, shifts):
-        if shift % width == 0:
-            out[bricks_dev * part_rows :, :] = table
+    for out in outs:
+        out[bricks_dev * part_rows :, :] = table
 
 
 def map_kernel(cells_ref, out_ref):
@@ -319,7 +318,7 @@
     bricks_dev = bricks_group // owners
     table_rows = -(-bricks * 8 // (8 * LANES)) * 8
     basis = block_data.shape[1]
-    width = 1
+    width = 2 if owners % 2 == 0 else 1
     part_rows = ROWS // width
     chunks = slots * width
     params = pltpu.CompilerParams(vmem_limit_bytes=32 * 1024 * 1024)
@@ -375,10 +374,8 @@
     partial = pl.pallas_call(
         functools.partial(group_kernel, items, bricks_dev, width, owners, shifts),
         out_shape=[
-            jax.ShapeDtypeStruct(
-                (bricks_dev * part_rows + (0 if d % width else table_rows), LANES), jnp.float32
-            )
-            for d in shifts
+            jax.ShapeDtypeStruct((bricks_dev * part_rows + table_rows, LANES), jnp.float32)
+            for _ in shifts
         ],
         in_specs=[vmem()],
         out_specs=[vmem()] * len(shifts),

time: 26.2 us -> 27.4 us (1.046)
  blocking collectives: 9.93 us -> 12 us
  waiting for transfers between devices: 3.92 us -> 2.98 us
    all_to_all x1, blocking collectives: 9.93 us -> 12 us  [body(): lax.all_to_all(outgoing.reshape(chunks, 1, (part_rows + 1) * LANES), ('ro...]
    ppermute x3, waiting for transfers between devices: 3.92 us -> 2.98 us  [body(): lax.ppermute(piece, 'basis', pairs)]
where the time goes in v9:
time: 27.4 us; the launch traced here: 27.2 us
  blocking collectives  12 us (44%)
  Pallas kernels  7.68 us (28%)
  starting transfers between devices  4.45 us (16%)
  waiting for transfers between devices  2.98 us (11%)
    all_to_all x1, blocking collectives, body(): lax.all_to_all(outgoing.reshape(chunks, 1, (part_rows + 1) * LANES), ('ro...  12 us
    pallas_call x1, Pallas kernels, body(): pl.pallas_call(functools.partial(pair_kernel, slot_depth, width, bricks_g...  6.4 us
    ppermute x3, starting transfers between devices, body(): lax.ppermute(piece, 'basis', pairs)  4.45 us
    ppermute x3, waiting for transfers between devices, body(): lax.ppermute(piece, 'basis', pairs)  2.98 us
    pallas_call x1, Pallas kernels, body(): pl.pallas_call(functools.partial(cell_kernel, width, shifts), out_shape=j...  0.88 us
  transfers between devices with their start and end apart: 3, of which 2 were waited for; matrix products, arithmetic and copies ran while one was open for 0% of the time, Pallas kernels for 1%

profile of v9, /device:TPU:0, one launch (start us, length us, event | category | flops | bytes accessed | tf_op | source)
XLA Modules:
  0.0 27.2 jit_solution(11578283213795138315)
XLA Ops:
  0.0 0.0 copy-start.1
  0.0 0.0 copy-start
  0.0 6.4 %pair_density.1 = f32[272,128]{1,0:T(8,128)S(1)} custom-call(s32[2,8]{1,0:T(2,128)} %bitcast.9, s32[8]{0:T(128)} %dest_hbm.1, s32[8]{0:T(128)} %tag_hbm.1, s32[64]{0:T(128)} %levels_hbm.1, bf16[8,128,128]{2,1,0:T(8,128)(2,1)} %blocks_hbm.1, f32[3,1024,128]{2,1,0:T(8,128)} %bitcast.8, f32[1024,128]{1,0:T(8,128)} %exponents_ref.1), custom_call_target="tpu_custom_call" | custom-call | tf_op jit(solution)/shard_map/pair_density/pallas_call | solution.py:326
  6.4 12.0 %all_to_all.5 = f32[16,1,2176]{2,1,0:T(1,128)S(1)} all-to-all(f32[16,1,2176]{2,1,0:T(1,128)S(1)} %bitcast.5), channel_id=1, replica_groups={{0,1,4,5,8,9,12,13,16,17,20,21,24,25,28,29},{2,3,6,7,10,11,14,15,18,19,..., dimensions={0} | all-to-all | bytes 278528 | tf_op jit(solution)/shard_map/all_to_all | solution.py:364
  18.5 0.3 group_sum.1
  18.7 2.8 %collective-permute-start = (f32[40,128]{1,0:T(8,128)S(1)}, f32[40,128]{1,0:T(8,128)S(1)}, u32[]{:S(2)}, u32[]{:S(2)}) collective-permute-start(f32[40,128]{1,0:T(8,128)S(1)} %get-tuple-element.10), channel_id=1, source_target_pairs={{0,3},{1,2},{2,1},{3,0},{4,7},{5,6},{6,5},{7,4},{8,11},{9,10},{10,... | collective-permute-start | bytes 61448 | tf_op jit(solution)/shard_map/ppermute | solution.py:386
  21.6 0.0 collective-permute-start.1
  21.6 1.6 %collective-permute-start.2 = (f32[40,128]{1,0:T(8,128)S(1)}, f32[40,128]{1,0:T(8,128)S(1)}, u32[]{:S(2)}, u32[]{:S(2)}) collective-permute-start(f32[40,128]{1,0:T(8,128)S(1)} %get-tuple-element.12), channel_id=1, source_target_pairs={{0,1},{1,0},{2,3},{3,2},{4,5},{5,4},{6,7},{7,6},{8,9},{9,8},{10,11... | collective-permute-start | bytes 61448 | tf_op jit(solution)/shard_map/ppermute | solution.py:386
  23.2 0.0 copy-done.1
  23.2 0.1 cell_map.1.refs_4_
  23.3 1.0 %collective-permute-done.refs_1_ = f32[40,128]{1,0:T(8,128)S(1)} collective-permute-done((f32[40,128]{1,0:T(8,128)S(1)}, f32[40,128]{1,0:T(8,128)S(1)}, u32[]{:S(2)}, u32[]{:S(2)}) %collective-permute-start) | collective-permute-done | bytes 20512 | tf_op jit(solution)/shard_map/ppermute | solution.py:386
  24.4 1.9 %collective-permute-done.1.refs_2_ = f32[40,128]{1,0:T(8,128)S(1)} collective-permute-done((f32[40,128]{1,0:T(8,128)S(1)}, f32[40,128]{1,0:T(8,128)S(1)}, u32[]{:S(2)}, u32[]{:S(2)}) %collective-permute-start.1) | collective-permute-done | bytes 20512 | tf_op jit(solution)/shard_map/ppermute | solution.py:386
  26.3 0.0 collective-permute-done.2.refs_3_
  26.3 0.0 copy-done
  26.3 0.9 %cells.1 = f32[2,4096]{1,0:T(2,128)} custom-call(f32[40,128]{1,0:T(8,128)S(1)} %get-tuple-element.9.refs_0_, f32[40,128]{1,0:T(8,128)S(1)} %collective-permute-done.refs_1_, f32[40,128]{1,0:T(8,128)S(1)} %collective-permute-done.1.refs_2_, f32[40,128]{1,0:T(8,128)S(1)} %collective-permute-done.2.refs_3_, s32[2,32,128]{2,1,0:T(8,128)S(1)} %cell_map.1.refs_4_, ...), custom_call_target="tpu_custom_call" | custom-call | tf_op jit(solution)/shard_map/cells/pallas_call | solution.py:397
Async XLA Ops:
  0.0 23.2 %copy-start.1 = (s32[2,256]{1,0:T(2,128)S(1)}, s32[2,256]{1,0:T(2,128)}, u32[]{:S(2)}) copy-start(s32[2,256]{1,0:T(2,128)} %cells_ref.1) | copy-start | bytes 6148
  0.0 26.3 %copy-start = (s32[2,256,8]{1,2,0:T(8,128)S(1)}, s32[2,256,8]{1,2,0:T(8,128)}, u32[]{:S(2)}) copy-start(s32[2,256,8]{1,2,0:T(8,128)} %param.17) | copy-start | bytes 49156
  18.7 5.6 %collective-permute-start = (f32[40,128]{1,0:T(8,128)S(1)}, f32[40,128]{1,0:T(8,128)S(1)}, u32[]{:S(2)}, u32[]{:S(2)}) collective-permute-start(f32[40,128]{1,0:T(8,128)S(1)} %get-tuple-element.10), channel_id=1, source_target_pairs={{0,3},{1,2},{2,1},{3,0},{4,7},{5,6},{6,5},{7,4},{8,11},{9,10},{10,... | collective-permute-start | bytes 61448 | tf_op jit(solution)/shard_map/ppermute | solution.py:386
  21.6 4.7 %collective-permute-start.1 = (f32[40,128]{1,0:T(8,128)S(1)}, f32[40,128]{1,0:T(8,128)S(1)}, u32[]{:S(2)}, u32[]{:S(2)}) collective-permute-start(f32[40,128]{1,0:T(8,128)S(1)} %get-tuple-element.11), channel_id=1, source_target_pairs={{0,2},{1,3},{2,0},{3,1},{4,6},{5,7},{6,4},{7,5},{8,10},{9,11},{10,... | collective-permute-start | bytes 61448 | tf_op jit(solution)/shard_map/ppermute | solution.py:386
  21.6 4.7 %collective-permute-start.2 = (f32[40,128]{1,0:T(8,128)S(1)}, f32[40,128]{1,0:T(8,128)S(1)}, u32[]{:S(2)}, u32[]{:S(2)}) collective-permute-start(f32[40,128]{1,0:T(8,128)S(1)} %get-tuple-element.12), channel_id=1, source_target_pairs={{0,1},{1,0},{2,3},{3,2},{4,5},{5,4},{6,7},{7,6},{8,9},{9,8},{10,11... | collective-permute-start | bytes 61448 | tf_op jit(solution)/shard_map/ppermute | solution.py:386

commit v10 on v8

--- a/solution.py
+++ b/solution.py
@@ -134,7 +134,11 @@
             product = lax.dot_general(
                 block, col, (((1,), (1,)), ((), ())), preferred_element_type=jnp.float32
             )
-            dens = jnp.sum(row_x[:, x : x + 1] * row_face * product, axis=0, keepdims=True)
+            total = jnp.zeros((TILE, FACE), jnp.float32)
+            for first in range(0, block.shape[0], TILE):
+                rows = slice(first, first + TILE)
+                total = total + row_x[rows, x : x + 1] * row_face[rows] * product[rows]
+            dens = jnp.sum(total, axis=0, keepdims=True)
             for half in range(FACE // LANES):
                 piece = dens[:, half * LANES : (half + 1) * LANES]
                 part, row = divmod(2 * x + half, part_rows)

time: 26.2 us -> 26.3 us (level)
  no operation moved by 1% of the time
where the time goes in v10:
time: 26.3 us; the launch traced here: 26 us
  blocking collectives  9.91 us (38%)
  Pallas kernels  7.71 us (29%)
  starting transfers between devices  4.45 us (17%)
  waiting for transfers between devices  3.92 us (15%)
    all_to_all x1, blocking collectives, body(): lax.all_to_all(outgoing.reshape(chunks, 1, (part_rows + 1) * LANES), ('ro...  9.91 us
    pallas_call x1, Pallas kernels, body(): pl.pallas_call(functools.partial(pair_kernel, slot_depth, width, bricks_g...  6.48 us
    ppermute x3, starting transfers between devices, body(): lax.ppermute(piece, 'basis', pairs)  4.45 us
    ppermute x3, waiting for transfers between devices, body(): lax.ppermute(piece, 'basis', pairs)  3.92 us
    pallas_call x1, Pallas kernels, body(): pl.pallas_call(functools.partial(cell_kernel, width, shifts), out_shape=j...  0.88 us
  transfers between devices with their start and end apart: 3, of which 2 were waited for; matrix products, arithmetic and copies ran while one was open for 0% of the time, Pallas kernels for 1%

profile of v10, /device:TPU:0, one launch (start us, length us, event | category | flops | bytes accessed | tf_op | source)
XLA Modules:
  0.0 26.0 jit_solution(14468796927334597523)
XLA Ops:
  0.0 0.0 copy-start.1
  0.0 0.0 copy-start
  0.0 6.5 %pair_density.1 = f32[264,128]{1,0:T(8,128)S(1)} custom-call(s32[2,8]{1,0:T(2,128)} %bitcast.9, s32[8]{0:T(128)} %dest_hbm.1, s32[8]{0:T(128)} %tag_hbm.1, s32[64]{0:T(128)} %levels_hbm.1, bf16[8,128,128]{2,1,0:T(8,128)(2,1)} %blocks_hbm.1, f32[3,1024,128]{2,1,0:T(8,128)} %bitcast.8, f32[1024,128]{1,0:T(8,128)} %exponents_ref.1), custom_call_target="tpu_custom_call" | custom-call | tf_op jit(solution)/shard_map/pair_density/pallas_call | solution.py:331
  6.5 9.9 %all_to_all.5 = f32[8,1,4224]{2,1,0:T(1,128)S(1)} all-to-all(f32[8,1,4224]{2,1,0:T(1,128)S(1)} %bitcast.5), channel_id=1, replica_groups={{0,4,8,12,16,20,24,28},{1,5,9,13,17,21,25,29},{2,6,10,14,18,22,26,30},{..., dimensions={0} | all-to-all | bytes 270336 | tf_op jit(solution)/shard_map/all_to_all | solution.py:369
  16.4 0.2 group_sum.1
  16.6 3.7 %collective-permute-start = (f32[72,128]{1,0:T(8,128)S(1)}, f32[72,128]{1,0:T(8,128)S(1)}, u32[]{:S(2)}, u32[]{:S(2)}) collective-permute-start(f32[72,128]{1,0:T(8,128)S(1)} %get-tuple-element.10), channel_id=1, source_target_pairs={{0,3},{1,2},{2,1},{3,0},{4,7},{5,6},{6,5},{7,4},{8,11},{9,10},{10,... | collective-permute-start | bytes 110600 | tf_op jit(solution)/shard_map/ppermute | solution.py:393
  20.3 0.0 collective-permute-start.1
  20.3 0.8 %collective-permute-start.2 = (f32[72,128]{1,0:T(8,128)S(1)}, f32[72,128]{1,0:T(8,128)S(1)}, u32[]{:S(2)}, u32[]{:S(2)}) collective-permute-start(f32[72,128]{1,0:T(8,128)S(1)} %get-tuple-element.12), channel_id=1, source_target_pairs={{0,1},{1,0},{2,3},{3,2},{4,5},{5,4},{6,7},{7,6},{8,9},{9,8},{10,11... | collective-permute-start | bytes 110600 | tf_op jit(solution)/shard_map/ppermute | solution.py:393
  21.1 0.0 copy-done.1
  21.1 0.1 cell_map.1.refs_4_
  21.2 1.2 %collective-permute-done.refs_1_ = f32[72,128]{1,0:T(8,128)S(1)} collective-permute-done((f32[72,128]{1,0:T(8,128)S(1)}, f32[72,128]{1,0:T(8,128)S(1)}, u32[]{:S(2)}, u32[]{:S(2)}) %collective-permute-start) | collective-permute-done | bytes 36896 | tf_op jit(solution)/shard_map/ppermute | solution.py:393
  22.4 2.7 %collective-permute-done.1.refs_2_ = f32[72,128]{1,0:T(8,128)S(1)} collective-permute-done((f32[72,128]{1,0:T(8,128)S(1)}, f32[72,128]{1,0:T(8,128)S(1)}, u32[]{:S(2)}, u32[]{:S(2)}) %collective-permute-start.1) | collective-permute-done | bytes 36896 | tf_op jit(solution)/shard_map/ppermute | solution.py:393
  25.1 0.0 collective-permute-done.2.refs_3_
  25.1 0.0 copy-done
  25.1 0.9 %cells.1 = f32[2,4096]{1,0:T(2,128)} custom-call(f32[72,128]{1,0:T(8,128)S(1)} %get-tuple-element.9.refs_0_, f32[72,128]{1,0:T(8,128)S(1)} %collective-permute-done.refs_1_, f32[72,128]{1,0:T(8,128)S(1)} %collective-permute-done.1.refs_2_, f32[72,128]{1,0:T(8,128)S(1)} %collective-permute-done.2.refs_3_, s32[2,32,128]{2,1,0:T(8,128)S(1)} %cell_map.1.refs_4_, ...), custom_call_target="tpu_custom_call" | custom-call | tf_op jit(solution)/shard_map/cells/pallas_call | solution.py:404
Async XLA Ops:
  0.0 21.1 %copy-start.1 = (s32[2,256]{1,0:T(2,128)S(1)}, s32[2,256]{1,0:T(2,128)}, u32[]{:S(2)}) copy-start(s32[2,256]{1,0:T(2,128)} %cells_ref.1) | copy-start | bytes 6148
  0.0 25.1 %copy-start = (s32[2,256,8]{1,2,0:T(8,128)S(1)}, s32[2,256,8]{1,2,0:T(8,128)}, u32[]{:S(2)}) copy-start(s32[2,256,8]{1,2,0:T(8,128)} %param.17) | copy-start | bytes 49156
  16.6 5.8 %collective-permute-start = (f32[72,128]{1,0:T(8,128)S(1)}, f32[72,128]{1,0:T(8,128)S(1)}, u32[]{:S(2)}, u32[]{:S(2)}) collective-permute-start(f32[72,128]{1,0:T(8,128)S(1)} %get-tuple-element.10), channel_id=1, source_target_pairs={{0,3},{1,2},{2,1},{3,0},{4,7},{5,6},{6,5},{7,4},{8,11},{9,10},{10,... | collective-permute-start | bytes 110600 | tf_op jit(solution)/shard_map/ppermute | solution.py:393
  20.3 4.9 %collective-permute-start.1 = (f32[72,128]{1,0:T(8,128)S(1)}, f32[72,128]{1,0:T(8,128)S(1)}, u32[]{:S(2)}, u32[]{:S(2)}) collective-permute-start(f32[72,128]{1,0:T(8,128)S(1)} %get-tuple-element.11), channel_id=1, source_target_pairs={{0,2},{1,3},{2,0},{3,1},{4,6},{5,7},{6,4},{7,5},{8,10},{9,11},{10,... | collective-permute-start | bytes 110600 | tf_op jit(solution)/shard_map/ppermute | solution.py:393
  20.3 4.9 %collective-permute-start.2 = (f32[72,128]{1,0:T(8,128)S(1)}, f32[72,128]{1,0:T(8,128)S(1)}, u32[]{:S(2)}, u32[]{:S(2)}) collective-permute-start(f32[72,128]{1,0:T(8,128)S(1)} %get-tuple-element.12), channel_id=1, source_target_pairs={{0,1},{1,0},{2,3},{3,2},{4,5},{5,4},{6,7},{7,6},{8,9},{9,8},{10,11... | collective-permute-start | bytes 110600 | tf_op jit(solution)/shard_map/ppermute | solution.py:393

commit v11 on v9

--- a/solution.py
+++ b/solution.py
@@ -13,6 +13,7 @@
 SHIFT = 7
 ROWS = EDGE * FACE // LANES
 COARSE = 0.2
+SLOT_ROWS = ROWS + 1
 TILE = 8
 
 
@@ -30,7 +31,6 @@
 
 def pair_kernel(
     slot_depth,
-    width,
     bricks_group,
     pairs_hbm,
     dest_hbm,
@@ -53,8 +53,7 @@
     block_sems,
 ):
     items = blocks_ref.shape[0]
-    part_rows = ROWS // width
-    chunks = out_ref.shape[0] // (part_rows + 1)
+    slots = out_ref.shape[0] // SLOT_ROWS
     lists = [
         pltpu.make_async_copy(source, target, list_sems.at[n])
         for n, (source, target) in enumerate(
@@ -94,14 +93,8 @@
                 copy.start()
     for copy in lists[1:]:
         copy.wait()
-    if chunks != items * width:
+    if slots != items:
         out_ref[...] = jnp.zeros_like(out_ref)
-
-    def first_row(k, part):
-        slot = dest_ref[k]
-        chunk = (slot // slot_depth * width + part) * slot_depth + lax.rem(slot, slot_depth)
-        return chunk * (part_rows + 1)
-
     steps = iota((EDGE, LANES), 0).astype(jnp.float32) - (EDGE - 1) / 2.0
 
     for k in range(items):
@@ -126,7 +119,6 @@
 
         row_x, row_face = factors(0)
         col_x, col_face = factors(1)
-        row_x = row_x.T
         row_face = row_face.T
         block = blocks_ref[k]
         for x in range(EDGE):
@@ -134,20 +126,17 @@
             product = lax.dot_general(
                 block, col, (((1,), (1,)), ((), ())), preferred_element_type=jnp.float32
             )
-            dens = jnp.sum(row_x[:, x : x + 1] * row_face * product, axis=0, keepdims=True)
+            weight = jnp.broadcast_to(row_x[x : x + 1, :], (LANES, block.shape[0])).T
+            weight = jnp.concatenate([weight] * (FACE // LANES), axis=1)
+            dens = jnp.sum(weight * row_face * product, axis=0, keepdims=True)
             for half in range(FACE // LANES):
                 piece = dens[:, half * LANES : (half + 1) * LANES]
-                part, row = divmod(2 * x + half, part_rows)
-                out_ref[pl.ds(first_row(k, part) + row, 1), :] = piece
+                out_ref[pl.ds(dest_ref[k] * SLOT_ROWS + 2 * x + half, 1), :] = piece
                 if x in (0, EDGE - 1):
                     corner_buf[2 * (x // (EDGE - 1)) + half, pl.ds(k, 1), :] = piece
 
-    unroll = 4 if items % 4 == 0 else 1
-
-    @pl.loop(0, items // unroll)
-    def _(step):
-        for n in range(unroll):
-            one(step * unroll + n)
+    for k in range(items):
+        one(k)
 
     shape = (items, LANES)
     lane = iota(shape, 1)
@@ -169,46 +158,36 @@
     placed = jnp.where(lane == 8 * items + row, brick.astype(jnp.float32), placed)
     meta = jnp.sum(placed, axis=0, keepdims=True)
     last_lane = iota((1, LANES), 1) == LANES - 1
-    if chunks != items * width:
-
-        @pl.loop(0, chunks)
+    if slots != items:
+
+        @pl.loop(0, slots)
         def _(n):
-            out_ref[pl.ds(n * (part_rows + 1) + part_rows, 1), :] = jnp.where(
-                last_lane, -1.0, meta
-            )
+            out_ref[pl.ds(n * SLOT_ROWS + ROWS, 1), :] = jnp.where(last_lane, -1.0, meta)
 
     for k in range(items):
         tagged = jnp.where(last_lane, tag_ref[k].astype(jnp.float32), meta)
-        for part in range(width):
-            out_ref[pl.ds(first_row(k, part) + part_rows, 1), :] = tagged
-
-
-def group_kernel(items, bricks_dev, width, owners, shifts, in_ref, *outs):
+        out_ref[pl.ds(dest_ref[k] * SLOT_ROWS + ROWS, 1), :] = tagged
+
+
+def group_kernel(items, bricks_dev, moves, in_ref, *outs):
     me = lax.axis_index("basis")
-    part_rows = ROWS // width
-    chunks = in_ref.shape[0] // (part_rows + 1)
-    meta = [
-        in_ref[n * (part_rows + 1) + part_rows : (n + 1) * (part_rows + 1), :]
-        for n in range(chunks)
-    ]
-    tags = [
-        jnp.broadcast_to(line[:, LANES - 1 :], (part_rows, LANES)) for line in meta
-    ]
-    for d in range(owners):
+    slots = in_ref.shape[0] // SLOT_ROWS
+    meta = [in_ref[n * SLOT_ROWS + ROWS : (n + 1) * SLOT_ROWS, :] for n in range(slots)]
+    tags = [jnp.broadcast_to(line[:, LANES - 1 :], (ROWS, LANES)) for line in meta]
+    for out, move in zip(outs, [range(len(outs)), *moves]):
+        owner = sum(jnp.where(me == i, to, 0) for i, to in enumerate(move))
         for b in range(bricks_dev):
-            brick = (owner_of(me, d, owners, width) * bricks_dev + b).astype(jnp.float32)
-            total = jnp.zeros((part_rows, LANES), jnp.float32)
-            for n in range(chunks):
-                dens = in_ref[n * (part_rows + 1) : n * (part_rows + 1) + part_rows, :]
+            brick = (owner * bricks_dev + b).astype(jnp.float32)
+            total = jnp.zeros((ROWS, LANES), jnp.float32)
+            for n in range(slots):
+                dens = in_ref[n * SLOT_ROWS : n * SLOT_ROWS + ROWS, :]
                 total = total + jnp.where(tags[n] == brick, dens, 0.0)
-            for out, shift in zip(outs, shifts):
-                if shift == d:
-                    out[b * part_rows : (b + 1) * part_rows, :] = total
-    table_rows = outs[0].shape[0] - bricks_dev * part_rows
+            out[b * ROWS : (b + 1) * ROWS, :] = total
+    table_rows = outs[0].shape[0] - bricks_dev * ROWS
     shape = (TILE, LANES)
     lane = iota(shape, 1)
     lines = [jnp.zeros(shape, jnp.float32) for _ in range(table_rows)]
-    for first in range(0, chunks, TILE):
+    for first in range(0, slots, TILE):
         block = jnp.concatenate(meta[first : first + TILE], axis=0)
         for k in range(items):
             values = lane_pick(block, 8 * k + (lane & 7))
@@ -218,7 +197,7 @@
                 lines[r] = lines[r] + jnp.where(brick >> 4 == r, values, 0.0)
     table = jnp.concatenate([jnp.sum(line, axis=0, keepdims=True) for line in lines], axis=0)
     for out in outs:
-        out[bricks_dev * part_rows :, :] = table
+        out[bricks_dev * ROWS :, :] = table
 
 
 def map_kernel(cells_ref, out_ref):
@@ -237,29 +216,13 @@
         out_ref[b] = found.astype(jnp.int32) - 1
 
 
-def cell_kernel(width, shifts, *refs):
+def cell_kernel(*refs):
     *ins, map_ref, refs_ref, out_ref = refs
     bricks_dev, _, cells = refs_ref.shape
-    part_rows = ROWS // width
-    mine = lax.axis_index("basis") % width
-
-    totals = []
-    for offset in range(width):
-        parts = [part for part, shift in zip(ins, shifts) if shift % width == offset]
-        total = parts[0][...]
-        for part in parts[1:]:
-            total = total + part[...]
-        totals.append(total)
-    table = totals[0][bricks_dev * part_rows :]
-
-    def own_points(b):
-        halves = [total[b * part_rows : (b + 1) * part_rows] for total in totals]
-        if width == 1:
-            return halves[0]
-        straight = jnp.concatenate(halves, axis=0)
-        crossed = jnp.concatenate(halves[::-1], axis=0)
-        return jnp.where(mine == 0, straight, crossed)
-
+    total = ins[0][...]
+    for part in ins[1:]:
+        total = total + part[...]
+    table = total[bricks_dev * ROWS :]
     chunk = (TILE, LANES)
     tiles = cells // LANES
     refs = [
@@ -280,25 +243,16 @@
             line = jnp.sum(picked[b][c], axis=0, keepdims=True) * (0.5 / 8.0)
             found = lane_pick(jnp.broadcast_to(line, (ROWS, LANES)), (cell & (LANES - 1)))
             mean = jnp.where(cell >> SHIFT == c, found, mean)
-        own = own_points(b)
+        own = total[b * ROWS : (b + 1) * ROWS]
         result = jnp.where(cell >= 0, 0.5 * own + mean, own)
         for row in range(ROWS):
             out_ref[b : b + 1, row * LANES : (row + 1) * LANES] = result[row : row + 1, :]
 
 
-def owner_of(index, shift, owners, width):
-    sets = owners // width
-    pair, side = index // width, index % width
-    jump, turn = divmod(shift, width)
-    pair = pair ^ jump if sets & (sets - 1) == 0 else (pair + jump) % sets
-    return pair * width + (side ^ turn)
-
-
-def exchanges(owners, width):
-    return [
-        (d, [(i, owner_of(i, d, owners, width)) for i in range(owners)])
-        for d in range(owners - 1, 0, -1)
-    ]
+def moves_of(owners):
+    if owners == 4:
+        return [(2, 3, 1, 0), (3, 2, 0, 1), (1, 0, 3, 2)]
+    return [tuple((i + d) % owners for i in range(owners)) for d in range(1, owners)]
 
 
 def vmem():
@@ -318,14 +272,11 @@
     bricks_dev = bricks_group // owners
     table_rows = -(-bricks * 8 // (8 * LANES)) * 8
     basis = block_data.shape[1]
-    width = 2 if owners % 2 == 0 else 1
-    part_rows = ROWS // width
-    chunks = slots * width
     params = pltpu.CompilerParams(vmem_limit_bytes=32 * 1024 * 1024)
 
     outgoing = pl.pallas_call(
-        functools.partial(pair_kernel, slot_depth, width, bricks_group),
-        out_shape=jax.ShapeDtypeStruct((chunks * (part_rows + 1), LANES), jnp.float32),
+        functools.partial(pair_kernel, slot_depth, bricks_group),
+        out_shape=jax.ShapeDtypeStruct((slots * SLOT_ROWS, LANES), jnp.float32),
         in_specs=[pl.BlockSpec(memory_space=pltpu.HBM)] * 7,
         out_specs=vmem(),
         scratch_shapes=[
@@ -357,33 +308,26 @@
             )
         )
     )
-    sets = [
-        [g * owners + first + side for g in range(groups) for side in range(width)]
-        for first in range(0, owners, width)
-    ]
     arrived = lax.all_to_all(
-        outgoing.reshape(chunks, 1, (part_rows + 1) * LANES),
-        ("row", "col", "basis"),
+        outgoing.reshape(slots, 1, SLOT_ROWS * LANES),
+        ("row", "col"),
         split_axis=0,
         concat_axis=0,
         tiled=True,
-        axis_index_groups=sets,
     ).reshape(outgoing.shape)
-    moves = exchanges(owners, width)
-    shifts = [0] + [d for d, _ in moves]
+    moves = moves_of(owners)
     partial = pl.pallas_call(
-        functools.partial(group_kernel, items, bricks_dev, width, owners, shifts),
-        out_shape=[
-            jax.ShapeDtypeStruct((bricks_dev * part_rows + table_rows, LANES), jnp.float32)
-            for _ in shifts
-        ],
+        functools.partial(group_kernel, items, bricks_dev, moves),
+        out_shape=[jax.ShapeDtypeStruct((bricks_dev * ROWS + table_rows, LANES), jnp.float32)]
+        * owners,
         in_specs=[vmem()],
-        out_specs=[vmem()] * len(shifts),
+        out_specs=[vmem()] * owners,
         compiler_params=params,
         name="group_sum",
     )(arrived)
     parts = [partial[0]] + [
-        lax.ppermute(piece, "basis", pairs) for piece, (_, pairs) in zip(partial[1:], moves)
+        lax.ppermute(piece, "basis", list(enumerate(move)))
+        for piece, move in zip(partial[1:], moves)
     ]
     cell_map = pl.pallas_call(
         map_kernel,
@@ -395,7 +339,7 @@
         name="cell_map",
     )(cell_pos)
     return pl.pallas_call(
-        functools.partial(cell_kernel, width, shifts),
+        cell_kernel,
         out_shape=jax.ShapeDtypeStruct((bricks_dev, EDGE * FACE), jnp.float32),
         in_specs=[vmem()] * (len(parts) + 2),
         out_specs=vmem(),

time: 27.4 us -> 25.1 us (0.916)
  blocking collectives: 12 us -> 9.92 us
  waiting for transfers between devices: 2.98 us -> 3.73 us
  Pallas kernels: 7.68 us -> 6.99 us
    all_to_all x1, blocking collectives: 12 us -> 9.92 us  [body(): lax.all_to_all(outgoing.reshape(slots, 1, SLOT_ROWS * LANES), ('row', 'co...]
    ppermute x3, waiting for transfers between devices: 2.98 us -> 3.73 us  [body(): lax.ppermute(piece, 'basis', list(enumerate(move)))]
    pallas_call x3, Pallas kernels: 7.53 us -> 6.84 us  [the longest x1 5.76 us: body(): pl.pallas_call(functools.partial(pair_kernel, slot_depth, bricks_group),...]
  transfers between devices with their start and end apart: 3 -> 3, of which waited for: 2 -> 3; matrix products, arithmetic and copies ran while one was open for 0% -> 0% of each run, Pallas kernels for 1% -> 1%
where the time goes in v11:
time: 25.1 us; the launch traced here: 24.9 us
  blocking collectives  9.92 us (40%)
  Pallas kernels  6.99 us (28%)
  starting transfers between devices  4.23 us (17%)
  waiting for transfers between devices  3.73 us (15%)
    all_to_all x1, blocking collectives, body(): lax.all_to_all(outgoing.reshape(slots, 1, SLOT_ROWS * LANES), ('row', 'co...  9.92 us
    pallas_call x1, Pallas kernels, body(): pl.pallas_call(functools.partial(pair_kernel, slot_depth, bricks_group),...  5.76 us
    ppermute x3, starting transfers between devices, body(): lax.ppermute(piece, 'basis', list(enumerate(move)))  4.23 us
    ppermute x3, waiting for transfers between devices, body(): lax.ppermute(piece, 'basis', list(enumerate(move)))  3.73 us
    pallas_call x1, Pallas kernels, body(): pl.pallas_call(cell_kernel, out_shape=jax.ShapeDtypeStruct((bricks_dev, E...  0.88 us
  transfers between devices with their start and end apart: 3, of which 3 were waited for; matrix products, arithmetic and copies ran while one was open for 0% of the time, Pallas kernels for 1%

profile of v11, /device:TPU:0, one launch (start us, length us, event | category | flops | bytes accessed | tf_op | source)
XLA Modules:
  0.0 24.9 jit_solution(10415841991623015327)
XLA Ops:
  0.0 0.0 copy-start.1
  0.0 0.0 copy-start
  0.0 5.8 %pair_density.1 = f32[264,128]{1,0:T(8,128)S(1)} custom-call(s32[2,8]{1,0:T(2,128)} %bitcast.9, s32[8]{0:T(128)} %dest_hbm.1, s32[8]{0:T(128)} %tag_hbm.1, s32[64]{0:T(128)} %levels_hbm.1, bf16[8,128,128]{2,1,0:T(8,128)(2,1)} %blocks_hbm.1, f32[3,1024,128]{2,1,0:T(8,128)} %bitcast.8, f32[1024,128]{1,0:T(8,128)} %exponents_ref.1), custom_call_target="tpu_custom_call" | custom-call | tf_op jit(solution)/shard_map/pair_density/pallas_call | solution.py:277
  5.8 9.9 %all_to_all.5 = f32[8,1,4224]{2,1,0:T(1,128)S(1)} all-to-all(f32[8,1,4224]{2,1,0:T(1,128)S(1)} %bitcast.5), channel_id=1, replica_groups=mesh['row'=4,'col'=2,'basis'=4] {'row','col'}, dimensions={0} | all-to-all | bytes 270336 | tf_op jit(solution)/shard_map/all_to_all | solution.py:311
  15.7 0.2 group_sum.1
  15.9 2.6 %collective-permute-start = (f32[72,128]{1,0:T(8,128)S(1)}, f32[72,128]{1,0:T(8,128)S(1)}, u32[]{:S(2)}, u32[]{:S(2)}) collective-permute-start(f32[72,128]{1,0:T(8,128)S(1)} %get-tuple-element.10), channel_id=1, source_target_pairs={{0,2},{1,3},{2,1},{3,0},{4,6},{5,7},{6,5},{7,4},{8,10},{9,11},{10,... | collective-permute-start | bytes 110600 | tf_op jit(solution)/shard_map/ppermute | solution.py:329
  18.6 1.2 %collective-permute-start.1 = (f32[72,128]{1,0:T(8,128)S(1)}, f32[72,128]{1,0:T(8,128)S(1)}, u32[]{:S(2)}, u32[]{:S(2)}) collective-permute-start(f32[72,128]{1,0:T(8,128)S(1)} %get-tuple-element.11), channel_id=1, source_target_pairs={{0,3},{1,2},{2,0},{3,1},{4,7},{5,6},{6,4},{7,5},{8,11},{9,10},{10,... | collective-permute-start | bytes 110600 | tf_op jit(solution)/shard_map/ppermute | solution.py:329
  19.8 0.4 %collective-permute-start.2 = (f32[72,128]{1,0:T(8,128)S(1)}, f32[72,128]{1,0:T(8,128)S(1)}, u32[]{:S(2)}, u32[]{:S(2)}) collective-permute-start(f32[72,128]{1,0:T(8,128)S(1)} %get-tuple-element.12), channel_id=1, source_target_pairs={{0,1},{1,0},{2,3},{3,2},{4,5},{5,4},{6,7},{7,6},{8,9},{9,8},{10,11... | collective-permute-start | bytes 110600 | tf_op jit(solution)/shard_map/ppermute | solution.py:329
  20.1 0.0 copy-done.1
  20.1 0.1 cell_map.1.refs_4_
  20.3 1.4 %collective-permute-done.refs_1_ = f32[72,128]{1,0:T(8,128)S(1)} collective-permute-done((f32[72,128]{1,0:T(8,128)S(1)}, f32[72,128]{1,0:T(8,128)S(1)}, u32[]{:S(2)}, u32[]{:S(2)}) %collective-permute-start) | collective-permute-done | bytes 36896 | tf_op jit(solution)/shard_map/ppermute | solution.py:329
  21.7 2.2 %collective-permute-done.1.refs_2_ = f32[72,128]{1,0:T(8,128)S(1)} collective-permute-done((f32[72,128]{1,0:T(8,128)S(1)}, f32[72,128]{1,0:T(8,128)S(1)}, u32[]{:S(2)}, u32[]{:S(2)}) %collective-permute-start.1) | collective-permute-done | bytes 36896 | tf_op jit(solution)/shard_map/ppermute | solution.py:329
  23.9 0.1 collective-permute-done.2.refs_3_
  24.0 0.0 copy-done
  24.0 0.9 %cells.1 = f32[2,4096]{1,0:T(2,128)} custom-call(f32[72,128]{1,0:T(8,128)S(1)} %get-tuple-element.9.refs_0_, f32[72,128]{1,0:T(8,128)S(1)} %collective-permute-done.refs_1_, f32[72,128]{1,0:T(8,128)S(1)} %collective-permute-done.1.refs_2_, f32[72,128]{1,0:T(8,128)S(1)} %collective-permute-done.2.refs_3_, s32[2,32,128]{2,1,0:T(8,128)S(1)} %cell_map.1.refs_4_, ...), custom_call_target="tpu_custom_call" | custom-call | tf_op jit(solution)/shard_map/cells/pallas_call | solution.py:341
Async XLA Ops:
  0.0 20.1 %copy-start.1 = (s32[2,256]{1,0:T(2,128)S(1)}, s32[2,256]{1,0:T(2,128)}, u32[]{:S(2)}) copy-start(s32[2,256]{1,0:T(2,128)} %cells_ref.1) | copy-start | bytes 6148
  0.0 24.0 %copy-start = (s32[2,256,8]{1,2,0:T(8,128)S(1)}, s32[2,256,8]{1,2,0:T(8,128)}, u32[]{:S(2)}) copy-start(s32[2,256,8]{1,2,0:T(8,128)} %param.17) | copy-start | bytes 49156
  15.9 5.8 %collective-permute-start = (f32[72,128]{1,0:T(8,128)S(1)}, f32[72,128]{1,0:T(8,128)S(1)}, u32[]{:S(2)}, u32[]{:S(2)}) collective-permute-start(f32[72,128]{1,0:T(8,128)S(1)} %get-tuple-element.10), channel_id=1, source_target_pairs={{0,2},{1,3},{2,1},{3,0},{4,6},{5,7},{6,5},{7,4},{8,10},{9,11},{10,... | collective-permute-start | bytes 110600 | tf_op jit(solution)/shard_map/ppermute | solution.py:329
  18.6 5.4 %collective-permute-start.1 = (f32[72,128]{1,0:T(8,128)S(1)}, f32[72,128]{1,0:T(8,128)S(1)}, u32[]{:S(2)}, u32[]{:S(2)}) collective-permute-start(f32[72,128]{1,0:T(8,128)S(1)} %get-tuple-element.11), channel_id=1, source_target_pairs={{0,3},{1,2},{2,0},{3,1},{4,7},{5,6},{6,4},{7,5},{8,11},{9,10},{10,... | collective-permute-start | bytes 110600 | tf_op jit(solution)/shard_map/ppermute | solution.py:329
  19.8 4.2 %collective-permute-start.2 = (f32[72,128]{1,0:T(8,128)S(1)}, f32[72,128]{1,0:T(8,128)S(1)}, u32[]{:S(2)}, u32[]{:S(2)}) collective-permute-start(f32[72,128]{1,0:T(8,128)S(1)} %get-tuple-element.12), channel_id=1, source_target_pairs={{0,1},{1,0},{2,3},{3,2},{4,5},{5,4},{6,7},{7,6},{8,9},{9,8},{10,11... | collective-permute-start | bytes 110600 | tf_op jit(solution)/shard_map/ppermute | solution.py:329

commit v12 on v11

--- a/solution.py
+++ b/solution.py
@@ -37,20 +37,19 @@
     tag_hbm,
     levels_hbm,
     blocks_hbm,
-    centres_ref,
-    exponents_ref,
+    centres_hbm,
+    exponents_hbm,
     out_ref,
     pairs_ref,
     dest_ref,
     tag_ref,
     levels_ref,
     blocks_ref,
-    centre_buf,
-    decay_buf,
+    centres_ref,
+    exponents_ref,
     corner_buf,
-    sems,
     list_sems,
-    block_sems,
+    table_sems,
 ):
     items = blocks_ref.shape[0]
     slots = out_ref.shape[0] // SLOT_ROWS
@@ -68,50 +67,29 @@
     for copy in lists:
         copy.start()
 
-    def block_copy(k):
-        return pltpu.make_async_copy(blocks_hbm.at[k], blocks_ref.at[k], block_sems.at[k])
-
-    for k in range(items):
-        block_copy(k).start()
-    lists[0].wait()
-
-    def copies(k, side):
-        block = pairs_ref[side, k]
-        at = 2 * k + side
-        return (
-            pltpu.make_async_copy(
-                centres_ref.at[:, pl.ds(block, 1), :], centre_buf.at[at], sems.at[0, at]
-            ),
-            pltpu.make_async_copy(
-                exponents_ref.at[pl.ds(block, 1), :], decay_buf.at[at], sems.at[1, at]
-            ),
-        )
-
-    for k in range(items):
-        for side in range(2):
-            for copy in copies(k, side):
-                copy.start()
-    for copy in lists[1:]:
+    tables = [
+        pltpu.make_async_copy(centres_hbm.at[d], centres_ref.at[d], table_sems.at[d])
+        for d in range(3)
+    ]
+    tables.append(pltpu.make_async_copy(exponents_hbm, exponents_ref, table_sems.at[3]))
+    tables.append(pltpu.make_async_copy(blocks_hbm, blocks_ref, table_sems.at[4]))
+    for copy in tables:
+        copy.start()
+    for copy in lists + tables:
         copy.wait()
     if slots != items:
         out_ref[...] = jnp.zeros_like(out_ref)
     steps = iota((EDGE, LANES), 0).astype(jnp.float32) - (EDGE - 1) / 2.0
 
-    for k in range(items):
-        for side in range(2):
-            for copy in copies(k, side):
-                copy.wait()
-        block_copy(k).wait()
-
     def one(k):
         target = dest_ref[k] // slot_depth * bricks_group + tag_ref[k]
         spacing = jnp.where(levels_ref[target] == 1, COARSE * 0.5, COARSE)
         coords = steps * spacing
 
         def factors(side):
-            at = 2 * k + side
-            decay = decay_buf[at]
-            found = [axis_factors(coords, centre_buf[at, d], decay) for d in range(3)]
+            row = pl.ds(pairs_ref[side, k], 1)
+            decay = exponents_ref[row, :]
+            found = [axis_factors(coords, centres_ref[d, row, :], decay) for d in range(3)]
             face = jnp.concatenate(
                 [found[1][y : y + 1, :] * found[2] for y in range(EDGE)], axis=0
             )
@@ -285,12 +263,11 @@
             pltpu.SMEM((items,), jnp.int32),
             pltpu.SMEM((bricks,), jnp.int32),
             pltpu.VMEM(block_data.shape, block_data.dtype),
-            pltpu.VMEM((2 * items, 3, 1, basis), jnp.float32),
-            pltpu.VMEM((2 * items, 1, basis), jnp.float32),
+            pltpu.VMEM((3, centres.shape[0], basis), jnp.float32),
+            pltpu.VMEM(exponents.shape, jnp.float32),
             pltpu.VMEM((4, items, LANES), jnp.float32),
-            pltpu.SemaphoreType.DMA((2, 2 * items)),
             pltpu.SemaphoreType.DMA((4,)),
-            pltpu.SemaphoreType.DMA((items,)),
+            pltpu.SemaphoreType.DMA((5,)),
         ],
         compiler_params=params,
         name="pair_density",

time: 25.1 us -> 24.6 us (0.980)
  Pallas kernels: 6.99 us -> 6.53 us
    pallas_call x1, Pallas kernels: 5.76 us -> 5.3 us  [body(): pl.pallas_call(functools.partial(pair_kernel, slot_depth, bricks_group),...]
where the time goes in v12:
time: 24.6 us; the launch traced here: 24.5 us
  blocking collectives  9.96 us (40%)
  Pallas kernels  6.53 us (27%)
  starting transfers between devices  4.19 us (17%)
  waiting for transfers between devices  3.76 us (15%)
    all_to_all x1, blocking collectives, body(): lax.all_to_all(outgoing.reshape(slots, 1, SLOT_ROWS * LANES), ('row', 'co...  9.96 us
    pallas_call x1, Pallas kernels, body(): pl.pallas_call(functools.partial(pair_kernel, slot_depth, bricks_group),...  5.3 us
    ppermute x3, starting transfers between devices, body(): lax.ppermute(piece, 'basis', list(enumerate(move)))  4.19 us
    ppermute x3, waiting for transfers between devices, body(): lax.ppermute(piece, 'basis', list(enumerate(move)))  3.76 us
    pallas_call x1, Pallas kernels, body(): pl.pallas_call(cell_kernel, out_shape=jax.ShapeDtypeStruct((bricks_dev, E...  0.88 us
  transfers between devices with their start and end apart: 3, of which 3 were waited for; matrix products, arithmetic and copies ran while one was open for 0% of the time, Pallas kernels for 1%

profile of v12, /device:TPU:0, one launch (start us, length us, event | category | flops | bytes accessed | tf_op | source)
XLA Modules:
  0.0 24.5 jit_solution(13741385095066999744)
XLA Ops:
  0.0 0.0 copy-start.1
  0.0 0.0 copy-start
  0.0 5.3 %pair_density.1 = f32[264,128]{1,0:T(8,128)S(1)} custom-call(s32[2,8]{1,0:T(2,128)} %bitcast.9, s32[8]{0:T(128)} %dest_hbm.1, s32[8]{0:T(128)} %tag_hbm.1, s32[64]{0:T(128)} %levels_hbm.1, bf16[8,128,128]{2,1,0:T(8,128)(2,1)} %blocks_hbm.1, f32[3,1024,128]{2,1,0:T(8,128)} %bitcast.8, f32[1024,128]{1,0:T(8,128)} %exponents_hbm.1), custom_call_target="tpu_custom_call" | custom-call | tf_op jit(solution)/shard_map/pair_density/pallas_call | solution.py:255
  5.3 10.0 %all_to_all.5 = f32[8,1,4224]{2,1,0:T(1,128)S(1)} all-to-all(f32[8,1,4224]{2,1,0:T(1,128)S(1)} %bitcast.5), channel_id=1, replica_groups=mesh['row'=4,'col'=2,'basis'=4] {'row','col'}, dimensions={0} | all-to-all | bytes 270336 | tf_op jit(solution)/shard_map/all_to_all | solution.py:288
  15.3 0.2 group_sum.1
  15.5 2.6 %collective-permute-start = (f32[72,128]{1,0:T(8,128)S(1)}, f32[72,128]{1,0:T(8,128)S(1)}, u32[]{:S(2)}, u32[]{:S(2)}) collective-permute-start(f32[72,128]{1,0:T(8,128)S(1)} %get-tuple-element.10), channel_id=1, source_target_pairs={{0,2},{1,3},{2,1},{3,0},{4,6},{5,7},{6,5},{7,4},{8,10},{9,11},{10,... | collective-permute-start | bytes 110600 | tf_op jit(solution)/shard_map/ppermute | solution.py:306
  18.1 1.3 %collective-permute-start.1 = (f32[72,128]{1,0:T(8,128)S(1)}, f32[72,128]{1,0:T(8,128)S(1)}, u32[]{:S(2)}, u32[]{:S(2)}) collective-permute-start(f32[72,128]{1,0:T(8,128)S(1)} %get-tuple-element.11), channel_id=1, source_target_pairs={{0,3},{1,2},{2,0},{3,1},{4,7},{5,6},{6,4},{7,5},{8,11},{9,10},{10,... | collective-permute-start | bytes 110600 | tf_op jit(solution)/shard_map/ppermute | solution.py:306
  19.4 0.3 %collective-permute-start.2 = (f32[72,128]{1,0:T(8,128)S(1)}, f32[72,128]{1,0:T(8,128)S(1)}, u32[]{:S(2)}, u32[]{:S(2)}) collective-permute-start(f32[72,128]{1,0:T(8,128)S(1)} %get-tuple-element.12), channel_id=1, source_target_pairs={{0,1},{1,0},{2,3},{3,2},{4,5},{5,4},{6,7},{7,6},{8,9},{9,8},{10,11... | collective-permute-start | bytes 110600 | tf_op jit(solution)/shard_map/ppermute | solution.py:306
  19.7 0.0 copy-done.1
  19.7 0.1 cell_map.1.refs_4_
  19.8 1.5 %collective-permute-done.refs_1_ = f32[72,128]{1,0:T(8,128)S(1)} collective-permute-done((f32[72,128]{1,0:T(8,128)S(1)}, f32[72,128]{1,0:T(8,128)S(1)}, u32[]{:S(2)}, u32[]{:S(2)}) %collective-permute-start) | collective-permute-done | bytes 36896 | tf_op jit(solution)/shard_map/ppermute | solution.py:306
  21.3 2.2 %collective-permute-done.1.refs_2_ = f32[72,128]{1,0:T(8,128)S(1)} collective-permute-done((f32[72,128]{1,0:T(8,128)S(1)}, f32[72,128]{1,0:T(8,128)S(1)}, u32[]{:S(2)}, u32[]{:S(2)}) %collective-permute-start.1) | collective-permute-done | bytes 36896 | tf_op jit(solution)/shard_map/ppermute | solution.py:306
  23.4 0.1 collective-permute-done.2.refs_3_
  23.6 0.0 copy-done
  23.6 0.9 %cells.1 = f32[2,4096]{1,0:T(2,128)} custom-call(f32[72,128]{1,0:T(8,128)S(1)} %get-tuple-element.9.refs_0_, f32[72,128]{1,0:T(8,128)S(1)} %collective-permute-done.refs_1_, f32[72,128]{1,0:T(8,128)S(1)} %collective-permute-done.1.refs_2_, f32[72,128]{1,0:T(8,128)S(1)} %collective-permute-done.2.refs_3_, s32[2,32,128]{2,1,0:T(8,128)S(1)} %cell_map.1.refs_4_, ...), custom_call_target="tpu_custom_call" | custom-call | tf_op jit(solution)/shard_map/cells/pallas_call | solution.py:318
Async XLA Ops:
  0.0 19.7 %copy-start.1 = (s32[2,256]{1,0:T(2,128)S(1)}, s32[2,256]{1,0:T(2,128)}, u32[]{:S(2)}) copy-start(s32[2,256]{1,0:T(2,128)} %cells_ref.1) | copy-start | bytes 6148
  0.0 23.6 %copy-start = (s32[2,256,8]{1,2,0:T(8,128)S(1)}, s32[2,256,8]{1,2,0:T(8,128)}, u32[]{:S(2)}) copy-start(s32[2,256,8]{1,2,0:T(8,128)} %param.17) | copy-start | bytes 49156
  15.5 5.8 %collective-permute-start = (f32[72,128]{1,0:T(8,128)S(1)}, f32[72,128]{1,0:T(8,128)S(1)}, u32[]{:S(2)}, u32[]{:S(2)}) collective-permute-start(f32[72,128]{1,0:T(8,128)S(1)} %get-tuple-element.10), channel_id=1, source_target_pairs={{0,2},{1,3},{2,1},{3,0},{4,6},{5,7},{6,5},{7,4},{8,10},{9,11},{10,... | collective-permute-start | bytes 110600 | tf_op jit(solution)/shard_map/ppermute | solution.py:306
  18.1 5.4 %collective-permute-start.1 = (f32[72,128]{1,0:T(8,128)S(1)}, f32[72,128]{1,0:T(8,128)S(1)}, u32[]{:S(2)}, u32[]{:S(2)}) collective-permute-start(f32[72,128]{1,0:T(8,128)S(1)} %get-tuple-element.11), channel_id=1, source_target_pairs={{0,3},{1,2},{2,0},{3,1},{4,7},{5,6},{6,4},{7,5},{8,11},{9,10},{10,... | collective-permute-start | bytes 110600 | tf_op jit(solution)/shard_map/ppermute | solution.py:306
  19.4 4.2 %collective-permute-start.2 = (f32[72,128]{1,0:T(8,128)S(1)}, f32[72,128]{1,0:T(8,128)S(1)}, u32[]{:S(2)}, u32[]{:S(2)}) collective-permute-start(f32[72,128]{1,0:T(8,128)S(1)} %get-tuple-element.12), channel_id=1, source_target_pairs={{0,1},{1,0},{2,3},{3,2},{4,5},{5,4},{6,7},{7,6},{8,9},{9,8},{10,11... | collective-permute-start | bytes 110600 | tf_op jit(solution)/shard_map/ppermute | solution.py:306

commit v13 on v12

--- a/solution.py
+++ b/solution.py
@@ -50,6 +50,7 @@
     corner_buf,
     list_sems,
     table_sems,
+    block_sem,
 ):
     items = blocks_ref.shape[0]
     slots = out_ref.shape[0] // SLOT_ROWS
@@ -67,13 +68,19 @@
     for copy in lists:
         copy.start()
 
+    pieces = 4
+    rows = exponents_ref.shape[0] // pieces
+    tables = []
+    for n in range(pieces):
+        part = pl.ds(n * rows, rows)
+        tables.append((exponents_hbm.at[part], exponents_ref.at[part]))
+        tables.extend((centres_hbm.at[d, part], centres_ref.at[d, part]) for d in range(3))
     tables = [
-        pltpu.make_async_copy(centres_hbm.at[d], centres_ref.at[d], table_sems.at[d])
-        for d in range(3)
+        pltpu.make_async_copy(source, target, table_sems.at[n])
+        for n, (source, target) in enumerate(tables)
     ]
-    tables.append(pltpu.make_async_copy(exponents_hbm, exponents_ref, table_sems.at[3]))
-    tables.append(pltpu.make_async_copy(blocks_hbm, blocks_ref, table_sems.at[4]))
-    for copy in tables:
+    blocks = pltpu.make_async_copy(blocks_hbm, blocks_ref, block_sem)
+    for copy in tables + [blocks]:
         copy.start()
     for copy in lists + tables:
         copy.wait()
@@ -98,6 +105,8 @@
         row_x, row_face = factors(0)
         col_x, col_face = factors(1)
         row_face = row_face.T
+        if k == 0:
+            blocks.wait()
         block = blocks_ref[k]
         for x in range(EDGE):
             col = (col_x[x : x + 1, :] * col_face).astype(jnp.bfloat16)
@@ -267,7 +276,8 @@
             pltpu.VMEM(exponents.shape, jnp.float32),
             pltpu.VMEM((4, items, LANES), jnp.float32),
             pltpu.SemaphoreType.DMA((4,)),
-            pltpu.SemaphoreType.DMA((5,)),
+            pltpu.SemaphoreType.DMA((16,)),
+            pltpu.SemaphoreType.DMA,
         ],
         compiler_params=params,
         name="pair_density",

time: 24.6 us -> 24.9 us (1.012)
  Pallas kernels: 6.53 us -> 6.81 us
    pallas_call x1, Pallas kernels: 5.3 us -> 5.58 us  [body(): pl.pallas_call(functools.partial(pair_kernel, slot_depth, bricks_group),...]
where the time goes in v13:
time: 24.9 us; the launch traced here: 24.7 us
  blocking collectives  9.94 us (40%)
  Pallas kernels  6.81 us (27%)
  starting transfers between devices  4.21 us (17%)
  waiting for transfers between devices  3.76 us (15%)
    all_to_all x1, blocking collectives, body(): lax.all_to_all(outgoing.reshape(slots, 1, SLOT_ROWS * LANES), ('row', 'co...  9.94 us
    pallas_call x1, Pallas kernels, body(): pl.pallas_call(functools.partial(pair_kernel, slot_depth, bricks_group),...  5.58 us
    ppermute x3, starting transfers between devices, body(): lax.ppermute(piece, 'basis', list(enumerate(move)))  4.21 us
    ppermute x3, waiting for transfers between devices, body(): lax.ppermute(piece, 'basis', list(enumerate(move)))  3.76 us
    pallas_call x1, Pallas kernels, body(): pl.pallas_call(cell_kernel, out_shape=jax.ShapeDtypeStruct((bricks_dev, E...  0.88 us
  transfers between devices with their start and end apart: 3, of which 3 were waited for; matrix products, arithmetic and copies ran while one was open for 0% of the time, Pallas kernels for 1%

profile of v13, /device:TPU:0, one launch (start us, length us, event | category | flops | bytes accessed | tf_op | source)
XLA Modules:
  0.0 24.7 jit_solution(9874348451151618584)
XLA Ops:
  0.0 0.0 copy-start.1
  0.0 0.0 copy-start
  0.0 5.6 %pair_density.1 = f32[264,128]{1,0:T(8,128)S(1)} custom-call(s32[2,8]{1,0:T(2,128)} %bitcast.9, s32[8]{0:T(128)} %dest_hbm.1, s32[8]{0:T(128)} %tag_hbm.1, s32[64]{0:T(128)} %levels_hbm.1, bf16[8,128,128]{2,1,0:T(8,128)(2,1)} %blocks_hbm.1, f32[3,1024,128]{2,1,0:T(8,128)} %bitcast.8, f32[1024,128]{1,0:T(8,128)} %exponents_hbm.1), custom_call_target="tpu_custom_call" | custom-call | tf_op jit(solution)/shard_map/pair_density/pallas_call | solution.py:264
  5.6 9.9 %all_to_all.5 = f32[8,1,4224]{2,1,0:T(1,128)S(1)} all-to-all(f32[8,1,4224]{2,1,0:T(1,128)S(1)} %bitcast.5), channel_id=1, replica_groups=mesh['row'=4,'col'=2,'basis'=4] {'row','col'}, dimensions={0} | all-to-all | bytes 270336 | tf_op jit(solution)/shard_map/all_to_all | solution.py:298
  15.5 0.2 group_sum.1
  15.7 2.6 %collective-permute-start = (f32[72,128]{1,0:T(8,128)S(1)}, f32[72,128]{1,0:T(8,128)S(1)}, u32[]{:S(2)}, u32[]{:S(2)}) collective-permute-start(f32[72,128]{1,0:T(8,128)S(1)} %get-tuple-element.10), channel_id=1, source_target_pairs={{0,2},{1,3},{2,1},{3,0},{4,6},{5,7},{6,5},{7,4},{8,10},{9,11},{10,... | collective-permute-start | bytes 110600 | tf_op jit(solution)/shard_map/ppermute | solution.py:316
  18.4 1.2 %collective-permute-start.1 = (f32[72,128]{1,0:T(8,128)S(1)}, f32[72,128]{1,0:T(8,128)S(1)}, u32[]{:S(2)}, u32[]{:S(2)}) collective-permute-start(f32[72,128]{1,0:T(8,128)S(1)} %get-tuple-element.11), channel_id=1, source_target_pairs={{0,3},{1,2},{2,0},{3,1},{4,7},{5,6},{6,4},{7,5},{8,11},{9,10},{10,... | collective-permute-start | bytes 110600 | tf_op jit(solution)/shard_map/ppermute | solution.py:316
  19.6 0.3 %collective-permute-start.2 = (f32[72,128]{1,0:T(8,128)S(1)}, f32[72,128]{1,0:T(8,128)S(1)}, u32[]{:S(2)}, u32[]{:S(2)}) collective-permute-start(f32[72,128]{1,0:T(8,128)S(1)} %get-tuple-element.12), channel_id=1, source_target_pairs={{0,1},{1,0},{2,3},{3,2},{4,5},{5,4},{6,7},{7,6},{8,9},{9,8},{10,11... | collective-permute-start | bytes 110600 | tf_op jit(solution)/shard_map/ppermute | solution.py:316
  20.0 0.0 copy-done.1
  20.0 0.1 cell_map.1.refs_4_
  20.1 1.4 %collective-permute-done.refs_1_ = f32[72,128]{1,0:T(8,128)S(1)} collective-permute-done((f32[72,128]{1,0:T(8,128)S(1)}, f32[72,128]{1,0:T(8,128)S(1)}, u32[]{:S(2)}, u32[]{:S(2)}) %collective-permute-start) | collective-permute-done | bytes 36896 | tf_op jit(solution)/shard_map/ppermute | solution.py:316
  21.6 2.2 %collective-permute-done.1.refs_2_ = f32[72,128]{1,0:T(8,128)S(1)} collective-permute-done((f32[72,128]{1,0:T(8,128)S(1)}, f32[72,128]{1,0:T(8,128)S(1)}, u32[]{:S(2)}, u32[]{:S(2)}) %collective-permute-start.1) | collective-permute-done | bytes 36896 | tf_op jit(solution)/shard_map/ppermute | solution.py:316
  23.7 0.1 collective-permute-done.2.refs_3_
  23.9 0.0 copy-done
  23.9 0.9 %cells.1 = f32[2,4096]{1,0:T(2,128)} custom-call(f32[72,128]{1,0:T(8,128)S(1)} %get-tuple-element.9.refs_0_, f32[72,128]{1,0:T(8,128)S(1)} %collective-permute-done.refs_1_, f32[72,128]{1,0:T(8,128)S(1)} %collective-permute-done.1.refs_2_, f32[72,128]{1,0:T(8,128)S(1)} %collective-permute-done.2.refs_3_, s32[2,32,128]{2,1,0:T(8,128)S(1)} %cell_map.1.refs_4_, ...), custom_call_target="tpu_custom_call" | custom-call | tf_op jit(solution)/shard_map/cells/pallas_call | solution.py:328
Async XLA Ops:
  0.0 20.0 %copy-start.1 = (s32[2,256]{1,0:T(2,128)S(1)}, s32[2,256]{1,0:T(2,128)}, u32[]{:S(2)}) copy-start(s32[2,256]{1,0:T(2,128)} %cells_ref.1) | copy-start | bytes 6148
  0.0 23.9 %copy-start = (s32[2,256,8]{1,2,0:T(8,128)S(1)}, s32[2,256,8]{1,2,0:T(8,128)}, u32[]{:S(2)}) copy-start(s32[2,256,8]{1,2,0:T(8,128)} %param.17) | copy-start | bytes 49156
  15.7 5.8 %collective-permute-start = (f32[72,128]{1,0:T(8,128)S(1)}, f32[72,128]{1,0:T(8,128)S(1)}, u32[]{:S(2)}, u32[]{:S(2)}) collective-permute-start(f32[72,128]{1,0:T(8,128)S(1)} %get-tuple-element.10), channel_id=1, source_target_pairs={{0,2},{1,3},{2,1},{3,0},{4,6},{5,7},{6,5},{7,4},{8,10},{9,11},{10,... | collective-permute-start | bytes 110600 | tf_op jit(solution)/shard_map/ppermute | solution.py:316
  18.4 5.4 %collective-permute-start.1 = (f32[72,128]{1,0:T(8,128)S(1)}, f32[72,128]{1,0:T(8,128)S(1)}, u32[]{:S(2)}, u32[]{:S(2)}) collective-permute-start(f32[72,128]{1,0:T(8,128)S(1)} %get-tuple-element.11), channel_id=1, source_target_pairs={{0,3},{1,2},{2,0},{3,1},{4,7},{5,6},{6,4},{7,5},{8,11},{9,10},{10,... | collective-permute-start | bytes 110600 | tf_op jit(solution)/shard_map/ppermute | solution.py:316
  19.6 4.2 %collective-permute-start.2 = (f32[72,128]{1,0:T(8,128)S(1)}, f32[72,128]{1,0:T(8,128)S(1)}, u32[]{:S(2)}, u32[]{:S(2)}) collective-permute-start(f32[72,128]{1,0:T(8,128)S(1)} %get-tuple-element.12), channel_id=1, source_target_pairs={{0,1},{1,0},{2,3},{3,2},{4,5},{5,4},{6,7},{7,6},{8,9},{9,8},{10,11... | collective-permute-start | bytes 110600 | tf_op jit(solution)/shard_map/ppermute | solution.py:316

commit v14 on v12

--- a/solution.py
+++ b/solution.py
@@ -152,10 +152,15 @@
     slots = in_ref.shape[0] // SLOT_ROWS
     meta = [in_ref[n * SLOT_ROWS + ROWS : (n + 1) * SLOT_ROWS, :] for n in range(slots)]
     tags = [jnp.broadcast_to(line[:, LANES - 1 :], (ROWS, LANES)) for line in meta]
-    for out, move in zip(outs, [range(len(outs)), *moves]):
-        owner = sum(jnp.where(me == i, to, 0) for i, to in enumerate(move))
+    owned = sum(jnp.where(me == i, i, 0) for i in range(len(moves[0])))
+    sends = []
+    for out, move in zip(outs, [None, *moves]):
+        owner = owned
+        if move is not None:
+            owner = sum(jnp.where(me == i, -1 if i == to else to, 0) for i, to in enumerate(move))
+        sends.append(owner)
         for b in range(bricks_dev):
-            brick = (owner * bricks_dev + b).astype(jnp.float32)
+            brick = jnp.where(owner < 0, -2, owner * bricks_dev + b).astype(jnp.float32)
             total = jnp.zeros((ROWS, LANES), jnp.float32)
             for n in range(slots):
                 dens = in_ref[n * SLOT_ROWS : n * SLOT_ROWS + ROWS, :]
@@ -174,8 +179,8 @@
             for r in range(table_rows):
                 lines[r] = lines[r] + jnp.where(brick >> 4 == r, values, 0.0)
     table = jnp.concatenate([jnp.sum(line, axis=0, keepdims=True) for line in lines], axis=0)
-    for out in outs:
-        out[bricks_dev * ROWS :, :] = table
+    for out, owner in zip(outs, sends):
+        out[bricks_dev * ROWS :, :] = jnp.where(owner < 0, 0.0, table)
 
 
 def map_kernel(cells_ref, out_ref):
@@ -229,7 +234,9 @@
 
 def moves_of(owners):
     if owners == 4:
-        return [(2, 3, 1, 0), (3, 2, 0, 1), (1, 0, 3, 2)]
+        early = [(1, 2, 0, 3), (2, 0, 1, 3)]
+        late = [(3, 1, 2, 0), (0, 3, 2, 1), (0, 1, 3, 2)]
+        return early + late
     return [tuple((i + d) % owners for i in range(owners)) for d in range(1, owners)]
 
 
@@ -296,9 +303,9 @@
     partial = pl.pallas_call(
         functools.partial(group_kernel, items, bricks_dev, moves),
         out_shape=[jax.ShapeDtypeStruct((bricks_dev * ROWS + table_rows, LANES), jnp.float32)]
-        * owners,
+        * (len(moves) + 1),
         in_specs=[vmem()],
-        out_specs=[vmem()] * owners,
+        out_specs=[vmem()] * (len(moves) + 1),
         compiler_params=params,
         name="group_sum",
     )(arrived)

time: 24.6 us -> 31.9 us (1.30)
  the two profiles are of different devices: /device:TPU:0 before, /device:TPU:24 now
where the time goes in v14:
time: 31.9 us; the launch traced here: 31.7 us
  starting transfers between devices  12.7 us (40%)
  blocking collectives  8.49 us (27%)
  Pallas kernels  6.59 us (21%)
  waiting for transfers between devices  3.74 us (12%)
    ppermute x5, starting transfers between devices, body(): lax.ppermute(piece, 'basis', list(enumerate(move)))  12.7 us
    all_to_all x1, blocking collectives, body(): lax.all_to_all(outgoing.reshape(slots, 1, SLOT_ROWS * LANES), ('row', 'co...  8.49 us
    pallas_call x1, Pallas kernels, body(): pl.pallas_call(functools.partial(pair_kernel, slot_depth, bricks_group),...  5.32 us
    ppermute x5, waiting for transfers between devices, body(): lax.ppermute(piece, 'basis', list(enumerate(move)))  3.74 us
    pallas_call x1, Pallas kernels, body(): pl.pallas_call(cell_kernel, out_shape=jax.ShapeDtypeStruct((bricks_dev, E...  0.88 us
  transfers between devices with their start and end apart: 5, of which 2 were waited for; matrix products, arithmetic and copies ran while one was open for 0% of the time, Pallas kernels for 0%

profile of v14, /device:TPU:24, one launch (start us, length us, event | category | flops | bytes accessed | tf_op | source)
XLA Modules:
  0.0 31.7 jit_solution(9752150066972562145)
XLA Ops:
  0.0 0.0 copy-start.1
  0.0 0.0 copy-start
  0.0 5.3 %pair_density.1 = f32[264,128]{1,0:T(8,128)S(1)} custom-call(s32[2,8]{1,0:T(2,128)} %bitcast.9, s32[8]{0:T(128)} %dest_hbm.1, s32[8]{0:T(128)} %tag_hbm.1, s32[64]{0:T(128)} %levels_hbm.1, bf16[8,128,128]{2,1,0:T(8,128)(2,1)} %blocks_hbm.1, f32[3,1024,128]{2,1,0:T(8,128)} %bitcast.8, f32[1024,128]{1,0:T(8,128)} %exponents_hbm.1), custom_call_target="tpu_custom_call" | custom-call | tf_op jit(solution)/shard_map/pair_density/pallas_call | solution.py:262
  5.3 8.5 %all_to_all.5 = f32[8,1,4224]{2,1,0:T(1,128)S(1)} all-to-all(f32[8,1,4224]{2,1,0:T(1,128)S(1)} %bitcast.5), channel_id=1, replica_groups=mesh['row'=4,'col'=2,'basis'=4] {'row','col'}, dimensions={0} | all-to-all | bytes 270336 | tf_op jit(solution)/shard_map/all_to_all | solution.py:295
  13.8 0.2 group_sum.1
  14.1 0.7 %collective-permute-start = (f32[72,128]{1,0:T(8,128)S(1)}, f32[72,128]{1,0:T(8,128)S(1)}, u32[]{:S(2)}, u32[]{:S(2)}) collective-permute-start(f32[72,128]{1,0:T(8,128)S(1)} %get-tuple-element.12), channel_id=1, source_target_pairs={{0,1},{1,2},{2,0},{3,3},{4,5},{5,6},{6,4},{7,7},{8,9},{9,10},{10,8... | collective-permute-start | bytes 110600 | tf_op jit(solution)/shard_map/ppermute | solution.py:313
  14.7 0.7 %collective-permute-start.1 = (f32[72,128]{1,0:T(8,128)S(1)}, f32[72,128]{1,0:T(8,128)S(1)}, u32[]{:S(2)}, u32[]{:S(2)}) collective-permute-start(f32[72,128]{1,0:T(8,128)S(1)} %get-tuple-element.13), channel_id=1, source_target_pairs={{0,2},{1,0},{2,1},{3,3},{4,6},{5,4},{6,5},{7,7},{8,10},{9,8},{10,9... | collective-permute-start | bytes 110600 | tf_op jit(solution)/shard_map/ppermute | solution.py:313
  15.4 7.6 %collective-permute-start.2 = (f32[72,128]{1,0:T(8,128)S(1)}, f32[72,128]{1,0:T(8,128)S(1)}, u32[]{:S(2)}, u32[]{:S(2)}) collective-permute-start(f32[72,128]{1,0:T(8,128)S(1)} %get-tuple-element.14), channel_id=1, source_target_pairs={{0,3},{1,1},{2,2},{3,0},{4,7},{5,5},{6,6},{7,4},{8,11},{9,9},{10,1... | collective-permute-start | bytes 110600 | tf_op jit(solution)/shard_map/ppermute | solution.py:313
  23.0 1.9 %collective-permute-start.3 = (f32[72,128]{1,0:T(8,128)S(1)}, f32[72,128]{1,0:T(8,128)S(1)}, u32[]{:S(2)}, u32[]{:S(2)}) collective-permute-start(f32[72,128]{1,0:T(8,128)S(1)} %get-tuple-element.15), channel_id=1, source_target_pairs={{0,0},{1,3},{2,2},{3,1},{4,4},{5,7},{6,6},{7,5},{8,8},{9,11},{10,1... | collective-permute-start | bytes 110600 | tf_op jit(solution)/shard_map/ppermute | solution.py:313
  24.9 1.9 %collective-permute-start.4 = (f32[72,128]{1,0:T(8,128)S(1)}, f32[72,128]{1,0:T(8,128)S(1)}, u32[]{:S(2)}, u32[]{:S(2)}) collective-permute-start(f32[72,128]{1,0:T(8,128)S(1)} %get-tuple-element.16), channel_id=1, source_target_pairs={{0,0},{1,1},{2,3},{3,2},{4,4},{5,5},{6,7},{7,6},{8,8},{9,9},{10,11... | collective-permute-start | bytes 110600 | tf_op jit(solution)/shard_map/ppermute | solution.py:313
  26.8 0.0 copy-done.1
  26.9 0.1 cell_map.1.refs_6_
  27.0 0.0 collective-permute-done.refs_1_
  27.0 0.0 collective-permute-done.1.refs_2_
  27.0 0.0 collective-permute-done.2.refs_3_
  27.0 2.7 %collective-permute-done.3.refs_4_ = f32[72,128]{1,0:T(8,128)S(1)} collective-permute-done((f32[72,128]{1,0:T(8,128)S(1)}, f32[72,128]{1,0:T(8,128)S(1)}, u32[]{:S(2)}, u32[]{:S(2)}) %collective-permute-start.3) | collective-permute-done | bytes 36896 | tf_op jit(solution)/shard_map/ppermute | solution.py:313
  29.7 1.0 %collective-permute-done.4.refs_5_ = f32[72,128]{1,0:T(8,128)S(1)} collective-permute-done((f32[72,128]{1,0:T(8,128)S(1)}, f32[72,128]{1,0:T(8,128)S(1)}, u32[]{:S(2)}, u32[]{:S(2)}) %collective-permute-start.4) | collective-permute-done | bytes 36896 | tf_op jit(solution)/shard_map/ppermute | solution.py:313
  30.8 0.0 copy-done
  30.8 0.9 %cells.1 = f32[2,4096]{1,0:T(2,128)} custom-call(f32[72,128]{1,0:T(8,128)S(1)} %get-tuple-element.11.refs_0_, f32[72,128]{1,0:T(8,128)S(1)} %collective-permute-done.refs_1_, f32[72,128]{1,0:T(8,128)S(1)} %collective-permute-done.1.refs_2_, f32[72,128]{1,0:T(8,128)S(1)} %collective-permute-done.2.refs_3_, f32[72,128]{1,0:T(8,128)S(1)} %collective-permute-done.3.refs_4_, ...), custom_call_target="tpu_custom_call" | custom-call | tf_op jit(solution)/shard_map/cells/pallas_call | solution.py:325
Async XLA Ops:
  0.0 26.8 %copy-start.1 = (s32[2,256]{1,0:T(2,128)S(1)}, s32[2,256]{1,0:T(2,128)}, u32[]{:S(2)}) copy-start(s32[2,256]{1,0:T(2,128)} %cells_ref.1) | copy-start | bytes 6148
  0.0 30.8 %copy-start = (s32[2,256,8]{1,2,0:T(8,128)S(1)}, s32[2,256,8]{1,2,0:T(8,128)}, u32[]{:S(2)}) copy-start(s32[2,256,8]{1,2,0:T(8,128)} %param.17) | copy-start | bytes 49156
  14.1 12.9 %collective-permute-start = (f32[72,128]{1,0:T(8,128)S(1)}, f32[72,128]{1,0:T(8,128)S(1)}, u32[]{:S(2)}, u32[]{:S(2)}) collective-permute-start(f32[72,128]{1,0:T(8,128)S(1)} %get-tuple-element.12), channel_id=1, source_target_pairs={{0,1},{1,2},{2,0},{3,3},{4,5},{5,6},{6,4},{7,7},{8,9},{9,10},{10,8... | collective-permute-start | bytes 110600 | tf_op jit(solution)/shard_map/ppermute | solution.py:313
  14.7 12.3 %collective-permute-start.1 = (f32[72,128]{1,0:T(8,128)S(1)}, f32[72,128]{1,0:T(8,128)S(1)}, u32[]{:S(2)}, u32[]{:S(2)}) collective-permute-start(f32[72,128]{1,0:T(8,128)S(1)} %get-tuple-element.13), channel_id=1, source_target_pairs={{0,2},{1,0},{2,1},{3,3},{4,6},{5,4},{6,5},{7,7},{8,10},{9,8},{10,9... | collective-permute-start | bytes 110600 | tf_op jit(solution)/shard_map/ppermute | solution.py:313
  15.4 11.6 %collective-permute-start.2 = (f32[72,128]{1,0:T(8,128)S(1)}, f32[72,128]{1,0:T(8,128)S(1)}, u32[]{:S(2)}, u32[]{:S(2)}) collective-permute-start(f32[72,128]{1,0:T(8,128)S(1)} %get-tuple-element.14), channel_id=1, source_target_pairs={{0,3},{1,1},{2,2},{3,0},{4,7},{5,5},{6,6},{7,4},{8,11},{9,9},{10,1... | collective-permute-start | bytes 110600 | tf_op jit(solution)/shard_map/ppermute | solution.py:313
  23.0 6.8 %collective-permute-start.3 = (f32[72,128]{1,0:T(8,128)S(1)}, f32[72,128]{1,0:T(8,128)S(1)}, u32[]{:S(2)}, u32[]{:S(2)}) collective-permute-start(f32[72,128]{1,0:T(8,128)S(1)} %get-tuple-element.15), channel_id=1, source_target_pairs={{0,0},{1,3},{2,2},{3,1},{4,4},{5,7},{6,6},{7,5},{8,8},{9,11},{10,1... | collective-permute-start | bytes 110600 | tf_op jit(solution)/shard_map/ppermute | solution.py:313
  24.9 5.9 %collective-permute-start.4 = (f32[72,128]{1,0:T(8,128)S(1)}, f32[72,128]{1,0:T(8,128)S(1)}, u32[]{:S(2)}, u32[]{:S(2)}) collective-permute-start(f32[72,128]{1,0:T(8,128)S(1)} %get-tuple-element.16), channel_id=1, source_target_pairs={{0,0},{1,1},{2,3},{3,2},{4,4},{5,5},{6,7},{7,6},{8,8},{9,9},{10,11... | collective-permute-start | bytes 110600 | tf_op jit(solution)/shard_map/ppermute | solution.py:313

commit v15 on v14

--- a/solution.py
+++ b/solution.py
@@ -232,12 +232,24 @@
             out_ref[b : b + 1, row * LANES : (row + 1) * LANES] = result[row : row + 1, :]
 
 
-def moves_of(owners):
-    if owners == 4:
+def moves_of(rows, owners):
+    if owners == 4 and rows % 2 == 0:
         early = [(1, 2, 0, 3), (2, 0, 1, 3)]
         late = [(3, 1, 2, 0), (0, 3, 2, 1), (0, 1, 3, 2)]
         return early + late
     return [tuple((i + d) % owners for i in range(owners)) for d in range(1, owners)]
+
+
+def pairs_of(move, rows, cols):
+    owners = len(move)
+    pairs = []
+    for row in range(rows):
+        for col in range(cols):
+            for z, to in enumerate(move):
+                target = row ^ 1 if to == z else row
+                source = (row * cols + col) * owners + z
+                pairs.append((source, (target * cols + col) * owners + to))
+    return pairs
 
 
 def vmem():
@@ -299,7 +311,8 @@
         concat_axis=0,
         tiled=True,
     ).reshape(outgoing.shape)
-    moves = moves_of(owners)
+    rows, cols = lax.axis_size("row"), lax.axis_size("col")
+    moves = moves_of(rows, owners)
     partial = pl.pallas_call(
         functools.partial(group_kernel, items, bricks_dev, moves),
         out_shape=[jax.ShapeDtypeStruct((bricks_dev * ROWS + table_rows, LANES), jnp.float32)]
@@ -310,7 +323,7 @@
         name="group_sum",
     )(arrived)
     parts = [partial[0]] + [
-        lax.ppermute(piece, "basis", list(enumerate(move)))
+        lax.ppermute(piece, ("row", "col", "basis"), pairs_of(move, rows, cols))
         for piece, move in zip(partial[1:], moves)
     ]
     cell_map = pl.pallas_call(

time: 31.9 us -> 25.3 us (0.79)
  the two profiles are of different devices: /device:TPU:24 before, /device:TPU:0 now
where the time goes in v15:
time: 25.3 us; the launch traced here: 25.1 us
  blocking collectives  9.96 us (39%)
  Pallas kernels  6.57 us (26%)
  starting transfers between devices  4.65 us (18%)
  waiting for transfers between devices  3.94 us (16%)
    all_to_all x1, blocking collectives, body(): lax.all_to_all(outgoing.reshape(slots, 1, SLOT_ROWS * LANES), ('row', 'co...  9.96 us
    pallas_call x1, Pallas kernels, body(): pl.pallas_call(functools.partial(pair_kernel, slot_depth, bricks_group),...  5.29 us
    ppermute x5, starting transfers between devices, body(): lax.ppermute(piece, ('row', 'col', 'basis'), pairs_of(move, rows, cols))  4.65 us
    ppermute x5, waiting for transfers between devices, body(): lax.ppermute(piece, ('row', 'col', 'basis'), pairs_of(move, rows, cols))  3.94 us
    pallas_call x1, Pallas kernels, body(): pl.pallas_call(cell_kernel, out_shape=jax.ShapeDtypeStruct((bricks_dev, E...  0.88 us
  transfers between devices with their start and end apart: 5, of which 3 were waited for; matrix products, arithmetic and copies ran while one was open for 0% of the time, Pallas kernels for 1%

profile of v15, /device:TPU:0, one launch (start us, length us, event | category | flops | bytes accessed | tf_op | source)
XLA Modules:
  0.0 25.1 jit_solution(7013308755932761981)
XLA Ops:
  0.0 0.0 copy-start.1
  0.0 0.0 copy-start
  0.0 5.3 %pair_density.1 = f32[264,128]{1,0:T(8,128)S(1)} custom-call(s32[2,8]{1,0:T(2,128)} %bitcast.9, s32[8]{0:T(128)} %dest_hbm.1, s32[8]{0:T(128)} %tag_hbm.1, s32[64]{0:T(128)} %levels_hbm.1, bf16[8,128,128]{2,1,0:T(8,128)(2,1)} %blocks_hbm.1, f32[3,1024,128]{2,1,0:T(8,128)} %bitcast.8, f32[1024,128]{1,0:T(8,128)} %exponents_hbm.1), custom_call_target="tpu_custom_call" | custom-call | tf_op jit(solution)/shard_map/pair_density/pallas_call | solution.py:274
  5.3 10.0 %all_to_all.5 = f32[8,1,4224]{2,1,0:T(1,128)S(1)} all-to-all(f32[8,1,4224]{2,1,0:T(1,128)S(1)} %bitcast.5), channel_id=1, replica_groups=mesh['row'=4,'col'=2,'basis'=4] {'row','col'}, dimensions={0} | all-to-all | bytes 270336 | tf_op jit(solution)/shard_map/all_to_all | solution.py:307
  15.3 0.2 group_sum.1
  15.5 1.6 %collective-permute-start = (f32[72,128]{1,0:T(8,128)S(1)}, f32[72,128]{1,0:T(8,128)S(1)}, u32[]{:S(2)}, u32[]{:S(2)}) collective-permute-start(f32[72,128]{1,0:T(8,128)S(1)} %get-tuple-element.12), channel_id=1, source_target_pairs={{0,1},{1,2},{2,0},{3,11},{4,5},{5,6},{6,4},{7,15},{8,9},{9,10},{10... | collective-permute-start | bytes 110600 | tf_op jit(solution)/shard_map/ppermute | solution.py:326
  17.1 1.4 %collective-permute-start.1 = (f32[72,128]{1,0:T(8,128)S(1)}, f32[72,128]{1,0:T(8,128)S(1)}, u32[]{:S(2)}, u32[]{:S(2)}) collective-permute-start(f32[72,128]{1,0:T(8,128)S(1)} %get-tuple-element.13), channel_id=1, source_target_pairs={{0,2},{1,0},{2,1},{3,11},{4,6},{5,4},{6,5},{7,15},{8,10},{9,8},{10... | collective-permute-start | bytes 110600 | tf_op jit(solution)/shard_map/ppermute | solution.py:326
  18.5 1.2 %collective-permute-start.2 = (f32[72,128]{1,0:T(8,128)S(1)}, f32[72,128]{1,0:T(8,128)S(1)}, u32[]{:S(2)}, u32[]{:S(2)}) collective-permute-start(f32[72,128]{1,0:T(8,128)S(1)} %get-tuple-element.14), channel_id=1, source_target_pairs={{0,3},{1,9},{2,10},{3,0},{4,7},{5,13},{6,14},{7,4},{8,11},{9,1},{1... | collective-permute-start | bytes 110600 | tf_op jit(solution)/shard_map/ppermute | solution.py:326
  19.7 0.0 collective-permute-start.3
  19.7 0.5 %collective-permute-start.4 = (f32[72,128]{1,0:T(8,128)S(1)}, f32[72,128]{1,0:T(8,128)S(1)}, u32[]{:S(2)}, u32[]{:S(2)}) collective-permute-start(f32[72,128]{1,0:T(8,128)S(1)} %get-tuple-element.16), channel_id=1, source_target_pairs={{0,8},{1,9},{2,3},{3,2},{4,12},{5,13},{6,7},{7,6},{8,0},{9,1},{10,... | collective-permute-start | bytes 110600 | tf_op jit(solution)/shard_map/ppermute | solution.py:326
  20.2 0.0 copy-done.1
  20.2 0.1 cell_map.1.refs_6_
  20.3 0.1 collective-permute-done.refs_1_
  20.5 0.6 %collective-permute-done.1.refs_2_ = f32[72,128]{1,0:T(8,128)S(1)} collective-permute-done((f32[72,128]{1,0:T(8,128)S(1)}, f32[72,128]{1,0:T(8,128)S(1)}, u32[]{:S(2)}, u32[]{:S(2)}) %collective-permute-start.1) | collective-permute-done | bytes 36896 | tf_op jit(solution)/shard_map/ppermute | solution.py:326
  21.1 3.2 %collective-permute-done.2.refs_3_ = f32[72,128]{1,0:T(8,128)S(1)} collective-permute-done((f32[72,128]{1,0:T(8,128)S(1)}, f32[72,128]{1,0:T(8,128)S(1)}, u32[]{:S(2)}, u32[]{:S(2)}) %collective-permute-start.2) | collective-permute-done | bytes 36896 | tf_op jit(solution)/shard_map/ppermute | solution.py:326
  24.2 0.0 collective-permute-done.3.refs_4_
  24.3 0.0 collective-permute-done.4.refs_5_
  24.3 0.0 copy-done
  24.3 0.9 %cells.1 = f32[2,4096]{1,0:T(2,128)} custom-call(f32[72,128]{1,0:T(8,128)S(1)} %get-tuple-element.11.refs_0_, f32[72,128]{1,0:T(8,128)S(1)} %collective-permute-done.refs_1_, f32[72,128]{1,0:T(8,128)S(1)} %collective-permute-done.1.refs_2_, f32[72,128]{1,0:T(8,128)S(1)} %collective-permute-done.2.refs_3_, f32[72,128]{1,0:T(8,128)S(1)} %collective-permute-done.3.refs_4_, ...), custom_call_target="tpu_custom_call" | custom-call | tf_op jit(solution)/shard_map/cells/pallas_call | solution.py:338
Async XLA Ops:
  0.0 20.2 %copy-start.1 = (s32[2,256]{1,0:T(2,128)S(1)}, s32[2,256]{1,0:T(2,128)}, u32[]{:S(2)}) copy-start(s32[2,256]{1,0:T(2,128)} %cells_ref.1) | copy-start | bytes 6148
  0.0 24.3 %copy-start = (s32[2,256,8]{1,2,0:T(8,128)S(1)}, s32[2,256,8]{1,2,0:T(8,128)}, u32[]{:S(2)}) copy-start(s32[2,256,8]{1,2,0:T(8,128)} %param.17) | copy-start | bytes 49156
  15.5 5.0 %collective-permute-start = (f32[72,128]{1,0:T(8,128)S(1)}, f32[72,128]{1,0:T(8,128)S(1)}, u32[]{:S(2)}, u32[]{:S(2)}) collective-permute-start(f32[72,128]{1,0:T(8,128)S(1)} %get-tuple-element.12), channel_id=1, source_target_pairs={{0,1},{1,2},{2,0},{3,11},{4,5},{5,6},{6,4},{7,15},{8,9},{9,10},{10... | collective-permute-start | bytes 110600 | tf_op jit(solution)/shard_map/ppermute | solution.py:326
  17.1 4.0 %collective-permute-start.1 = (f32[72,128]{1,0:T(8,128)S(1)}, f32[72,128]{1,0:T(8,128)S(1)}, u32[]{:S(2)}, u32[]{:S(2)}) collective-permute-start(f32[72,128]{1,0:T(8,128)S(1)} %get-tuple-element.13), channel_id=1, source_target_pairs={{0,2},{1,0},{2,1},{3,11},{4,6},{5,4},{6,5},{7,15},{8,10},{9,8},{10... | collective-permute-start | bytes 110600 | tf_op jit(solution)/shard_map/ppermute | solution.py:326
  18.5 5.8 %collective-permute-start.2 = (f32[72,128]{1,0:T(8,128)S(1)}, f32[72,128]{1,0:T(8,128)S(1)}, u32[]{:S(2)}, u32[]{:S(2)}) collective-permute-start(f32[72,128]{1,0:T(8,128)S(1)} %get-tuple-element.14), channel_id=1, source_target_pairs={{0,3},{1,9},{2,10},{3,0},{4,7},{5,13},{6,14},{7,4},{8,11},{9,1},{1... | collective-permute-start | bytes 110600 | tf_op jit(solution)/shard_map/ppermute | solution.py:326
  19.7 4.6 %collective-permute-start.3 = (f32[72,128]{1,0:T(8,128)S(1)}, f32[72,128]{1,0:T(8,128)S(1)}, u32[]{:S(2)}, u32[]{:S(2)}) collective-permute-start(f32[72,128]{1,0:T(8,128)S(1)} %get-tuple-element.15), channel_id=1, source_target_pairs={{0,8},{1,3},{2,10},{3,1},{4,12},{5,7},{6,14},{7,5},{8,0},{9,11},{1... | collective-permute-start | bytes 110600 | tf_op jit(solution)/shard_map/ppermute | solution.py:326
  19.7 4.6 %collective-permute-start.4 = (f32[72,128]{1,0:T(8,128)S(1)}, f32[72,128]{1,0:T(8,128)S(1)}, u32[]{:S(2)}, u32[]{:S(2)}) collective-permute-start(f32[72,128]{1,0:T(8,128)S(1)} %get-tuple-element.16), channel_id=1, source_target_pairs={{0,8},{1,9},{2,3},{3,2},{4,12},{5,13},{6,7},{7,6},{8,0},{9,1},{10,... | collective-permute-start | bytes 110600 | tf_op jit(solution)/shard_map/ppermute | solution.py:326

commit v16 on v15

--- a/solution.py
+++ b/solution.py
@@ -68,12 +68,11 @@
         copy.start()
 
     tables = [
-        pltpu.make_async_copy(centres_hbm.at[d], centres_ref.at[d], table_sems.at[d])
-        for d in range(3)
+        pltpu.make_async_copy(exponents_hbm, exponents_ref, table_sems.at[0]),
+        pltpu.make_async_copy(centres_hbm, centres_ref, table_sems.at[1]),
     ]
-    tables.append(pltpu.make_async_copy(exponents_hbm, exponents_ref, table_sems.at[3]))
-    tables.append(pltpu.make_async_copy(blocks_hbm, blocks_ref, table_sems.at[4]))
-    for copy in tables:
+    blocks = pltpu.make_async_copy(blocks_hbm, blocks_ref, table_sems.at[2])
+    for copy in tables + [blocks]:
         copy.start()
     for copy in lists + tables:
         copy.wait()
@@ -98,6 +97,8 @@
         row_x, row_face = factors(0)
         col_x, col_face = factors(1)
         row_face = row_face.T
+        if k == 0:
+            blocks.wait()
         block = blocks_ref[k]
         for x in range(EDGE):
             col = (col_x[x : x + 1, :] * col_face).astype(jnp.bfloat16)
@@ -234,9 +235,7 @@
 
 def moves_of(rows, owners):
     if owners == 4 and rows % 2 == 0:
-        early = [(1, 2, 0, 3), (2, 0, 1, 3)]
-        late = [(3, 1, 2, 0), (0, 3, 2, 1), (0, 1, 3, 2)]
-        return early + late
+        return [(1, 3, 2, 0), (2, 1, 0, 3), (3, 0, 1, 2), (0, 2, 3, 1)]
     return [tuple((i + d) % owners for i in range(owners)) for d in range(1, owners)]
 
 
@@ -286,7 +285,7 @@
             pltpu.VMEM(exponents.shape, jnp.float32),
             pltpu.VMEM((4, items, LANES), jnp.float32),
             pltpu.SemaphoreType.DMA((4,)),
-            pltpu.SemaphoreType.DMA((5,)),
+            pltpu.SemaphoreType.DMA((3,)),
         ],
         compiler_params=params,
         name="pair_density",

time: 25.3 us -> 23.8 us (0.941)
  waiting for transfers between devices: 3.94 us -> 2.84 us
  starting transfers between devices: 4.65 us -> 4.12 us
    ppermute x5 -> x4, waiting for transfers between devices: 3.94 us -> 2.84 us  [body(): lax.ppermute(piece, ('row', 'col', 'basis'), pairs_of(move, rows, cols))]
    ppermute x5 -> x4, starting transfers between devices: 4.65 us -> 4.12 us  [body(): lax.ppermute(piece, ('row', 'col', 'basis'), pairs_of(move, rows, cols))]
  transfers between devices with their start and end apart: 5 -> 4, of which waited for: 3 -> 3; matrix products, arithmetic and copies ran while one was open for 0% -> 0% of each run, Pallas kernels for 1% -> 1%
where the time goes in v16:
time: 23.8 us; the launch traced here: 23.6 us
  blocking collectives  9.94 us (42%)
  Pallas kernels  6.69 us (28%)
  starting transfers between devices  4.12 us (17%)
  waiting for transfers between devices  2.84 us (12%)
    all_to_all x1, blocking collectives, body(): lax.all_to_all(outgoing.reshape(slots, 1, SLOT_ROWS * LANES), ('row', 'co...  9.94 us
    pallas_call x1, Pallas kernels, body(): pl.pallas_call(functools.partial(pair_kernel, slot_depth, bricks_group),...  5.44 us
    ppermute x4, starting transfers between devices, body(): lax.ppermute(piece, ('row', 'col', 'basis'), pairs_of(move, rows, cols))  4.12 us
    ppermute x4, waiting for transfers between devices, body(): lax.ppermute(piece, ('row', 'col', 'basis'), pairs_of(move, rows, cols))  2.84 us
    pallas_call x1, Pallas kernels, body(): pl.pallas_call(cell_kernel, out_shape=jax.ShapeDtypeStruct((bricks_dev, E...  0.88 us
  transfers between devices with their start and end apart: 4, of which 3 were waited for; matrix products, arithmetic and copies ran while one was open for 0% of the time, Pallas kernels for 1%

profile of v16, /device:TPU:0, one launch (start us, length us, event | category | flops | bytes accessed | tf_op | source)
XLA Modules:
  0.0 23.6 jit_solution(5386398824121430660)
XLA Ops:
  0.0 0.0 copy-start.1
  0.0 0.0 copy-start
  0.0 5.4 %pair_density.1 = f32[264,128]{1,0:T(8,128)S(1)} custom-call(s32[2,8]{1,0:T(2,128)} %bitcast.9, s32[8]{0:T(128)} %dest_hbm.1, s32[8]{0:T(128)} %tag_hbm.1, s32[64]{0:T(128)} %levels_hbm.1, bf16[8,128,128]{2,1,0:T(8,128)(2,1)} %blocks_hbm.1, f32[3,1024,128]{2,1,0:T(8,128)} %bitcast.8, f32[1024,128]{1,0:T(8,128)} %exponents_hbm.1), custom_call_target="tpu_custom_call" | custom-call | tf_op jit(solution)/shard_map/pair_density/pallas_call | solution.py:273
  5.5 9.9 %all_to_all.5 = f32[8,1,4224]{2,1,0:T(1,128)S(1)} all-to-all(f32[8,1,4224]{2,1,0:T(1,128)S(1)} %bitcast.5), channel_id=1, replica_groups=mesh['row'=4,'col'=2,'basis'=4] {'row','col'}, dimensions={0} | all-to-all | bytes 270336 | tf_op jit(solution)/shard_map/all_to_all | solution.py:306
  15.4 0.2 group_sum.1
  15.6 1.6 %collective-permute-start = (f32[72,128]{1,0:T(8,128)S(1)}, f32[72,128]{1,0:T(8,128)S(1)}, u32[]{:S(2)}, u32[]{:S(2)}) collective-permute-start(f32[72,128]{1,0:T(8,128)S(1)} %get-tuple-element.11), channel_id=1, source_target_pairs={{0,1},{1,3},{2,10},{3,0},{4,5},{5,7},{6,14},{7,4},{8,9},{9,11},{10... | collective-permute-start | bytes 110600 | tf_op jit(solution)/shard_map/ppermute | solution.py:325
  17.3 1.3 %collective-permute-start.1 = (f32[72,128]{1,0:T(8,128)S(1)}, f32[72,128]{1,0:T(8,128)S(1)}, u32[]{:S(2)}, u32[]{:S(2)}) collective-permute-start(f32[72,128]{1,0:T(8,128)S(1)} %get-tuple-element.12), channel_id=1, source_target_pairs={{0,2},{1,9},{2,0},{3,11},{4,6},{5,13},{6,4},{7,15},{8,10},{9,1},{1... | collective-permute-start | bytes 110600 | tf_op jit(solution)/shard_map/ppermute | solution.py:325
  18.5 1.1 %collective-permute-start.2 = (f32[72,128]{1,0:T(8,128)S(1)}, f32[72,128]{1,0:T(8,128)S(1)}, u32[]{:S(2)}, u32[]{:S(2)}) collective-permute-start(f32[72,128]{1,0:T(8,128)S(1)} %get-tuple-element.13), channel_id=1, source_target_pairs={{0,3},{1,0},{2,1},{3,2},{4,7},{5,4},{6,5},{7,6},{8,11},{9,8},{10,9... | collective-permute-start | bytes 110600 | tf_op jit(solution)/shard_map/ppermute | solution.py:325
  19.6 0.2 collective-permute-start.3
  19.7 0.0 copy-done.1
  19.7 0.1 cell_map.1.refs_5_
  19.9 1.6 %collective-permute-done.refs_1_ = f32[72,128]{1,0:T(8,128)S(1)} collective-permute-done((f32[72,128]{1,0:T(8,128)S(1)}, f32[72,128]{1,0:T(8,128)S(1)}, u32[]{:S(2)}, u32[]{:S(2)}) %collective-permute-start) | collective-permute-done | bytes 36896 | tf_op jit(solution)/shard_map/ppermute | solution.py:325
  21.5 0.7 %collective-permute-done.1.refs_2_ = f32[72,128]{1,0:T(8,128)S(1)} collective-permute-done((f32[72,128]{1,0:T(8,128)S(1)}, f32[72,128]{1,0:T(8,128)S(1)}, u32[]{:S(2)}, u32[]{:S(2)}) %collective-permute-start.1) | collective-permute-done | bytes 36896 | tf_op jit(solution)/shard_map/ppermute | solution.py:325
  22.2 0.6 %collective-permute-done.2.refs_3_ = f32[72,128]{1,0:T(8,128)S(1)} collective-permute-done((f32[72,128]{1,0:T(8,128)S(1)}, f32[72,128]{1,0:T(8,128)S(1)}, u32[]{:S(2)}, u32[]{:S(2)}) %collective-permute-start.2) | collective-permute-done | bytes 36896 | tf_op jit(solution)/shard_map/ppermute | solution.py:325
  22.7 0.0 collective-permute-done.3.refs_4_
  22.7 0.0 copy-done
  22.7 0.9 %cells.1 = f32[2,4096]{1,0:T(2,128)} custom-call(f32[72,128]{1,0:T(8,128)S(1)} %get-tuple-element.10.refs_0_, f32[72,128]{1,0:T(8,128)S(1)} %collective-permute-done.refs_1_, f32[72,128]{1,0:T(8,128)S(1)} %collective-permute-done.1.refs_2_, f32[72,128]{1,0:T(8,128)S(1)} %collective-permute-done.2.refs_3_, f32[72,128]{1,0:T(8,128)S(1)} %collective-permute-done.3.refs_4_, ...), custom_call_target="tpu_custom_call" | custom-call | tf_op jit(solution)/shard_map/cells/pallas_call | solution.py:337
Async XLA Ops:
  0.0 19.7 %copy-start.1 = (s32[2,256]{1,0:T(2,128)S(1)}, s32[2,256]{1,0:T(2,128)}, u32[]{:S(2)}) copy-start(s32[2,256]{1,0:T(2,128)} %cells_ref.1) | copy-start | bytes 6148
  0.0 22.7 %copy-start = (s32[2,256,8]{1,2,0:T(8,128)S(1)}, s32[2,256,8]{1,2,0:T(8,128)}, u32[]{:S(2)}) copy-start(s32[2,256,8]{1,2,0:T(8,128)} %param.17) | copy-start | bytes 49156
  15.6 5.8 %collective-permute-start = (f32[72,128]{1,0:T(8,128)S(1)}, f32[72,128]{1,0:T(8,128)S(1)}, u32[]{:S(2)}, u32[]{:S(2)}) collective-permute-start(f32[72,128]{1,0:T(8,128)S(1)} %get-tuple-element.11), channel_id=1, source_target_pairs={{0,1},{1,3},{2,10},{3,0},{4,5},{5,7},{6,14},{7,4},{8,9},{9,11},{10... | collective-permute-start | bytes 110600 | tf_op jit(solution)/shard_map/ppermute | solution.py:325
  17.3 4.9 %collective-permute-start.1 = (f32[72,128]{1,0:T(8,128)S(1)}, f32[72,128]{1,0:T(8,128)S(1)}, u32[]{:S(2)}, u32[]{:S(2)}) collective-permute-start(f32[72,128]{1,0:T(8,128)S(1)} %get-tuple-element.12), channel_id=1, source_target_pairs={{0,2},{1,9},{2,0},{3,11},{4,6},{5,13},{6,4},{7,15},{8,10},{9,1},{1... | collective-permute-start | bytes 110600 | tf_op jit(solution)/shard_map/ppermute | solution.py:325
  18.5 4.2 %collective-permute-start.2 = (f32[72,128]{1,0:T(8,128)S(1)}, f32[72,128]{1,0:T(8,128)S(1)}, u32[]{:S(2)}, u32[]{:S(2)}) collective-permute-start(f32[72,128]{1,0:T(8,128)S(1)} %get-tuple-element.13), channel_id=1, source_target_pairs={{0,3},{1,0},{2,1},{3,2},{4,7},{5,4},{6,5},{7,6},{8,11},{9,8},{10,9... | collective-permute-start | bytes 110600 | tf_op jit(solution)/shard_map/ppermute | solution.py:325
  19.6 3.1 %collective-permute-start.3 = (f32[72,128]{1,0:T(8,128)S(1)}, f32[72,128]{1,0:T(8,128)S(1)}, u32[]{:S(2)}, u32[]{:S(2)}) collective-permute-start(f32[72,128]{1,0:T(8,128)S(1)} %get-tuple-element.14), channel_id=1, source_target_pairs={{0,8},{1,2},{2,3},{3,1},{4,12},{5,6},{6,7},{7,5},{8,0},{9,10},{10,... | collective-permute-start | bytes 110600 | tf_op jit(solution)/shard_map/ppermute | solution.py:325

commit v17 on v15

--- a/solution.py
+++ b/solution.py
@@ -234,9 +234,7 @@
 
 def moves_of(rows, owners):
     if owners == 4 and rows % 2 == 0:
-        early = [(1, 2, 0, 3), (2, 0, 1, 3)]
-        late = [(3, 1, 2, 0), (0, 3, 2, 1), (0, 1, 3, 2)]
-        return early + late
+        return [(1, 3, 2, 0), (2, 1, 0, 3), (3, 0, 1, 2), (0, 2, 3, 1)]
     return [tuple((i + d) % owners for i in range(owners)) for d in range(1, owners)]
 
 
@@ -267,7 +265,7 @@
     bricks = levels.shape[0]
     bricks_group = bricks // groups
     bricks_dev = bricks_group // owners
-    table_rows = -(-bricks * 8 // (8 * LANES)) * 8
+    table_rows = -(-bricks * 8 // LANES)
     basis = block_data.shape[1]
     params = pltpu.CompilerParams(vmem_limit_bytes=32 * 1024 * 1024)
 

time: 25.3 us -> 23.6 us (0.933)
  waiting for transfers between devices: 3.94 us -> 2.83 us
  starting transfers between devices: 4.65 us -> 4.11 us
    ppermute x5 -> x4, waiting for transfers between devices: 3.94 us -> 2.83 us  [body(): lax.ppermute(piece, ('row', 'col', 'basis'), pairs_of(move, rows, cols))]
    ppermute x5 -> x4, starting transfers between devices: 4.65 us -> 4.11 us  [body(): lax.ppermute(piece, ('row', 'col', 'basis'), pairs_of(move, rows, cols))]
  transfers between devices with their start and end apart: 5 -> 4, of which waited for: 3 -> 3; matrix products, arithmetic and copies ran while one was open for 0% -> 0% of each run, Pallas kernels for 1% -> 1%
where the time goes in v17:
time: 23.6 us; the launch traced here: 23.4 us
  blocking collectives  9.97 us (42%)
  Pallas kernels  6.5 us (28%)
  starting transfers between devices  4.11 us (17%)
  waiting for transfers between devices  2.83 us (12%)
    all_to_all x1, blocking collectives, body(): lax.all_to_all(outgoing.reshape(slots, 1, SLOT_ROWS * LANES), ('row', 'co...  9.97 us
    pallas_call x1, Pallas kernels, body(): pl.pallas_call(functools.partial(pair_kernel, slot_depth, bricks_group),...  5.29 us
    ppermute x4, starting transfers between devices, body(): lax.ppermute(piece, ('row', 'col', 'basis'), pairs_of(move, rows, cols))  4.11 us
    ppermute x4, waiting for transfers between devices, body(): lax.ppermute(piece, ('row', 'col', 'basis'), pairs_of(move, rows, cols))  2.83 us
    pallas_call x1, Pallas kernels, body(): pl.pallas_call(cell_kernel, out_shape=jax.ShapeDtypeStruct((bricks_dev, E...  0.84 us
  transfers between devices with their start and end apart: 4, of which 3 were waited for; matrix products, arithmetic and copies ran while one was open for 0% of the time, Pallas kernels for 1%

profile of v17, /device:TPU:0, one launch (start us, length us, event | category | flops | bytes accessed | tf_op | source)
XLA Modules:
  0.0 23.4 jit_solution(10236463928768928421)
XLA Ops:
  0.0 0.0 copy-start.1
  0.0 0.0 copy-start
  0.0 5.3 %pair_density.1 = f32[264,128]{1,0:T(8,128)S(1)} custom-call(s32[2,8]{1,0:T(2,128)} %bitcast.9, s32[8]{0:T(128)} %dest_hbm.1, s32[8]{0:T(128)} %tag_hbm.1, s32[64]{0:T(128)} %levels_hbm.1, bf16[8,128,128]{2,1,0:T(8,128)(2,1)} %blocks_hbm.1, f32[3,1024,128]{2,1,0:T(8,128)} %bitcast.8, f32[1024,128]{1,0:T(8,128)} %exponents_hbm.1), custom_call_target="tpu_custom_call" | custom-call | tf_op jit(solution)/shard_map/pair_density/pallas_call | solution.py:272
  5.3 10.0 %all_to_all.5 = f32[8,1,4224]{2,1,0:T(1,128)S(1)} all-to-all(f32[8,1,4224]{2,1,0:T(1,128)S(1)} %bitcast.5), channel_id=1, replica_groups=mesh['row'=4,'col'=2,'basis'=4] {'row','col'}, dimensions={0} | all-to-all | bytes 270336 | tf_op jit(solution)/shard_map/all_to_all | solution.py:305
  15.3 0.2 group_sum.1
  15.5 1.6 %collective-permute-start = (f32[68,128]{1,0:T(8,128)S(1)}, f32[68,128]{1,0:T(8,128)S(1)}, u32[]{:S(2)}, u32[]{:S(2)}) collective-permute-start(f32[68,128]{1,0:T(8,128)S(1)} %get-tuple-element.11), channel_id=1, source_target_pairs={{0,1},{1,3},{2,10},{3,0},{4,5},{5,7},{6,14},{7,4},{8,9},{9,11},{10... | collective-permute-start | bytes 104456 | tf_op jit(solution)/shard_map/ppermute | solution.py:324
  17.1 1.3 %collective-permute-start.1 = (f32[68,128]{1,0:T(8,128)S(1)}, f32[68,128]{1,0:T(8,128)S(1)}, u32[]{:S(2)}, u32[]{:S(2)}) collective-permute-start(f32[68,128]{1,0:T(8,128)S(1)} %get-tuple-element.12), channel_id=1, source_target_pairs={{0,2},{1,9},{2,0},{3,11},{4,6},{5,13},{6,4},{7,15},{8,10},{9,1},{1... | collective-permute-start | bytes 104456 | tf_op jit(solution)/shard_map/ppermute | solution.py:324
  18.3 1.1 %collective-permute-start.2 = (f32[68,128]{1,0:T(8,128)S(1)}, f32[68,128]{1,0:T(8,128)S(1)}, u32[]{:S(2)}, u32[]{:S(2)}) collective-permute-start(f32[68,128]{1,0:T(8,128)S(1)} %get-tuple-element.13), channel_id=1, source_target_pairs={{0,3},{1,0},{2,1},{3,2},{4,7},{5,4},{6,5},{7,6},{8,11},{9,8},{10,9... | collective-permute-start | bytes 104456 | tf_op jit(solution)/shard_map/ppermute | solution.py:324
  19.4 0.2 collective-permute-start.3
  19.6 0.0 copy-done.1
  19.6 0.1 cell_map.1.refs_5_
  19.8 1.6 %collective-permute-done.refs_1_ = f32[68,128]{1,0:T(8,128)S(1)} collective-permute-done((f32[68,128]{1,0:T(8,128)S(1)}, f32[68,128]{1,0:T(8,128)S(1)}, u32[]{:S(2)}, u32[]{:S(2)}) %collective-permute-start) | collective-permute-done | bytes 34848 | tf_op jit(solution)/shard_map/ppermute | solution.py:324
  21.3 0.6 %collective-permute-done.1.refs_2_ = f32[68,128]{1,0:T(8,128)S(1)} collective-permute-done((f32[68,128]{1,0:T(8,128)S(1)}, f32[68,128]{1,0:T(8,128)S(1)}, u32[]{:S(2)}, u32[]{:S(2)}) %collective-permute-start.1) | collective-permute-done | bytes 34848 | tf_op jit(solution)/shard_map/ppermute | solution.py:324
  22.0 0.6 %collective-permute-done.2.refs_3_ = f32[68,128]{1,0:T(8,128)S(1)} collective-permute-done((f32[68,128]{1,0:T(8,128)S(1)}, f32[68,128]{1,0:T(8,128)S(1)}, u32[]{:S(2)}, u32[]{:S(2)}) %collective-permute-start.2) | collective-permute-done | bytes 34848 | tf_op jit(solution)/shard_map/ppermute | solution.py:324
  22.6 0.0 collective-permute-done.3.refs_4_
  22.6 0.0 copy-done
  22.6 0.8 %cells.1 = f32[2,4096]{1,0:T(2,128)} custom-call(f32[68,128]{1,0:T(8,128)S(1)} %get-tuple-element.10.refs_0_, f32[68,128]{1,0:T(8,128)S(1)} %collective-permute-done.refs_1_, f32[68,128]{1,0:T(8,128)S(1)} %collective-permute-done.1.refs_2_, f32[68,128]{1,0:T(8,128)S(1)} %collective-permute-done.2.refs_3_, f32[68,128]{1,0:T(8,128)S(1)} %collective-permute-done.3.refs_4_, ...), custom_call_target="tpu_custom_call" | custom-call | tf_op jit(solution)/shard_map/cells/pallas_call | solution.py:336
Async XLA Ops:
  0.0 19.6 %copy-start.1 = (s32[2,256]{1,0:T(2,128)S(1)}, s32[2,256]{1,0:T(2,128)}, u32[]{:S(2)}) copy-start(s32[2,256]{1,0:T(2,128)} %cells_ref.1) | copy-start | bytes 6148
  0.0 22.6 %copy-start = (s32[2,256,8]{1,2,0:T(8,128)S(1)}, s32[2,256,8]{1,2,0:T(8,128)}, u32[]{:S(2)}) copy-start(s32[2,256,8]{1,2,0:T(8,128)} %param.17) | copy-start | bytes 49156
  15.5 5.8 %collective-permute-start = (f32[68,128]{1,0:T(8,128)S(1)}, f32[68,128]{1,0:T(8,128)S(1)}, u32[]{:S(2)}, u32[]{:S(2)}) collective-permute-start(f32[68,128]{1,0:T(8,128)S(1)} %get-tuple-element.11), channel_id=1, source_target_pairs={{0,1},{1,3},{2,10},{3,0},{4,5},{5,7},{6,14},{7,4},{8,9},{9,11},{10... | collective-permute-start | bytes 104456 | tf_op jit(solution)/shard_map/ppermute | solution.py:324
  17.1 4.9 %collective-permute-start.1 = (f32[68,128]{1,0:T(8,128)S(1)}, f32[68,128]{1,0:T(8,128)S(1)}, u32[]{:S(2)}, u32[]{:S(2)}) collective-permute-start(f32[68,128]{1,0:T(8,128)S(1)} %get-tuple-element.12), channel_id=1, source_target_pairs={{0,2},{1,9},{2,0},{3,11},{4,6},{5,13},{6,4},{7,15},{8,10},{9,1},{1... | collective-permute-start | bytes 104456 | tf_op jit(solution)/shard_map/ppermute | solution.py:324
  18.3 4.2 %collective-permute-start.2 = (f32[68,128]{1,0:T(8,128)S(1)}, f32[68,128]{1,0:T(8,128)S(1)}, u32[]{:S(2)}, u32[]{:S(2)}) collective-permute-start(f32[68,128]{1,0:T(8,128)S(1)} %get-tuple-element.13), channel_id=1, source_target_pairs={{0,3},{1,0},{2,1},{3,2},{4,7},{5,4},{6,5},{7,6},{8,11},{9,8},{10,9... | collective-permute-start | bytes 104456 | tf_op jit(solution)/shard_map/ppermute | solution.py:324
  19.4 3.1 %collective-permute-start.3 = (f32[68,128]{1,0:T(8,128)S(1)}, f32[68,128]{1,0:T(8,128)S(1)}, u32[]{:S(2)}, u32[]{:S(2)}) collective-permute-start(f32[68,128]{1,0:T(8,128)S(1)} %get-tuple-element.14), channel_id=1, source_target_pairs={{0,8},{1,2},{2,3},{3,1},{4,12},{5,6},{6,7},{7,5},{8,0},{9,10},{10,... | collective-permute-start | bytes 104456 | tf_op jit(solution)/shard_map/ppermute | solution.py:324

commit v18 on v17

--- a/solution.py
+++ b/solution.py
@@ -68,15 +68,22 @@
         copy.start()
 
     tables = [
-        pltpu.make_async_copy(centres_hbm.at[d], centres_ref.at[d], table_sems.at[d])
-        for d in range(3)
+        pltpu.make_async_copy(exponents_hbm, exponents_ref, table_sems.at[0]),
+        pltpu.make_async_copy(blocks_hbm, blocks_ref, table_sems.at[1]),
     ]
-    tables.append(pltpu.make_async_copy(exponents_hbm, exponents_ref, table_sems.at[3]))
-    tables.append(pltpu.make_async_copy(blocks_hbm, blocks_ref, table_sems.at[4]))
     for copy in tables:
         copy.start()
-    for copy in lists + tables:
+    lists[0].wait()
+    for k in range(items):
+        for side in range(2):
+            pltpu.make_async_copy(
+                centres_hbm.at[:, pl.ds(pairs_ref[side, k], 1), :],
+                centres_ref.at[2 * k + side],
+                table_sems.at[2],
+            ).start()
+    for copy in lists[1:] + tables:
         copy.wait()
+    pltpu.make_async_copy(centres_ref, centres_ref, table_sems.at[2]).wait()
     if slots != items:
         out_ref[...] = jnp.zeros_like(out_ref)
     steps = iota((EDGE, LANES), 0).astype(jnp.float32) - (EDGE - 1) / 2.0
@@ -89,7 +96,7 @@
         def factors(side):
             row = pl.ds(pairs_ref[side, k], 1)
             decay = exponents_ref[row, :]
-            found = [axis_factors(coords, centres_ref[d, row, :], decay) for d in range(3)]
+            found = [axis_factors(coords, centres_ref[2 * k + side, d], decay) for d in range(3)]
             face = jnp.concatenate(
                 [found[1][y : y + 1, :] * found[2] for y in range(EDGE)], axis=0
             )
@@ -280,11 +287,11 @@
             pltpu.SMEM((items,), jnp.int32),
             pltpu.SMEM((bricks,), jnp.int32),
             pltpu.VMEM(block_data.shape, block_data.dtype),
-            pltpu.VMEM((3, centres.shape[0], basis), jnp.float32),
+            pltpu.VMEM((2 * items, 3, 1, basis), jnp.float32),
             pltpu.VMEM(exponents.shape, jnp.float32),
             pltpu.VMEM((4, items, LANES), jnp.float32),
             pltpu.SemaphoreType.DMA((4,)),
-            pltpu.SemaphoreType.DMA((5,)),
+            pltpu.SemaphoreType.DMA((3,)),
         ],
         compiler_params=params,
         name="pair_density",

time: 23.6 us -> 23.7 us (level)
  no operation moved by 1% of the time
where the time goes in v18:
time: 23.7 us; the launch traced here: 23.5 us
  blocking collectives  9.93 us (42%)
  Pallas kernels  6.61 us (28%)
  starting transfers between devices  4.13 us (17%)
  waiting for transfers between devices  2.84 us (12%)
    all_to_all x1, blocking collectives, body(): lax.all_to_all(outgoing.reshape(slots, 1, SLOT_ROWS * LANES), ('row', 'co...  9.93 us
    pallas_call x1, Pallas kernels, body(): pl.pallas_call(functools.partial(pair_kernel, slot_depth, bricks_group),...  5.4 us
    ppermute x4, starting transfers between devices, body(): lax.ppermute(piece, ('row', 'col', 'basis'), pairs_of(move, rows, cols))  4.13 us
    ppermute x4, waiting for transfers between devices, body(): lax.ppermute(piece, ('row', 'col', 'basis'), pairs_of(move, rows, cols))  2.84 us
    pallas_call x1, Pallas kernels, body(): pl.pallas_call(cell_kernel, out_shape=jax.ShapeDtypeStruct((bricks_dev, E...  0.84 us
  transfers between devices with their start and end apart: 4, of which 3 were waited for; matrix products, arithmetic and copies ran while one was open for 0% of the time, Pallas kernels for 1%

profile of v18, /device:TPU:0, one launch (start us, length us, event | category | flops | bytes accessed | tf_op | source)
XLA Modules:
  0.0 23.5 jit_solution(8850343131302162504)
XLA Ops:
  0.0 0.0 copy-start.1
  0.0 0.0 copy-start
  0.0 5.4 %pair_density.1 = f32[264,128]{1,0:T(8,128)S(1)} custom-call(s32[2,8]{1,0:T(2,128)} %bitcast.9, s32[8]{0:T(128)} %dest_hbm.1, s32[8]{0:T(128)} %tag_hbm.1, s32[64]{0:T(128)} %levels_hbm.1, bf16[8,128,128]{2,1,0:T(8,128)(2,1)} %blocks_hbm.1, f32[3,1024,128]{2,1,0:T(8,128)} %bitcast.8, f32[1024,128]{1,0:T(8,128)} %exponents_hbm.1), custom_call_target="tpu_custom_call" | custom-call | tf_op jit(solution)/shard_map/pair_density/pallas_call | solution.py:279
  5.4 9.9 %all_to_all.5 = f32[8,1,4224]{2,1,0:T(1,128)S(1)} all-to-all(f32[8,1,4224]{2,1,0:T(1,128)S(1)} %bitcast.5), channel_id=1, replica_groups=mesh['row'=4,'col'=2,'basis'=4] {'row','col'}, dimensions={0} | all-to-all | bytes 270336 | tf_op jit(solution)/shard_map/all_to_all | solution.py:312
  15.3 0.2 group_sum.1
  15.6 1.6 %collective-permute-start = (f32[68,128]{1,0:T(8,128)S(1)}, f32[68,128]{1,0:T(8,128)S(1)}, u32[]{:S(2)}, u32[]{:S(2)}) collective-permute-start(f32[68,128]{1,0:T(8,128)S(1)} %get-tuple-element.11), channel_id=1, source_target_pairs={{0,1},{1,3},{2,10},{3,0},{4,5},{5,7},{6,14},{7,4},{8,9},{9,11},{10... | collective-permute-start | bytes 104456 | tf_op jit(solution)/shard_map/ppermute | solution.py:331
  17.2 1.3 %collective-permute-start.1 = (f32[68,128]{1,0:T(8,128)S(1)}, f32[68,128]{1,0:T(8,128)S(1)}, u32[]{:S(2)}, u32[]{:S(2)}) collective-permute-start(f32[68,128]{1,0:T(8,128)S(1)} %get-tuple-element.12), channel_id=1, source_target_pairs={{0,2},{1,9},{2,0},{3,11},{4,6},{5,13},{6,4},{7,15},{8,10},{9,1},{1... | collective-permute-start | bytes 104456 | tf_op jit(solution)/shard_map/ppermute | solution.py:331
  18.5 1.1 %collective-permute-start.2 = (f32[68,128]{1,0:T(8,128)S(1)}, f32[68,128]{1,0:T(8,128)S(1)}, u32[]{:S(2)}, u32[]{:S(2)}) collective-permute-start(f32[68,128]{1,0:T(8,128)S(1)} %get-tuple-element.13), channel_id=1, source_target_pairs={{0,3},{1,0},{2,1},{3,2},{4,7},{5,4},{6,5},{7,6},{8,11},{9,8},{10,9... | collective-permute-start | bytes 104456 | tf_op jit(solution)/shard_map/ppermute | solution.py:331
  19.5 0.1 collective-permute-start.3
  19.7 0.0 copy-done.1
  19.7 0.1 cell_map.1.refs_5_
  19.8 1.5 %collective-permute-done.refs_1_ = f32[68,128]{1,0:T(8,128)S(1)} collective-permute-done((f32[68,128]{1,0:T(8,128)S(1)}, f32[68,128]{1,0:T(8,128)S(1)}, u32[]{:S(2)}, u32[]{:S(2)}) %collective-permute-start) | collective-permute-done | bytes 34848 | tf_op jit(solution)/shard_map/ppermute | solution.py:331
  21.4 0.7 %collective-permute-done.1.refs_2_ = f32[68,128]{1,0:T(8,128)S(1)} collective-permute-done((f32[68,128]{1,0:T(8,128)S(1)}, f32[68,128]{1,0:T(8,128)S(1)}, u32[]{:S(2)}, u32[]{:S(2)}) %collective-permute-start.1) | collective-permute-done | bytes 34848 | tf_op jit(solution)/shard_map/ppermute | solution.py:331
  22.1 0.6 %collective-permute-done.2.refs_3_ = f32[68,128]{1,0:T(8,128)S(1)} collective-permute-done((f32[68,128]{1,0:T(8,128)S(1)}, f32[68,128]{1,0:T(8,128)S(1)}, u32[]{:S(2)}, u32[]{:S(2)}) %collective-permute-start.2) | collective-permute-done | bytes 34848 | tf_op jit(solution)/shard_map/ppermute | solution.py:331
  22.7 0.0 collective-permute-done.3.refs_4_
  22.7 0.0 copy-done
  22.7 0.8 %cells.1 = f32[2,4096]{1,0:T(2,128)} custom-call(f32[68,128]{1,0:T(8,128)S(1)} %get-tuple-element.10.refs_0_, f32[68,128]{1,0:T(8,128)S(1)} %collective-permute-done.refs_1_, f32[68,128]{1,0:T(8,128)S(1)} %collective-permute-done.1.refs_2_, f32[68,128]{1,0:T(8,128)S(1)} %collective-permute-done.2.refs_3_, f32[68,128]{1,0:T(8,128)S(1)} %collective-permute-done.3.refs_4_, ...), custom_call_target="tpu_custom_call" | custom-call | tf_op jit(solution)/shard_map/cells/pallas_call | solution.py:343
Async XLA Ops:
  0.0 19.7 %copy-start.1 = (s32[2,256]{1,0:T(2,128)S(1)}, s32[2,256]{1,0:T(2,128)}, u32[]{:S(2)}) copy-start(s32[2,256]{1,0:T(2,128)} %cells_ref.1) | copy-start | bytes 6148
  0.0 22.7 %copy-start = (s32[2,256,8]{1,2,0:T(8,128)S(1)}, s32[2,256,8]{1,2,0:T(8,128)}, u32[]{:S(2)}) copy-start(s32[2,256,8]{1,2,0:T(8,128)} %param.17) | copy-start | bytes 49156
  15.6 5.8 %collective-permute-start = (f32[68,128]{1,0:T(8,128)S(1)}, f32[68,128]{1,0:T(8,128)S(1)}, u32[]{:S(2)}, u32[]{:S(2)}) collective-permute-start(f32[68,128]{1,0:T(8,128)S(1)} %get-tuple-element.11), channel_id=1, source_target_pairs={{0,1},{1,3},{2,10},{3,0},{4,5},{5,7},{6,14},{7,4},{8,9},{9,11},{10... | collective-permute-start | bytes 104456 | tf_op jit(solution)/shard_map/ppermute | solution.py:331
  17.2 4.9 %collective-permute-start.1 = (f32[68,128]{1,0:T(8,128)S(1)}, f32[68,128]{1,0:T(8,128)S(1)}, u32[]{:S(2)}, u32[]{:S(2)}) collective-permute-start(f32[68,128]{1,0:T(8,128)S(1)} %get-tuple-element.12), channel_id=1, source_target_pairs={{0,2},{1,9},{2,0},{3,11},{4,6},{5,13},{6,4},{7,15},{8,10},{9,1},{1... | collective-permute-start | bytes 104456 | tf_op jit(solution)/shard_map/ppermute | solution.py:331
  18.5 4.2 %collective-permute-start.2 = (f32[68,128]{1,0:T(8,128)S(1)}, f32[68,128]{1,0:T(8,128)S(1)}, u32[]{:S(2)}, u32[]{:S(2)}) collective-permute-start(f32[68,128]{1,0:T(8,128)S(1)} %get-tuple-element.13), channel_id=1, source_target_pairs={{0,3},{1,0},{2,1},{3,2},{4,7},{5,4},{6,5},{7,6},{8,11},{9,8},{10,9... | collective-permute-start | bytes 104456 | tf_op jit(solution)/shard_map/ppermute | solution.py:331
  19.5 3.1 %collective-permute-start.3 = (f32[68,128]{1,0:T(8,128)S(1)}, f32[68,128]{1,0:T(8,128)S(1)}, u32[]{:S(2)}, u32[]{:S(2)}) collective-permute-start(f32[68,128]{1,0:T(8,128)S(1)} %get-tuple-element.14), channel_id=1, source_target_pairs={{0,8},{1,2},{2,3},{3,1},{4,12},{5,6},{6,7},{7,5},{8,0},{9,10},{10,... | collective-permute-start | bytes 104456 | tf_op jit(solution)/shard_map/ppermute | solution.py:331

commit v19 on v18

--- a/solution.py
+++ b/solution.py
@@ -67,12 +67,9 @@
     for copy in lists:
         copy.start()
 
-    tables = [
-        pltpu.make_async_copy(exponents_hbm, exponents_ref, table_sems.at[0]),
-        pltpu.make_async_copy(blocks_hbm, blocks_ref, table_sems.at[1]),
-    ]
-    for copy in tables:
-        copy.start()
+    table = pltpu.make_async_copy(exponents_hbm, exponents_ref, table_sems.at[0])
+    blocks = pltpu.make_async_copy(blocks_hbm, blocks_ref, table_sems.at[1])
+    table.start()
     lists[0].wait()
     for k in range(items):
         for side in range(2):
@@ -81,7 +78,8 @@
                 centres_ref.at[2 * k + side],
                 table_sems.at[2],
             ).start()
-    for copy in lists[1:] + tables:
+    blocks.start()
+    for copy in lists[1:] + [table]:
         copy.wait()
     pltpu.make_async_copy(centres_ref, centres_ref, table_sems.at[2]).wait()
     if slots != items:
@@ -105,6 +103,8 @@
         row_x, row_face = factors(0)
         col_x, col_face = factors(1)
         row_face = row_face.T
+        if k == 0:
+            blocks.wait()
         block = blocks_ref[k]
         for x in range(EDGE):
             col = (col_x[x : x + 1, :] * col_face).astype(jnp.bfloat16)

time: 23.7 us -> 24 us (1.013)
  Pallas kernels: 6.61 us -> 6.92 us
    pallas_call x1, Pallas kernels: 5.4 us -> 5.72 us  [body(): pl.pallas_call(functools.partial(pair_kernel, slot_depth, bricks_group),...]
where the time goes in v19:
time: 24 us; the launch traced here: 23.9 us
  blocking collectives  9.93 us (41%)
  Pallas kernels  6.92 us (29%)
  starting transfers between devices  4.13 us (17%)
  waiting for transfers between devices  2.84 us (12%)
    all_to_all x1, blocking collectives, body(): lax.all_to_all(outgoing.reshape(slots, 1, SLOT_ROWS * LANES), ('row', 'co...  9.93 us
    pallas_call x1, Pallas kernels, body(): pl.pallas_call(functools.partial(pair_kernel, slot_depth, bricks_group),...  5.72 us
    ppermute x4, starting transfers between devices, body(): lax.ppermute(piece, ('row', 'col', 'basis'), pairs_of(move, rows, cols))  4.13 us
    ppermute x4, waiting for transfers between devices, body(): lax.ppermute(piece, ('row', 'col', 'basis'), pairs_of(move, rows, cols))  2.84 us
    pallas_call x1, Pallas kernels, body(): pl.pallas_call(cell_kernel, out_shape=jax.ShapeDtypeStruct((bricks_dev, E...  0.84 us
  transfers between devices with their start and end apart: 4, of which 3 were waited for; matrix products, arithmetic and copies ran while one was open for 0% of the time, Pallas kernels for 1%

profile of v19, /device:TPU:0, one launch (start us, length us, event | category | flops | bytes accessed | tf_op | source)
XLA Modules:
  0.0 23.9 jit_solution(5458775437821912152)
XLA Ops:
  0.0 0.0 copy-start.1
  0.0 0.0 copy-start
  0.0 5.7 %pair_density.1 = f32[264,128]{1,0:T(8,128)S(1)} custom-call(s32[2,8]{1,0:T(2,128)} %bitcast.9, s32[8]{0:T(128)} %dest_hbm.1, s32[8]{0:T(128)} %tag_hbm.1, s32[64]{0:T(128)} %levels_hbm.1, bf16[8,128,128]{2,1,0:T(8,128)(2,1)} %blocks_hbm.1, f32[3,1024,128]{2,1,0:T(8,128)} %bitcast.8, f32[1024,128]{1,0:T(8,128)} %exponents_hbm.1), custom_call_target="tpu_custom_call" | custom-call | tf_op jit(solution)/shard_map/pair_density/pallas_call | solution.py:279
  5.7 9.9 %all_to_all.5 = f32[8,1,4224]{2,1,0:T(1,128)S(1)} all-to-all(f32[8,1,4224]{2,1,0:T(1,128)S(1)} %bitcast.5), channel_id=1, replica_groups=mesh['row'=4,'col'=2,'basis'=4] {'row','col'}, dimensions={0} | all-to-all | bytes 270336 | tf_op jit(solution)/shard_map/all_to_all | solution.py:312
  15.7 0.2 group_sum.1
  15.9 1.6 %collective-permute-start = (f32[68,128]{1,0:T(8,128)S(1)}, f32[68,128]{1,0:T(8,128)S(1)}, u32[]{:S(2)}, u32[]{:S(2)}) collective-permute-start(f32[68,128]{1,0:T(8,128)S(1)} %get-tuple-element.11), channel_id=1, source_target_pairs={{0,1},{1,3},{2,10},{3,0},{4,5},{5,7},{6,14},{7,4},{8,9},{9,11},{10... | collective-permute-start | bytes 104456 | tf_op jit(solution)/shard_map/ppermute | solution.py:331
  17.5 1.3 %collective-permute-start.1 = (f32[68,128]{1,0:T(8,128)S(1)}, f32[68,128]{1,0:T(8,128)S(1)}, u32[]{:S(2)}, u32[]{:S(2)}) collective-permute-start(f32[68,128]{1,0:T(8,128)S(1)} %get-tuple-element.12), channel_id=1, source_target_pairs={{0,2},{1,9},{2,0},{3,11},{4,6},{5,13},{6,4},{7,15},{8,10},{9,1},{1... | collective-permute-start | bytes 104456 | tf_op jit(solution)/shard_map/ppermute | solution.py:331
  18.8 1.1 %collective-permute-start.2 = (f32[68,128]{1,0:T(8,128)S(1)}, f32[68,128]{1,0:T(8,128)S(1)}, u32[]{:S(2)}, u32[]{:S(2)}) collective-permute-start(f32[68,128]{1,0:T(8,128)S(1)} %get-tuple-element.13), channel_id=1, source_target_pairs={{0,3},{1,0},{2,1},{3,2},{4,7},{5,4},{6,5},{7,6},{8,11},{9,8},{10,9... | collective-permute-start | bytes 104456 | tf_op jit(solution)/shard_map/ppermute | solution.py:331
  19.9 0.1 collective-permute-start.3
  20.0 0.0 copy-done.1
  20.0 0.1 cell_map.1.refs_5_
  20.2 1.5 %collective-permute-done.refs_1_ = f32[68,128]{1,0:T(8,128)S(1)} collective-permute-done((f32[68,128]{1,0:T(8,128)S(1)}, f32[68,128]{1,0:T(8,128)S(1)}, u32[]{:S(2)}, u32[]{:S(2)}) %collective-permute-start) | collective-permute-done | bytes 34848 | tf_op jit(solution)/shard_map/ppermute | solution.py:331
  21.7 0.7 %collective-permute-done.1.refs_2_ = f32[68,128]{1,0:T(8,128)S(1)} collective-permute-done((f32[68,128]{1,0:T(8,128)S(1)}, f32[68,128]{1,0:T(8,128)S(1)}, u32[]{:S(2)}, u32[]{:S(2)}) %collective-permute-start.1) | collective-permute-done | bytes 34848 | tf_op jit(solution)/shard_map/ppermute | solution.py:331
  22.4 0.6 %collective-permute-done.2.refs_3_ = f32[68,128]{1,0:T(8,128)S(1)} collective-permute-done((f32[68,128]{1,0:T(8,128)S(1)}, f32[68,128]{1,0:T(8,128)S(1)}, u32[]{:S(2)}, u32[]{:S(2)}) %collective-permute-start.2) | collective-permute-done | bytes 34848 | tf_op jit(solution)/shard_map/ppermute | solution.py:331
  23.0 0.0 collective-permute-done.3.refs_4_
  23.0 0.0 copy-done
  23.0 0.8 %cells.1 = f32[2,4096]{1,0:T(2,128)} custom-call(f32[68,128]{1,0:T(8,128)S(1)} %get-tuple-element.10.refs_0_, f32[68,128]{1,0:T(8,128)S(1)} %collective-permute-done.refs_1_, f32[68,128]{1,0:T(8,128)S(1)} %collective-permute-done.1.refs_2_, f32[68,128]{1,0:T(8,128)S(1)} %collective-permute-done.2.refs_3_, f32[68,128]{1,0:T(8,128)S(1)} %collective-permute-done.3.refs_4_, ...), custom_call_target="tpu_custom_call" | custom-call | tf_op jit(solution)/shard_map/cells/pallas_call | solution.py:343
Async XLA Ops:
  0.0 20.0 %copy-start.1 = (s32[2,256]{1,0:T(2,128)S(1)}, s32[2,256]{1,0:T(2,128)}, u32[]{:S(2)}) copy-start(s32[2,256]{1,0:T(2,128)} %cells_ref.1) | copy-start | bytes 6148
  0.0 23.0 %copy-start = (s32[2,256,8]{1,2,0:T(8,128)S(1)}, s32[2,256,8]{1,2,0:T(8,128)}, u32[]{:S(2)}) copy-start(s32[2,256,8]{1,2,0:T(8,128)} %param.17) | copy-start | bytes 49156
  15.9 5.8 %collective-permute-start = (f32[68,128]{1,0:T(8,128)S(1)}, f32[68,128]{1,0:T(8,128)S(1)}, u32[]{:S(2)}, u32[]{:S(2)}) collective-permute-start(f32[68,128]{1,0:T(8,128)S(1)} %get-tuple-element.11), channel_id=1, source_target_pairs={{0,1},{1,3},{2,10},{3,0},{4,5},{5,7},{6,14},{7,4},{8,9},{9,11},{10... | collective-permute-start | bytes 104456 | tf_op jit(solution)/shard_map/ppermute | solution.py:331
  17.5 4.9 %collective-permute-start.1 = (f32[68,128]{1,0:T(8,128)S(1)}, f32[68,128]{1,0:T(8,128)S(1)}, u32[]{:S(2)}, u32[]{:S(2)}) collective-permute-start(f32[68,128]{1,0:T(8,128)S(1)} %get-tuple-element.12), channel_id=1, source_target_pairs={{0,2},{1,9},{2,0},{3,11},{4,6},{5,13},{6,4},{7,15},{8,10},{9,1},{1... | collective-permute-start | bytes 104456 | tf_op jit(solution)/shard_map/ppermute | solution.py:331
  18.8 4.2 %collective-permute-start.2 = (f32[68,128]{1,0:T(8,128)S(1)}, f32[68,128]{1,0:T(8,128)S(1)}, u32[]{:S(2)}, u32[]{:S(2)}) collective-permute-start(f32[68,128]{1,0:T(8,128)S(1)} %get-tuple-element.13), channel_id=1, source_target_pairs={{0,3},{1,0},{2,1},{3,2},{4,7},{5,4},{6,5},{7,6},{8,11},{9,8},{10,9... | collective-permute-start | bytes 104456 | tf_op jit(solution)/shard_map/ppermute | solution.py:331
  19.9 3.1 %collective-permute-start.3 = (f32[68,128]{1,0:T(8,128)S(1)}, f32[68,128]{1,0:T(8,128)S(1)}, u32[]{:S(2)}, u32[]{:S(2)}) collective-permute-start(f32[68,128]{1,0:T(8,128)S(1)} %get-tuple-element.14), channel_id=1, source_target_pairs={{0,8},{1,2},{2,3},{3,1},{4,12},{5,6},{6,7},{7,5},{8,0},{9,10},{10,... | collective-permute-start | bytes 104456 | tf_op jit(solution)/shard_map/ppermute | solution.py:331

commit v20 on v16

--- a/solution.py
+++ b/solution.py
@@ -23,6 +23,20 @@
 
 def iota(shape, axis):
     return lax.broadcasted_iota(jnp.int32, shape, axis)
+
+
+def fold(tiles):
+    row = iota((TILE, LANES), 0)
+    step = 1
+    while len(tiles) > 1:
+        odd = (row & step) != 0
+        tiles = [
+            jnp.where(odd, b, a)
+            + jnp.where(odd, pltpu.roll(b, step, 0), pltpu.roll(a, TILE - step, 0))
+            for a, b in zip(tiles[::2], tiles[1::2])
+        ]
+        step *= 2
+    return tiles[0]
 
 
 def axis_factors(coords, middle, decay):
@@ -44,6 +58,7 @@
     dest_ref,
     tag_ref,
     levels_ref,
+    order_ref,
     blocks_ref,
     centres_ref,
     exponents_ref,
@@ -70,9 +85,9 @@
     tables = [
         pltpu.make_async_copy(exponents_hbm, exponents_ref, table_sems.at[0]),
         pltpu.make_async_copy(centres_hbm, centres_ref, table_sems.at[1]),
+        pltpu.make_async_copy(blocks_hbm, blocks_ref, table_sems.at[2]),
     ]
-    blocks = pltpu.make_async_copy(blocks_hbm, blocks_ref, table_sems.at[2])
-    for copy in tables + [blocks]:
+    for copy in tables:
         copy.start()
     for copy in lists + tables:
         copy.wait()
@@ -80,8 +95,15 @@
         out_ref[...] = jnp.zeros_like(out_ref)
     steps = iota((EDGE, LANES), 0).astype(jnp.float32) - (EDGE - 1) / 2.0
 
-    def one(k):
-        target = dest_ref[k] // slot_depth * bricks_group + tag_ref[k]
+    if slots == items:
+        for k in range(items):
+            order_ref[dest_ref[k]] = k
+        work = [(order_ref[slot], slot) for slot in range(slots)]
+    else:
+        work = [(k, dest_ref[k]) for k in range(items)]
+
+    def one(n, k, slot):
+        target = slot // slot_depth * bricks_group + tag_ref[k]
         spacing = jnp.where(levels_ref[target] == 1, COARSE * 0.5, COARSE)
         coords = steps * spacing
 
@@ -97,9 +119,8 @@
         row_x, row_face = factors(0)
         col_x, col_face = factors(1)
         row_face = row_face.T
-        if k == 0:
-            blocks.wait()
         block = blocks_ref[k]
+        sums = []
         for x in range(EDGE):
             col = (col_x[x : x + 1, :] * col_face).astype(jnp.bfloat16)
             product = lax.dot_general(
@@ -107,15 +128,20 @@
             )
             weight = jnp.broadcast_to(row_x[x : x + 1, :], (LANES, block.shape[0])).T
             weight = jnp.concatenate([weight] * (FACE // LANES), axis=1)
-            dens = jnp.sum(weight * row_face * product, axis=0, keepdims=True)
-            for half in range(FACE // LANES):
-                piece = dens[:, half * LANES : (half + 1) * LANES]
-                out_ref[pl.ds(dest_ref[k] * SLOT_ROWS + 2 * x + half, 1), :] = piece
-                if x in (0, EDGE - 1):
-                    corner_buf[2 * (x // (EDGE - 1)) + half, pl.ds(k, 1), :] = piece
-
-    for k in range(items):
-        one(k)
+            parts = (weight * row_face * product).reshape(-1, TILE, FACE).sum(axis=0)
+            sums.extend(parts[:, c : c + LANES] for c in range(0, FACE, LANES))
+            if len(sums) == TILE:
+                tile = fold(sums)
+                sums = []
+                first = 2 * (x + 1) - TILE
+                out_ref[pl.ds(slot * SLOT_ROWS + first, TILE), :] = tile
+                if first == 0:
+                    corner_buf[:2, n] = tile[:2]
+                if first == ROWS - TILE:
+                    corner_buf[2:, n] = tile[TILE - 2 :]
+
+    for n, (k, slot) in enumerate(work):
+        one(n, k, slot)
 
     shape = (items, LANES)
     lane = iota(shape, 1)
@@ -130,9 +156,9 @@
     values = jnp.where(corner >= 4, last, first)
     row = iota(shape, 0)
     brick = jnp.zeros(shape, jnp.int32)
-    for k in range(items):
-        target = dest_ref[k] // slot_depth * bricks_group + tag_ref[k]
-        brick = jnp.where(row == k, target, brick)
+    for n, (k, slot) in enumerate(work):
+        target = slot // slot_depth * bricks_group + tag_ref[k]
+        brick = jnp.where(row == n, target, brick)
     placed = jnp.where(lane // 8 == row, values, 0.0)
     placed = jnp.where(lane == 8 * items + row, brick.astype(jnp.float32), placed)
     meta = jnp.sum(placed, axis=0, keepdims=True)
@@ -143,9 +169,9 @@
         def _(n):
             out_ref[pl.ds(n * SLOT_ROWS + ROWS, 1), :] = jnp.where(last_lane, -1.0, meta)
 
-    for k in range(items):
+    for k, slot in work:
         tagged = jnp.where(last_lane, tag_ref[k].astype(jnp.float32), meta)
-        out_ref[pl.ds(dest_ref[k] * SLOT_ROWS + ROWS, 1), :] = tagged
+        out_ref[pl.ds(slot * SLOT_ROWS + ROWS, 1), :] = tagged
 
 
 def group_kernel(items, bricks_dev, moves, in_ref, *outs):
@@ -266,7 +292,7 @@
     bricks = levels.shape[0]
     bricks_group = bricks // groups
     bricks_dev = bricks_group // owners
-    table_rows = -(-bricks * 8 // (8 * LANES)) * 8
+    table_rows = -(-bricks * 8 // LANES)
     basis = block_data.shape[1]
     params = pltpu.CompilerParams(vmem_limit_bytes=32 * 1024 * 1024)
 
@@ -280,6 +306,7 @@
             pltpu.SMEM((items,), jnp.int32),
             pltpu.SMEM((items,), jnp.int32),
             pltpu.SMEM((bricks,), jnp.int32),
+            pltpu.SMEM((items,), jnp.int32),
             pltpu.VMEM(block_data.shape, block_data.dtype),
             pltpu.VMEM((3, centres.shape[0], basis), jnp.float32),
             pltpu.VMEM(exponents.shape, jnp.float32),

time: 23.8 us -> 23.6 us (level)
  no operation moved by 1% of the time
where the time goes in v20:
time: 23.6 us; the launch traced here: 23.4 us
  blocking collectives  9.93 us (42%)
  Pallas kernels  6.51 us (28%)
  starting transfers between devices  4.13 us (18%)
  waiting for transfers between devices  2.84 us (12%)
    all_to_all x1, blocking collectives, body(): lax.all_to_all(outgoing.reshape(slots, 1, SLOT_ROWS * LANES), ('row', 'co...  9.93 us
    pallas_call x1, Pallas kernels, body(): pl.pallas_call(functools.partial(pair_kernel, slot_depth, bricks_group),...  5.3 us
    ppermute x4, starting transfers between devices, body(): lax.ppermute(piece, ('row', 'col', 'basis'), pairs_of(move, rows, cols))  4.13 us
    ppermute x4, waiting for transfers between devices, body(): lax.ppermute(piece, ('row', 'col', 'basis'), pairs_of(move, rows, cols))  2.84 us
    pallas_call x1, Pallas kernels, body(): pl.pallas_call(cell_kernel, out_shape=jax.ShapeDtypeStruct((bricks_dev, E...  0.84 us
  transfers between devices with their start and end apart: 4, of which 3 were waited for; matrix products, arithmetic and copies ran while one was open for 0% of the time, Pallas kernels for 1%

profile of v20, /device:TPU:0, one launch (start us, length us, event | category | flops | bytes accessed | tf_op | source)
XLA Modules:
  0.0 23.4 jit_solution(9804979484109650157)
XLA Ops:
  0.0 0.0 copy-start.1
  0.0 0.0 copy-start
  0.0 5.3 %pair_density.1 = f32[264,128]{1,0:T(8,128)S(1)} custom-call(s32[2,8]{1,0:T(2,128)} %bitcast.9, s32[8]{0:T(128)} %dest_hbm.1, s32[8]{0:T(128)} %tag_hbm.1, s32[64]{0:T(128)} %levels_hbm.1, bf16[8,128,128]{2,1,0:T(8,128)(2,1)} %blocks_hbm.1, f32[3,1024,128]{2,1,0:T(8,128)} %bitcast.8, f32[1024,128]{1,0:T(8,128)} %exponents_hbm.1), custom_call_target="tpu_custom_call" | custom-call | tf_op jit(solution)/shard_map/pair_density/pallas_call | solution.py:299
  5.3 9.9 %all_to_all.5 = f32[8,1,4224]{2,1,0:T(1,128)S(1)} all-to-all(f32[8,1,4224]{2,1,0:T(1,128)S(1)} %bitcast.5), channel_id=1, replica_groups=mesh['row'=4,'col'=2,'basis'=4] {'row','col'}, dimensions={0} | all-to-all | bytes 270336 | tf_op jit(solution)/shard_map/all_to_all | solution.py:333
  15.2 0.2 group_sum.1
  15.5 1.6 %collective-permute-start = (f32[68,128]{1,0:T(8,128)S(1)}, f32[68,128]{1,0:T(8,128)S(1)}, u32[]{:S(2)}, u32[]{:S(2)}) collective-permute-start(f32[68,128]{1,0:T(8,128)S(1)} %get-tuple-element.11), channel_id=1, source_target_pairs={{0,1},{1,3},{2,10},{3,0},{4,5},{5,7},{6,14},{7,4},{8,9},{9,11},{10... | collective-permute-start | bytes 104456 | tf_op jit(solution)/shard_map/ppermute | solution.py:352
  17.1 1.3 %collective-permute-start.1 = (f32[68,128]{1,0:T(8,128)S(1)}, f32[68,128]{1,0:T(8,128)S(1)}, u32[]{:S(2)}, u32[]{:S(2)}) collective-permute-start(f32[68,128]{1,0:T(8,128)S(1)} %get-tuple-element.12), channel_id=1, source_target_pairs={{0,2},{1,9},{2,0},{3,11},{4,6},{5,13},{6,4},{7,15},{8,10},{9,1},{1... | collective-permute-start | bytes 104456 | tf_op jit(solution)/shard_map/ppermute | solution.py:352
  18.3 1.1 %collective-permute-start.2 = (f32[68,128]{1,0:T(8,128)S(1)}, f32[68,128]{1,0:T(8,128)S(1)}, u32[]{:S(2)}, u32[]{:S(2)}) collective-permute-start(f32[68,128]{1,0:T(8,128)S(1)} %get-tuple-element.13), channel_id=1, source_target_pairs={{0,3},{1,0},{2,1},{3,2},{4,7},{5,4},{6,5},{7,6},{8,11},{9,8},{10,9... | collective-permute-start | bytes 104456 | tf_op jit(solution)/shard_map/ppermute | solution.py:352
  19.4 0.1 collective-permute-start.3
  19.6 0.0 copy-done.1
  19.6 0.1 cell_map.1.refs_5_
  19.7 1.6 %collective-permute-done.refs_1_ = f32[68,128]{1,0:T(8,128)S(1)} collective-permute-done((f32[68,128]{1,0:T(8,128)S(1)}, f32[68,128]{1,0:T(8,128)S(1)}, u32[]{:S(2)}, u32[]{:S(2)}) %collective-permute-start) | collective-permute-done | bytes 34848 | tf_op jit(solution)/shard_map/ppermute | solution.py:352
  21.3 0.7 %collective-permute-done.1.refs_2_ = f32[68,128]{1,0:T(8,128)S(1)} collective-permute-done((f32[68,128]{1,0:T(8,128)S(1)}, f32[68,128]{1,0:T(8,128)S(1)}, u32[]{:S(2)}, u32[]{:S(2)}) %collective-permute-start.1) | collective-permute-done | bytes 34848 | tf_op jit(solution)/shard_map/ppermute | solution.py:352
  22.0 0.6 %collective-permute-done.2.refs_3_ = f32[68,128]{1,0:T(8,128)S(1)} collective-permute-done((f32[68,128]{1,0:T(8,128)S(1)}, f32[68,128]{1,0:T(8,128)S(1)}, u32[]{:S(2)}, u32[]{:S(2)}) %collective-permute-start.2) | collective-permute-done | bytes 34848 | tf_op jit(solution)/shard_map/ppermute | solution.py:352
  22.6 0.0 collective-permute-done.3.refs_4_
  22.6 0.0 copy-done
  22.6 0.8 %cells.1 = f32[2,4096]{1,0:T(2,128)} custom-call(f32[68,128]{1,0:T(8,128)S(1)} %get-tuple-element.10.refs_0_, f32[68,128]{1,0:T(8,128)S(1)} %collective-permute-done.refs_1_, f32[68,128]{1,0:T(8,128)S(1)} %collective-permute-done.1.refs_2_, f32[68,128]{1,0:T(8,128)S(1)} %collective-permute-done.2.refs_3_, f32[68,128]{1,0:T(8,128)S(1)} %collective-permute-done.3.refs_4_, ...), custom_call_target="tpu_custom_call" | custom-call | tf_op jit(solution)/shard_map/cells/pallas_call | solution.py:364
Async XLA Ops:
  0.0 19.6 %copy-start.1 = (s32[2,256]{1,0:T(2,128)S(1)}, s32[2,256]{1,0:T(2,128)}, u32[]{:S(2)}) copy-start(s32[2,256]{1,0:T(2,128)} %cells_ref.1) | copy-start | bytes 6148
  0.0 22.6 %copy-start = (s32[2,256,8]{1,2,0:T(8,128)S(1)}, s32[2,256,8]{1,2,0:T(8,128)}, u32[]{:S(2)}) copy-start(s32[2,256,8]{1,2,0:T(8,128)} %param.17) | copy-start | bytes 49156
  15.5 5.8 %collective-permute-start = (f32[68,128]{1,0:T(8,128)S(1)}, f32[68,128]{1,0:T(8,128)S(1)}, u32[]{:S(2)}, u32[]{:S(2)}) collective-permute-start(f32[68,128]{1,0:T(8,128)S(1)} %get-tuple-element.11), channel_id=1, source_target_pairs={{0,1},{1,3},{2,10},{3,0},{4,5},{5,7},{6,14},{7,4},{8,9},{9,11},{10... | collective-permute-start | bytes 104456 | tf_op jit(solution)/shard_map/ppermute | solution.py:352
  17.1 4.9 %collective-permute-start.1 = (f32[68,128]{1,0:T(8,128)S(1)}, f32[68,128]{1,0:T(8,128)S(1)}, u32[]{:S(2)}, u32[]{:S(2)}) collective-permute-start(f32[68,128]{1,0:T(8,128)S(1)} %get-tuple-element.12), channel_id=1, source_target_pairs={{0,2},{1,9},{2,0},{3,11},{4,6},{5,13},{6,4},{7,15},{8,10},{9,1},{1... | collective-permute-start | bytes 104456 | tf_op jit(solution)/shard_map/ppermute | solution.py:352
  18.3 4.2 %collective-permute-start.2 = (f32[68,128]{1,0:T(8,128)S(1)}, f32[68,128]{1,0:T(8,128)S(1)}, u32[]{:S(2)}, u32[]{:S(2)}) collective-permute-start(f32[68,128]{1,0:T(8,128)S(1)} %get-tuple-element.13), channel_id=1, source_target_pairs={{0,3},{1,0},{2,1},{3,2},{4,7},{5,4},{6,5},{7,6},{8,11},{9,8},{10,9... | collective-permute-start | bytes 104456 | tf_op jit(solution)/shard_map/ppermute | solution.py:352
  19.4 3.1 %collective-permute-start.3 = (f32[68,128]{1,0:T(8,128)S(1)}, f32[68,128]{1,0:T(8,128)S(1)}, u32[]{:S(2)}, u32[]{:S(2)}) collective-permute-start(f32[68,128]{1,0:T(8,128)S(1)} %get-tuple-element.14), channel_id=1, source_target_pairs={{0,8},{1,2},{2,3},{3,1},{4,12},{5,6},{6,7},{7,5},{8,0},{9,10},{10,... | collective-permute-start | bytes 104456 | tf_op jit(solution)/shard_map/ppermute | solution.py:352

commit v21 on v20

--- a/solution.py
+++ b/solution.py
@@ -82,15 +82,24 @@
     for copy in lists:
         copy.start()
 
-    tables = [
-        pltpu.make_async_copy(exponents_hbm, exponents_ref, table_sems.at[0]),
-        pltpu.make_async_copy(centres_hbm, centres_ref, table_sems.at[1]),
-        pltpu.make_async_copy(blocks_hbm, blocks_ref, table_sems.at[2]),
-    ]
-    for copy in tables:
-        copy.start()
-    for copy in lists + tables:
+    lists[0].wait()
+    for k in range(items):
+        for side in range(2):
+            row = pl.ds(pairs_ref[side, k], 1)
+            at = 2 * k + side
+            pltpu.make_async_copy(
+                centres_hbm.at[:, row, :], centres_ref.at[at], table_sems.at[0]
+            ).start()
+            pltpu.make_async_copy(
+                exponents_hbm.at[row, :], exponents_ref.at[at], table_sems.at[1]
+            ).start()
+    blocks = pltpu.make_async_copy(blocks_hbm, blocks_ref, table_sems.at[2])
+    blocks.start()
+    for copy in lists[1:]:
         copy.wait()
+    pltpu.make_async_copy(centres_ref, centres_ref, table_sems.at[0]).wait()
+    pltpu.make_async_copy(exponents_ref, exponents_ref, table_sems.at[1]).wait()
+    blocks.wait()
     if slots != items:
         out_ref[...] = jnp.zeros_like(out_ref)
     steps = iota((EDGE, LANES), 0).astype(jnp.float32) - (EDGE - 1) / 2.0
@@ -108,9 +117,9 @@
         coords = steps * spacing
 
         def factors(side):
-            row = pl.ds(pairs_ref[side, k], 1)
-            decay = exponents_ref[row, :]
-            found = [axis_factors(coords, centres_ref[d, row, :], decay) for d in range(3)]
+            at = 2 * k + side
+            decay = exponents_ref[at]
+            found = [axis_factors(coords, centres_ref[at, d], decay) for d in range(3)]
             face = jnp.concatenate(
                 [found[1][y : y + 1, :] * found[2] for y in range(EDGE)], axis=0
             )
@@ -308,8 +317,8 @@
             pltpu.SMEM((bricks,), jnp.int32),
             pltpu.SMEM((items,), jnp.int32),
             pltpu.VMEM(block_data.shape, block_data.dtype),
-            pltpu.VMEM((3, centres.shape[0], basis), jnp.float32),
-            pltpu.VMEM(exponents.shape, jnp.float32),
+            pltpu.VMEM((2 * items, 3, 1, basis), jnp.float32),
+            pltpu.VMEM((2 * items, 1, basis), jnp.float32),
             pltpu.VMEM((4, items, LANES), jnp.float32),
             pltpu.SemaphoreType.DMA((4,)),
             pltpu.SemaphoreType.DMA((3,)),

time: 23.6 us -> 24 us (1.017)
  Pallas kernels: 6.51 us -> 6.87 us
    pallas_call x1, Pallas kernels: 5.3 us -> 5.67 us  [body(): pl.pallas_call(functools.partial(pair_kernel, slot_depth, bricks_group),...]
where the time goes in v21:
time: 24 us; the launch traced here: 23.8 us
  blocking collectives  9.93 us (41%)
  Pallas kernels  6.87 us (29%)
  starting transfers between devices  4.14 us (17%)
  waiting for transfers between devices  2.84 us (12%)
    all_to_all x1, blocking collectives, body(): lax.all_to_all(outgoing.reshape(slots, 1, SLOT_ROWS * LANES), ('row', 'co...  9.93 us
    pallas_call x1, Pallas kernels, body(): pl.pallas_call(functools.partial(pair_kernel, slot_depth, bricks_group),...  5.67 us
    ppermute x4, starting transfers between devices, body(): lax.ppermute(piece, ('row', 'col', 'basis'), pairs_of(move, rows, cols))  4.14 us
    ppermute x4, waiting for transfers between devices, body(): lax.ppermute(piece, ('row', 'col', 'basis'), pairs_of(move, rows, cols))  2.84 us
    pallas_call x1, Pallas kernels, body(): pl.pallas_call(cell_kernel, out_shape=jax.ShapeDtypeStruct((bricks_dev, E...  0.84 us
  transfers between devices with their start and end apart: 4, of which 3 were waited for; matrix products, arithmetic and copies ran while one was open for 0% of the time, Pallas kernels for 1%

profile of v21, /device:TPU:0, one launch (start us, length us, event | category | flops | bytes accessed | tf_op | source)
XLA Modules:
  0.0 23.8 jit_solution(5469161445504425011)
XLA Ops:
  0.0 0.0 copy-start.1
  0.0 0.0 copy-start
  0.0 5.7 %pair_density.1 = f32[264,128]{1,0:T(8,128)S(1)} custom-call(s32[2,8]{1,0:T(2,128)} %bitcast.9, s32[8]{0:T(128)} %dest_hbm.1, s32[8]{0:T(128)} %tag_hbm.1, s32[64]{0:T(128)} %levels_hbm.1, bf16[8,128,128]{2,1,0:T(8,128)(2,1)} %blocks_hbm.1, f32[3,1024,128]{2,1,0:T(8,128)} %bitcast.8, f32[1024,128]{1,0:T(8,128)} %exponents_hbm.1), custom_call_target="tpu_custom_call" | custom-call | tf_op jit(solution)/shard_map/pair_density/pallas_call | solution.py:308
  5.7 9.9 %all_to_all.5 = f32[8,1,4224]{2,1,0:T(1,128)S(1)} all-to-all(f32[8,1,4224]{2,1,0:T(1,128)S(1)} %bitcast.5), channel_id=1, replica_groups=mesh['row'=4,'col'=2,'basis'=4] {'row','col'}, dimensions={0} | all-to-all | bytes 270336 | tf_op jit(solution)/shard_map/all_to_all | solution.py:342
  15.6 0.2 group_sum.1
  15.8 1.6 %collective-permute-start = (f32[68,128]{1,0:T(8,128)S(1)}, f32[68,128]{1,0:T(8,128)S(1)}, u32[]{:S(2)}, u32[]{:S(2)}) collective-permute-start(f32[68,128]{1,0:T(8,128)S(1)} %get-tuple-element.11), channel_id=1, source_target_pairs={{0,1},{1,3},{2,10},{3,0},{4,5},{5,7},{6,14},{7,4},{8,9},{9,11},{10... | collective-permute-start | bytes 104456 | tf_op jit(solution)/shard_map/ppermute | solution.py:361
  17.5 1.3 %collective-permute-start.1 = (f32[68,128]{1,0:T(8,128)S(1)}, f32[68,128]{1,0:T(8,128)S(1)}, u32[]{:S(2)}, u32[]{:S(2)}) collective-permute-start(f32[68,128]{1,0:T(8,128)S(1)} %get-tuple-element.12), channel_id=1, source_target_pairs={{0,2},{1,9},{2,0},{3,11},{4,6},{5,13},{6,4},{7,15},{8,10},{9,1},{1... | collective-permute-start | bytes 104456 | tf_op jit(solution)/shard_map/ppermute | solution.py:361
  18.7 1.1 %collective-permute-start.2 = (f32[68,128]{1,0:T(8,128)S(1)}, f32[68,128]{1,0:T(8,128)S(1)}, u32[]{:S(2)}, u32[]{:S(2)}) collective-permute-start(f32[68,128]{1,0:T(8,128)S(1)} %get-tuple-element.13), channel_id=1, source_target_pairs={{0,3},{1,0},{2,1},{3,2},{4,7},{5,4},{6,5},{7,6},{8,11},{9,8},{10,9... | collective-permute-start | bytes 104456 | tf_op jit(solution)/shard_map/ppermute | solution.py:361
  19.8 0.1 collective-permute-start.3
  20.0 0.0 copy-done.1
  20.0 0.1 cell_map.1.refs_5_
  20.1 1.5 %collective-permute-done.refs_1_ = f32[68,128]{1,0:T(8,128)S(1)} collective-permute-done((f32[68,128]{1,0:T(8,128)S(1)}, f32[68,128]{1,0:T(8,128)S(1)}, u32[]{:S(2)}, u32[]{:S(2)}) %collective-permute-start) | collective-permute-done | bytes 34848 | tf_op jit(solution)/shard_map/ppermute | solution.py:361
  21.7 0.7 %collective-permute-done.1.refs_2_ = f32[68,128]{1,0:T(8,128)S(1)} collective-permute-done((f32[68,128]{1,0:T(8,128)S(1)}, f32[68,128]{1,0:T(8,128)S(1)}, u32[]{:S(2)}, u32[]{:S(2)}) %collective-permute-start.1) | collective-permute-done | bytes 34848 | tf_op jit(solution)/shard_map/ppermute | solution.py:361
  22.4 0.6 %collective-permute-done.2.refs_3_ = f32[68,128]{1,0:T(8,128)S(1)} collective-permute-done((f32[68,128]{1,0:T(8,128)S(1)}, f32[68,128]{1,0:T(8,128)S(1)}, u32[]{:S(2)}, u32[]{:S(2)}) %collective-permute-start.2) | collective-permute-done | bytes 34848 | tf_op jit(solution)/shard_map/ppermute | solution.py:361
  23.0 0.0 collective-permute-done.3.refs_4_
  23.0 0.0 copy-done
  23.0 0.8 %cells.1 = f32[2,4096]{1,0:T(2,128)} custom-call(f32[68,128]{1,0:T(8,128)S(1)} %get-tuple-element.10.refs_0_, f32[68,128]{1,0:T(8,128)S(1)} %collective-permute-done.refs_1_, f32[68,128]{1,0:T(8,128)S(1)} %collective-permute-done.1.refs_2_, f32[68,128]{1,0:T(8,128)S(1)} %collective-permute-done.2.refs_3_, f32[68,128]{1,0:T(8,128)S(1)} %collective-permute-done.3.refs_4_, ...), custom_call_target="tpu_custom_call" | custom-call | tf_op jit(solution)/shard_map/cells/pallas_call | solution.py:373
Async XLA Ops:
  0.0 20.0 %copy-start.1 = (s32[2,256]{1,0:T(2,128)S(1)}, s32[2,256]{1,0:T(2,128)}, u32[]{:S(2)}) copy-start(s32[2,256]{1,0:T(2,128)} %cells_ref.1) | copy-start | bytes 6148
  0.0 23.0 %copy-start = (s32[2,256,8]{1,2,0:T(8,128)S(1)}, s32[2,256,8]{1,2,0:T(8,128)}, u32[]{:S(2)}) copy-start(s32[2,256,8]{1,2,0:T(8,128)} %param.17) | copy-start | bytes 49156
  15.8 5.8 %collective-permute-start = (f32[68,128]{1,0:T(8,128)S(1)}, f32[68,128]{1,0:T(8,128)S(1)}, u32[]{:S(2)}, u32[]{:S(2)}) collective-permute-start(f32[68,128]{1,0:T(8,128)S(1)} %get-tuple-element.11), channel_id=1, source_target_pairs={{0,1},{1,3},{2,10},{3,0},{4,5},{5,7},{6,14},{7,4},{8,9},{9,11},{10... | collective-permute-start | bytes 104456 | tf_op jit(solution)/shard_map/ppermute | solution.py:361
  17.5 4.9 %collective-permute-start.1 = (f32[68,128]{1,0:T(8,128)S(1)}, f32[68,128]{1,0:T(8,128)S(1)}, u32[]{:S(2)}, u32[]{:S(2)}) collective-permute-start(f32[68,128]{1,0:T(8,128)S(1)} %get-tuple-element.12), channel_id=1, source_target_pairs={{0,2},{1,9},{2,0},{3,11},{4,6},{5,13},{6,4},{7,15},{8,10},{9,1},{1... | collective-permute-start | bytes 104456 | tf_op jit(solution)/shard_map/ppermute | solution.py:361
  18.7 4.2 %collective-permute-start.2 = (f32[68,128]{1,0:T(8,128)S(1)}, f32[68,128]{1,0:T(8,128)S(1)}, u32[]{:S(2)}, u32[]{:S(2)}) collective-permute-start(f32[68,128]{1,0:T(8,128)S(1)} %get-tuple-element.13), channel_id=1, source_target_pairs={{0,3},{1,0},{2,1},{3,2},{4,7},{5,4},{6,5},{7,6},{8,11},{9,8},{10,9... | collective-permute-start | bytes 104456 | tf_op jit(solution)/shard_map/ppermute | solution.py:361
  19.8 3.1 %collective-permute-start.3 = (f32[68,128]{1,0:T(8,128)S(1)}, f32[68,128]{1,0:T(8,128)S(1)}, u32[]{:S(2)}, u32[]{:S(2)}) collective-permute-start(f32[68,128]{1,0:T(8,128)S(1)} %get-tuple-element.14), channel_id=1, source_target_pairs={{0,8},{1,2},{2,3},{3,1},{4,12},{5,6},{6,7},{7,5},{8,0},{9,10},{10,... | collective-permute-start | bytes 104456 | tf_op jit(solution)/shard_map/ppermute | solution.py:361

commit v22 on v20

--- a/solution.py
+++ b/solution.py
@@ -102,7 +102,7 @@
     else:
         work = [(k, dest_ref[k]) for k in range(items)]
 
-    def one(n, k, slot):
+    def prepare(k, slot):
         target = slot // slot_depth * bricks_group + tag_ref[k]
         spacing = jnp.where(levels_ref[target] == 1, COARSE * 0.5, COARSE)
         coords = steps * spacing
@@ -117,31 +117,46 @@
             return found[0], face
 
         row_x, row_face = factors(0)
-        col_x, col_face = factors(1)
-        row_face = row_face.T
-        block = blocks_ref[k]
-        sums = []
-        for x in range(EDGE):
-            col = (col_x[x : x + 1, :] * col_face).astype(jnp.bfloat16)
-            product = lax.dot_general(
-                block, col, (((1,), (1,)), ((), ())), preferred_element_type=jnp.float32
-            )
-            weight = jnp.broadcast_to(row_x[x : x + 1, :], (LANES, block.shape[0])).T
-            weight = jnp.concatenate([weight] * (FACE // LANES), axis=1)
-            parts = (weight * row_face * product).reshape(-1, TILE, FACE).sum(axis=0)
-            sums.extend(parts[:, c : c + LANES] for c in range(0, FACE, LANES))
+        return row_x, row_face.T, *factors(1), blocks_ref[k]
+
+    def multiply(ready, x):
+        _, _, col_x, col_face, block = ready
+        col = (col_x[x : x + 1, :] * col_face).astype(jnp.bfloat16)
+        return lax.dot_general(
+            block, col, (((1,), (1,)), ((), ())), preferred_element_type=jnp.float32
+        )
+
+    def reduce(ready, x, product, sums):
+        row_x, row_face = ready[:2]
+        weight = jnp.broadcast_to(row_x[x : x + 1, :], (LANES, row_face.shape[0])).T
+        weight = jnp.concatenate([weight] * (FACE // LANES), axis=1)
+        parts = (weight * row_face * product).reshape(-1, TILE, FACE).sum(axis=0)
+        sums.extend(parts[:, c : c + LANES] for c in range(0, FACE, LANES))
+
+    def store(n, slot, x, sums):
+        tile = fold(sums)
+        sums.clear()
+        first = 2 * (x + 1) - TILE
+        out_ref[pl.ds(slot * SLOT_ROWS + first, TILE), :] = tile
+        if first == 0:
+            corner_buf[:2, n] = tile[:2]
+        if first == ROWS - TILE:
+            corner_buf[2:, n] = tile[TILE - 2 :]
+
+    ahead, early = 1, 8
+    flat = [(n, x) for n in range(items) for x in range(EDGE)]
+    ready, products, sums = {0: prepare(*work[0])}, {}, []
+    for at in range(-ahead, len(flat)):
+        if at + ahead < len(flat):
+            n, x = flat[at + ahead]
+            products[n, x] = multiply(ready[n], x)
+            if x == early and n + 1 < items:
+                ready[n + 1] = prepare(*work[n + 1])
+        if at >= 0:
+            n, x = flat[at]
+            reduce(ready[n], x, products.pop((n, x)), sums)
             if len(sums) == TILE:
-                tile = fold(sums)
-                sums = []
-                first = 2 * (x + 1) - TILE
-                out_ref[pl.ds(slot * SLOT_ROWS + first, TILE), :] = tile
-                if first == 0:
-                    corner_buf[:2, n] = tile[:2]
-                if first == ROWS - TILE:
-                    corner_buf[2:, n] = tile[TILE - 2 :]
-
-    for n, (k, slot) in enumerate(work):
-        one(n, k, slot)
+                store(n, work[n][1], x, sums)
 
     shape = (items, LANES)
     lane = iota(shape, 1)

time: 23.6 us -> 23.5 us (level)
  no operation moved by 1% of the time
where the time goes in v22:
time: 23.5 us; the launch traced here: 23.3 us
  blocking collectives  9.91 us (42%)
  Pallas kernels  6.4 us (27%)
  starting transfers between devices  4.11 us (17%)
  waiting for transfers between devices  2.89 us (12%)
    all_to_all x1, blocking collectives, body(): lax.all_to_all(outgoing.reshape(slots, 1, SLOT_ROWS * LANES), ('row', 'co...  9.91 us
    pallas_call x1, Pallas kernels, body(): pl.pallas_call(functools.partial(pair_kernel, slot_depth, bricks_group),...  5.19 us
    ppermute x4, starting transfers between devices, body(): lax.ppermute(piece, ('row', 'col', 'basis'), pairs_of(move, rows, cols))  4.11 us
    ppermute x4, waiting for transfers between devices, body(): lax.ppermute(piece, ('row', 'col', 'basis'), pairs_of(move, rows, cols))  2.89 us
    pallas_call x1, Pallas kernels, body(): pl.pallas_call(cell_kernel, out_shape=jax.ShapeDtypeStruct((bricks_dev, E...  0.84 us
  transfers between devices with their start and end apart: 4, of which 3 were waited for; matrix products, arithmetic and copies ran while one was open for 0% of the time, Pallas kernels for 1%

profile of v22, /device:TPU:0, one launch (start us, length us, event | category | flops | bytes accessed | tf_op | source)
XLA Modules:
  0.0 23.3 jit_solution(15599806997922203258)
XLA Ops:
  0.0 0.0 copy-start.1
  0.0 0.0 copy-start
  0.0 5.2 %pair_density.1 = f32[264,128]{1,0:T(8,128)S(1)} custom-call(s32[2,8]{1,0:T(2,128)} %bitcast.9, s32[8]{0:T(128)} %dest_hbm.1, s32[8]{0:T(128)} %tag_hbm.1, s32[64]{0:T(128)} %levels_hbm.1, bf16[8,128,128]{2,1,0:T(8,128)(2,1)} %blocks_hbm.1, f32[3,1024,128]{2,1,0:T(8,128)} %bitcast.8, f32[1024,128]{1,0:T(8,128)} %exponents_hbm.1), custom_call_target="tpu_custom_call" | custom-call | tf_op jit(solution)/shard_map/pair_density/pallas_call | solution.py:314
  5.2 9.9 %all_to_all.5 = f32[8,1,4224]{2,1,0:T(1,128)S(1)} all-to-all(f32[8,1,4224]{2,1,0:T(1,128)S(1)} %bitcast.5), channel_id=1, replica_groups=mesh['row'=4,'col'=2,'basis'=4] {'row','col'}, dimensions={0} | all-to-all | bytes 270336 | tf_op jit(solution)/shard_map/all_to_all | solution.py:348
  15.1 0.2 group_sum.1
  15.3 1.6 %collective-permute-start = (f32[68,128]{1,0:T(8,128)S(1)}, f32[68,128]{1,0:T(8,128)S(1)}, u32[]{:S(2)}, u32[]{:S(2)}) collective-permute-start(f32[68,128]{1,0:T(8,128)S(1)} %get-tuple-element.11), channel_id=1, source_target_pairs={{0,1},{1,3},{2,10},{3,0},{4,5},{5,7},{6,14},{7,4},{8,9},{9,11},{10... | collective-permute-start | bytes 104456 | tf_op jit(solution)/shard_map/ppermute | solution.py:367
  17.0 1.3 %collective-permute-start.1 = (f32[68,128]{1,0:T(8,128)S(1)}, f32[68,128]{1,0:T(8,128)S(1)}, u32[]{:S(2)}, u32[]{:S(2)}) collective-permute-start(f32[68,128]{1,0:T(8,128)S(1)} %get-tuple-element.12), channel_id=1, source_target_pairs={{0,2},{1,9},{2,0},{3,11},{4,6},{5,13},{6,4},{7,15},{8,10},{9,1},{1... | collective-permute-start | bytes 104456 | tf_op jit(solution)/shard_map/ppermute | solution.py:367
  18.3 1.1 %collective-permute-start.2 = (f32[68,128]{1,0:T(8,128)S(1)}, f32[68,128]{1,0:T(8,128)S(1)}, u32[]{:S(2)}, u32[]{:S(2)}) collective-permute-start(f32[68,128]{1,0:T(8,128)S(1)} %get-tuple-element.13), channel_id=1, source_target_pairs={{0,3},{1,0},{2,1},{3,2},{4,7},{5,4},{6,5},{7,6},{8,11},{9,8},{10,9... | collective-permute-start | bytes 104456 | tf_op jit(solution)/shard_map/ppermute | solution.py:367
  19.4 0.1 collective-permute-start.3
  19.4 0.0 copy-done.1
  19.4 0.1 cell_map.1.refs_5_
  19.6 1.6 %collective-permute-done.refs_1_ = f32[68,128]{1,0:T(8,128)S(1)} collective-permute-done((f32[68,128]{1,0:T(8,128)S(1)}, f32[68,128]{1,0:T(8,128)S(1)}, u32[]{:S(2)}, u32[]{:S(2)}) %collective-permute-start) | collective-permute-done | bytes 34848 | tf_op jit(solution)/shard_map/ppermute | solution.py:367
  21.2 0.7 %collective-permute-done.1.refs_2_ = f32[68,128]{1,0:T(8,128)S(1)} collective-permute-done((f32[68,128]{1,0:T(8,128)S(1)}, f32[68,128]{1,0:T(8,128)S(1)}, u32[]{:S(2)}, u32[]{:S(2)}) %collective-permute-start.1) | collective-permute-done | bytes 34848 | tf_op jit(solution)/shard_map/ppermute | solution.py:367
  21.9 0.6 %collective-permute-done.2.refs_3_ = f32[68,128]{1,0:T(8,128)S(1)} collective-permute-done((f32[68,128]{1,0:T(8,128)S(1)}, f32[68,128]{1,0:T(8,128)S(1)}, u32[]{:S(2)}, u32[]{:S(2)}) %collective-permute-start.2) | collective-permute-done | bytes 34848 | tf_op jit(solution)/shard_map/ppermute | solution.py:367
  22.5 0.0 collective-permute-done.3.refs_4_
  22.5 0.0 copy-done
  22.5 0.8 %cells.1 = f32[2,4096]{1,0:T(2,128)} custom-call(f32[68,128]{1,0:T(8,128)S(1)} %get-tuple-element.10.refs_0_, f32[68,128]{1,0:T(8,128)S(1)} %collective-permute-done.refs_1_, f32[68,128]{1,0:T(8,128)S(1)} %collective-permute-done.1.refs_2_, f32[68,128]{1,0:T(8,128)S(1)} %collective-permute-done.2.refs_3_, f32[68,128]{1,0:T(8,128)S(1)} %collective-permute-done.3.refs_4_, ...), custom_call_target="tpu_custom_call" | custom-call | tf_op jit(solution)/shard_map/cells/pallas_call | solution.py:379
Async XLA Ops:
  0.0 19.4 %copy-start.1 = (s32[2,256]{1,0:T(2,128)S(1)}, s32[2,256]{1,0:T(2,128)}, u32[]{:S(2)}) copy-start(s32[2,256]{1,0:T(2,128)} %cells_ref.1) | copy-start | bytes 6148
  0.0 22.5 %copy-start = (s32[2,256,8]{1,2,0:T(8,128)S(1)}, s32[2,256,8]{1,2,0:T(8,128)}, u32[]{:S(2)}) copy-start(s32[2,256,8]{1,2,0:T(8,128)} %param.17) | copy-start | bytes 49156
  15.3 5.8 %collective-permute-start = (f32[68,128]{1,0:T(8,128)S(1)}, f32[68,128]{1,0:T(8,128)S(1)}, u32[]{:S(2)}, u32[]{:S(2)}) collective-permute-start(f32[68,128]{1,0:T(8,128)S(1)} %get-tuple-element.11), channel_id=1, source_target_pairs={{0,1},{1,3},{2,10},{3,0},{4,5},{5,7},{6,14},{7,4},{8,9},{9,11},{10... | collective-permute-start | bytes 104456 | tf_op jit(solution)/shard_map/ppermute | solution.py:367
  17.0 4.9 %collective-permute-start.1 = (f32[68,128]{1,0:T(8,128)S(1)}, f32[68,128]{1,0:T(8,128)S(1)}, u32[]{:S(2)}, u32[]{:S(2)}) collective-permute-start(f32[68,128]{1,0:T(8,128)S(1)} %get-tuple-element.12), channel_id=1, source_target_pairs={{0,2},{1,9},{2,0},{3,11},{4,6},{5,13},{6,4},{7,15},{8,10},{9,1},{1... | collective-permute-start | bytes 104456 | tf_op jit(solution)/shard_map/ppermute | solution.py:367
  18.3 4.2 %collective-permute-start.2 = (f32[68,128]{1,0:T(8,128)S(1)}, f32[68,128]{1,0:T(8,128)S(1)}, u32[]{:S(2)}, u32[]{:S(2)}) collective-permute-start(f32[68,128]{1,0:T(8,128)S(1)} %get-tuple-element.13), channel_id=1, source_target_pairs={{0,3},{1,0},{2,1},{3,2},{4,7},{5,4},{6,5},{7,6},{8,11},{9,8},{10,9... | collective-permute-start | bytes 104456 | tf_op jit(solution)/shard_map/ppermute | solution.py:367
  19.4 3.1 %collective-permute-start.3 = (f32[68,128]{1,0:T(8,128)S(1)}, f32[68,128]{1,0:T(8,128)S(1)}, u32[]{:S(2)}, u32[]{:S(2)}) collective-permute-start(f32[68,128]{1,0:T(8,128)S(1)} %get-tuple-element.14), channel_id=1, source_target_pairs={{0,8},{1,2},{2,3},{3,1},{4,12},{5,6},{6,7},{7,5},{8,0},{9,10},{10,... | collective-permute-start | bytes 104456 | tf_op jit(solution)/shard_map/ppermute | solution.py:367

commit v23 on v22

--- a/solution.py
+++ b/solution.py
@@ -79,15 +79,12 @@
             )
         )
     ]
-    for copy in lists:
-        copy.start()
-
     tables = [
-        pltpu.make_async_copy(exponents_hbm, exponents_ref, table_sems.at[0]),
-        pltpu.make_async_copy(centres_hbm, centres_ref, table_sems.at[1]),
+        pltpu.make_async_copy(centres_hbm, centres_ref, table_sems.at[0]),
+        pltpu.make_async_copy(exponents_hbm, exponents_ref, table_sems.at[1]),
         pltpu.make_async_copy(blocks_hbm, blocks_ref, table_sems.at[2]),
     ]
-    for copy in tables:
+    for copy in tables + lists:
         copy.start()
     for copy in lists + tables:
         copy.wait()
@@ -189,25 +186,21 @@
         out_ref[pl.ds(slot * SLOT_ROWS + ROWS, 1), :] = tagged
 
 
-def group_kernel(items, bricks_dev, moves, in_ref, *outs):
+def group_kernel(items, bricks_dev, moves, in_ref, *refs):
+    *outs, sums_ref = refs
     me = lax.axis_index("basis")
     slots = in_ref.shape[0] // SLOT_ROWS
     meta = [in_ref[n * SLOT_ROWS + ROWS : (n + 1) * SLOT_ROWS, :] for n in range(slots)]
     tags = [jnp.broadcast_to(line[:, LANES - 1 :], (ROWS, LANES)) for line in meta]
-    owned = sum(jnp.where(me == i, i, 0) for i in range(len(moves[0])))
-    sends = []
-    for out, move in zip(outs, [None, *moves]):
-        owner = owned
-        if move is not None:
-            owner = sum(jnp.where(me == i, -1 if i == to else to, 0) for i, to in enumerate(move))
-        sends.append(owner)
-        for b in range(bricks_dev):
-            brick = jnp.where(owner < 0, -2, owner * bricks_dev + b).astype(jnp.float32)
-            total = jnp.zeros((ROWS, LANES), jnp.float32)
-            for n in range(slots):
-                dens = in_ref[n * SLOT_ROWS : n * SLOT_ROWS + ROWS, :]
-                total = total + jnp.where(tags[n] == brick, dens, 0.0)
-            out[b * ROWS : (b + 1) * ROWS, :] = total
+    owners = len(moves[0])
+    for brick in range(owners * bricks_dev):
+        total = jnp.zeros((ROWS, LANES), jnp.float32)
+        for n in range(slots):
+            dens = in_ref[n * SLOT_ROWS : n * SLOT_ROWS + ROWS, :]
+            total = total + jnp.where(tags[n] == float(brick), dens, 0.0)
+        first = brick % bricks_dev * ROWS
+        sums_ref[brick // bricks_dev, first : first + ROWS, :] = total
+    sums_ref[owners] = jnp.zeros(sums_ref.shape[1:], jnp.float32)
     table_rows = outs[0].shape[0] - bricks_dev * ROWS
     shape = (TILE, LANES)
     lane = iota(shape, 1)
@@ -221,8 +214,15 @@
             for r in range(table_rows):
                 lines[r] = lines[r] + jnp.where(brick >> 4 == r, values, 0.0)
     table = jnp.concatenate([jnp.sum(line, axis=0, keepdims=True) for line in lines], axis=0)
-    for out, owner in zip(outs, sends):
-        out[bricks_dev * ROWS :, :] = jnp.where(owner < 0, 0.0, table)
+    for owner in range(owners):
+        sums_ref[owner, bricks_dev * ROWS :, :] = table
+    for out, move in zip(outs, [range(owners), *moves]):
+        stays = out is not outs[0]
+        to = sum(
+            jnp.where(me == i, owners if stays and i == owner else owner, 0)
+            for i, owner in enumerate(move)
+        )
+        out[...] = sums_ref[to]
 
 
 def map_kernel(cells_ref, out_ref):
@@ -360,6 +360,9 @@
         * (len(moves) + 1),
         in_specs=[vmem()],
         out_specs=[vmem()] * (len(moves) + 1),
+        scratch_shapes=[
+            pltpu.VMEM((owners + 1, bricks_dev * ROWS + table_rows, LANES), jnp.float32)
+        ],
         compiler_params=params,
         name="group_sum",
     )(arrived)

time: 23.5 us -> 23.5 us (level)
  no operation moved by 1% of the time
where the time goes in v23:
time: 23.5 us; the launch traced here: 23.3 us
  blocking collectives  9.9 us (42%)
  Pallas kernels  6.38 us (27%)
  starting transfers between devices  4.11 us (17%)
  waiting for transfers between devices  2.9 us (12%)
    all_to_all x1, blocking collectives, body(): lax.all_to_all(outgoing.reshape(slots, 1, SLOT_ROWS * LANES), ('row', 'co...  9.9 us
    pallas_call x1, Pallas kernels, body(): pl.pallas_call(functools.partial(pair_kernel, slot_depth, bricks_group),...  5.19 us
    ppermute x4, starting transfers between devices, body(): lax.ppermute(piece, ('row', 'col', 'basis'), pairs_of(move, rows, cols))  4.11 us
    ppermute x4, waiting for transfers between devices, body(): lax.ppermute(piece, ('row', 'col', 'basis'), pairs_of(move, rows, cols))  2.9 us
    pallas_call x1, Pallas kernels, body(): pl.pallas_call(cell_kernel, out_shape=jax.ShapeDtypeStruct((bricks_dev, E...  0.84 us
  transfers between devices with their start and end apart: 4, of which 3 were waited for; matrix products, arithmetic and copies ran while one was open for 0% of the time, Pallas kernels for 1%

profile of v23, /device:TPU:0, one launch (start us, length us, event | category | flops | bytes accessed | tf_op | source)
XLA Modules:
  0.0 23.3 jit_solution(16873216150654490608)
XLA Ops:
  0.0 0.0 copy-start.1
  0.0 0.0 copy-start
  0.0 5.2 %pair_density.1 = f32[264,128]{1,0:T(8,128)S(1)} custom-call(s32[2,8]{1,0:T(2,128)} %bitcast.9, s32[8]{0:T(128)} %dest_hbm.1, s32[8]{0:T(128)} %tag_hbm.1, s32[64]{0:T(128)} %levels_hbm.1, bf16[8,128,128]{2,1,0:T(8,128)(2,1)} %blocks_hbm.1, f32[3,1024,128]{2,1,0:T(8,128)} %bitcast.8, f32[1024,128]{1,0:T(8,128)} %exponents_hbm.1), custom_call_target="tpu_custom_call" | custom-call | tf_op jit(solution)/shard_map/pair_density/pallas_call | solution.py:314
  5.2 9.9 %all_to_all.5 = f32[8,1,4224]{2,1,0:T(1,128)S(1)} all-to-all(f32[8,1,4224]{2,1,0:T(1,128)S(1)} %bitcast.5), channel_id=1, replica_groups=mesh['row'=4,'col'=2,'basis'=4] {'row','col'}, dimensions={0} | all-to-all | bytes 270336 | tf_op jit(solution)/shard_map/all_to_all | solution.py:348
  15.1 0.2 group_sum.1
  15.3 1.7 %collective-permute-start = (f32[68,128]{1,0:T(8,128)S(1)}, f32[68,128]{1,0:T(8,128)S(1)}, u32[]{:S(2)}, u32[]{:S(2)}) collective-permute-start(f32[68,128]{1,0:T(8,128)S(1)} %get-tuple-element.11), channel_id=1, source_target_pairs={{0,1},{1,3},{2,10},{3,0},{4,5},{5,7},{6,14},{7,4},{8,9},{9,11},{10... | collective-permute-start | bytes 104456 | tf_op jit(solution)/shard_map/ppermute | solution.py:370
  17.0 1.3 %collective-permute-start.1 = (f32[68,128]{1,0:T(8,128)S(1)}, f32[68,128]{1,0:T(8,128)S(1)}, u32[]{:S(2)}, u32[]{:S(2)}) collective-permute-start(f32[68,128]{1,0:T(8,128)S(1)} %get-tuple-element.12), channel_id=1, source_target_pairs={{0,2},{1,9},{2,0},{3,11},{4,6},{5,13},{6,4},{7,15},{8,10},{9,1},{1... | collective-permute-start | bytes 104456 | tf_op jit(solution)/shard_map/ppermute | solution.py:370
  18.3 1.1 %collective-permute-start.2 = (f32[68,128]{1,0:T(8,128)S(1)}, f32[68,128]{1,0:T(8,128)S(1)}, u32[]{:S(2)}, u32[]{:S(2)}) collective-permute-start(f32[68,128]{1,0:T(8,128)S(1)} %get-tuple-element.13), channel_id=1, source_target_pairs={{0,3},{1,0},{2,1},{3,2},{4,7},{5,4},{6,5},{7,6},{8,11},{9,8},{10,9... | collective-permute-start | bytes 104456 | tf_op jit(solution)/shard_map/ppermute | solution.py:370
  19.3 0.1 collective-permute-start.3
  19.4 0.0 copy-done.1
  19.4 0.1 cell_map.1.refs_5_
  19.6 1.6 %collective-permute-done.refs_1_ = f32[68,128]{1,0:T(8,128)S(1)} collective-permute-done((f32[68,128]{1,0:T(8,128)S(1)}, f32[68,128]{1,0:T(8,128)S(1)}, u32[]{:S(2)}, u32[]{:S(2)}) %collective-permute-start) | collective-permute-done | bytes 34848 | tf_op jit(solution)/shard_map/ppermute | solution.py:370
  21.1 0.7 %collective-permute-done.1.refs_2_ = f32[68,128]{1,0:T(8,128)S(1)} collective-permute-done((f32[68,128]{1,0:T(8,128)S(1)}, f32[68,128]{1,0:T(8,128)S(1)}, u32[]{:S(2)}, u32[]{:S(2)}) %collective-permute-start.1) | collective-permute-done | bytes 34848 | tf_op jit(solution)/shard_map/ppermute | solution.py:370
  21.9 0.6 %collective-permute-done.2.refs_3_ = f32[68,128]{1,0:T(8,128)S(1)} collective-permute-done((f32[68,128]{1,0:T(8,128)S(1)}, f32[68,128]{1,0:T(8,128)S(1)}, u32[]{:S(2)}, u32[]{:S(2)}) %collective-permute-start.2) | collective-permute-done | bytes 34848 | tf_op jit(solution)/shard_map/ppermute | solution.py:370
  22.5 0.0 collective-permute-done.3.refs_4_
  22.5 0.0 copy-done
  22.5 0.8 %cells.1 = f32[2,4096]{1,0:T(2,128)} custom-call(f32[68,128]{1,0:T(8,128)S(1)} %get-tuple-element.10.refs_0_, f32[68,128]{1,0:T(8,128)S(1)} %collective-permute-done.refs_1_, f32[68,128]{1,0:T(8,128)S(1)} %collective-permute-done.1.refs_2_, f32[68,128]{1,0:T(8,128)S(1)} %collective-permute-done.2.refs_3_, f32[68,128]{1,0:T(8,128)S(1)} %collective-permute-done.3.refs_4_, ...), custom_call_target="tpu_custom_call" | custom-call | tf_op jit(solution)/shard_map/cells/pallas_call | solution.py:382
Async XLA Ops:
  0.0 19.4 %copy-start.1 = (s32[2,256]{1,0:T(2,128)S(1)}, s32[2,256]{1,0:T(2,128)}, u32[]{:S(2)}) copy-start(s32[2,256]{1,0:T(2,128)} %cells_ref.1) | copy-start | bytes 6148
  0.0 22.5 %copy-start = (s32[2,256,8]{1,2,0:T(8,128)S(1)}, s32[2,256,8]{1,2,0:T(8,128)}, u32[]{:S(2)}) copy-start(s32[2,256,8]{1,2,0:T(8,128)} %param.17) | copy-start | bytes 49156
  15.3 5.8 %collective-permute-start = (f32[68,128]{1,0:T(8,128)S(1)}, f32[68,128]{1,0:T(8,128)S(1)}, u32[]{:S(2)}, u32[]{:S(2)}) collective-permute-start(f32[68,128]{1,0:T(8,128)S(1)} %get-tuple-element.11), channel_id=1, source_target_pairs={{0,1},{1,3},{2,10},{3,0},{4,5},{5,7},{6,14},{7,4},{8,9},{9,11},{10... | collective-permute-start | bytes 104456 | tf_op jit(solution)/shard_map/ppermute | solution.py:370
  17.0 4.9 %collective-permute-start.1 = (f32[68,128]{1,0:T(8,128)S(1)}, f32[68,128]{1,0:T(8,128)S(1)}, u32[]{:S(2)}, u32[]{:S(2)}) collective-permute-start(f32[68,128]{1,0:T(8,128)S(1)} %get-tuple-element.12), channel_id=1, source_target_pairs={{0,2},{1,9},{2,0},{3,11},{4,6},{5,13},{6,4},{7,15},{8,10},{9,1},{1... | collective-permute-start | bytes 104456 | tf_op jit(solution)/shard_map/ppermute | solution.py:370
  18.3 4.2 %collective-permute-start.2 = (f32[68,128]{1,0:T(8,128)S(1)}, f32[68,128]{1,0:T(8,128)S(1)}, u32[]{:S(2)}, u32[]{:S(2)}) collective-permute-start(f32[68,128]{1,0:T(8,128)S(1)} %get-tuple-element.13), channel_id=1, source_target_pairs={{0,3},{1,0},{2,1},{3,2},{4,7},{5,4},{6,5},{7,6},{8,11},{9,8},{10,9... | collective-permute-start | bytes 104456 | tf_op jit(solution)/shard_map/ppermute | solution.py:370
  19.3 3.1 %collective-permute-start.3 = (f32[68,128]{1,0:T(8,128)S(1)}, f32[68,128]{1,0:T(8,128)S(1)}, u32[]{:S(2)}, u32[]{:S(2)}) collective-permute-start(f32[68,128]{1,0:T(8,128)S(1)} %get-tuple-element.14), channel_id=1, source_target_pairs={{0,8},{1,2},{2,3},{3,1},{4,12},{5,6},{6,7},{7,5},{8,0},{9,10},{10,... | collective-permute-start | bytes 104456 | tf_op jit(solution)/shard_map/ppermute | solution.py:370

commit v24 on v23

--- a/solution.py
+++ b/solution.py
@@ -242,7 +242,7 @@
 
 
 def cell_kernel(*refs):
-    *ins, map_ref, refs_ref, out_ref = refs
+    *ins, map_ref, refs_ref, out_hbm, out_ref, sems = refs
     bricks_dev, _, cells = refs_ref.shape
     total = ins[0][...]
     for part in ins[1:]:
@@ -261,6 +261,7 @@
             for c, index in enumerate(refs[b]):
                 found = lane_pick(line, (index & (LANES - 1)))
                 picked[b][c] = jnp.where(index >> SHIFT == r, found, picked[b][c])
+    results = []
     for b in range(bricks_dev):
         cell = map_ref[b]
         mean = jnp.zeros((ROWS, LANES), jnp.float32)
@@ -269,9 +270,20 @@
             found = lane_pick(jnp.broadcast_to(line, (ROWS, LANES)), (cell & (LANES - 1)))
             mean = jnp.where(cell >> SHIFT == c, found, mean)
         own = total[b * ROWS : (b + 1) * ROWS]
-        result = jnp.where(cell >= 0, 0.5 * own + mean, own)
-        for row in range(ROWS):
-            out_ref[b : b + 1, row * LANES : (row + 1) * LANES] = result[row : row + 1, :]
+        results.append(jnp.where(cell >= 0, 0.5 * own + mean, own))
+    copies = []
+    for part in range(2):
+        span = ROWS // 2
+        for b, result in enumerate(results):
+            for row in range(part * span, (part + 1) * span):
+                out_ref[b : b + 1, row * LANES : (row + 1) * LANES] = result[row : row + 1, :]
+        lanes = pl.ds(part * span * LANES, span * LANES)
+        copies.append(
+            pltpu.make_async_copy(out_ref.at[:, lanes], out_hbm.at[:, lanes], sems.at[part])
+        )
+        copies[-1].start()
+    for copy in copies:
+        copy.wait()
 
 
 def moves_of(rows, owners):
@@ -383,7 +395,11 @@
         cell_kernel,
         out_shape=jax.ShapeDtypeStruct((bricks_dev, EDGE * FACE), jnp.float32),
         in_specs=[vmem()] * (len(parts) + 2),
-        out_specs=vmem(),
+        out_specs=pl.BlockSpec(memory_space=pltpu.HBM),
+        scratch_shapes=[
+            pltpu.VMEM((bricks_dev, EDGE * FACE), jnp.float32),
+            pltpu.SemaphoreType.DMA((2,)),
+        ],
         compiler_params=params,
         name="cells",
     )(*parts, cell_map, jnp.transpose(corner_refs, (0, 2, 1)))

time: 23.5 us -> 23.5 us (level)
  no operation moved by 1% of the time
where the time goes in v24:
time: 23.5 us; the launch traced here: 23.3 us
  blocking collectives  9.9 us (42%)
  Pallas kernels  6.42 us (27%)
  starting transfers between devices  4.14 us (18%)
  waiting for transfers between devices  2.84 us (12%)
    all_to_all x1, blocking collectives, body(): lax.all_to_all(outgoing.reshape(slots, 1, SLOT_ROWS * LANES), ('row', 'co...  9.9 us
    pallas_call x1, Pallas kernels, body(): pl.pallas_call(functools.partial(pair_kernel, slot_depth, bricks_group),...  5.22 us
    ppermute x4, starting transfers between devices, body(): lax.ppermute(piece, ('row', 'col', 'basis'), pairs_of(move, rows, cols))  4.14 us
    ppermute x4, waiting for transfers between devices, body(): lax.ppermute(piece, ('row', 'col', 'basis'), pairs_of(move, rows, cols))  2.84 us
    pallas_call x1, Pallas kernels, body(): pl.pallas_call(cell_kernel, out_shape=jax.ShapeDtypeStruct((bricks_dev, E...  0.85 us
  transfers between devices with their start and end apart: 4, of which 3 were waited for; matrix products, arithmetic and copies ran while one was open for 0% of the time, Pallas kernels for 1%

profile of v24, /device:TPU:0, one launch (start us, length us, event | category | flops | bytes accessed | tf_op | source)
XLA Modules:
  0.0 23.3 jit_solution(10956847817487959244)
XLA Ops:
  0.0 0.0 copy-start.1
  0.0 0.0 copy-start
  0.0 5.2 %pair_density.1 = f32[264,128]{1,0:T(8,128)S(1)} custom-call(s32[2,8]{1,0:T(2,128)} %bitcast.9, s32[8]{0:T(128)} %dest_hbm.1, s32[8]{0:T(128)} %tag_hbm.1, s32[64]{0:T(128)} %levels_hbm.1, bf16[8,128,128]{2,1,0:T(8,128)(2,1)} %blocks_hbm.1, f32[3,1024,128]{2,1,0:T(8,128)} %bitcast.8, f32[1024,128]{1,0:T(8,128)} %exponents_hbm.1), custom_call_target="tpu_custom_call" | custom-call | tf_op jit(solution)/shard_map/pair_density/pallas_call | solution.py:326
  5.2 9.9 %all_to_all.5 = f32[8,1,4224]{2,1,0:T(1,128)S(1)} all-to-all(f32[8,1,4224]{2,1,0:T(1,128)S(1)} %bitcast.5), channel_id=1, replica_groups=mesh['row'=4,'col'=2,'basis'=4] {'row','col'}, dimensions={0} | all-to-all | bytes 270336 | tf_op jit(solution)/shard_map/all_to_all | solution.py:360
  15.1 0.2 group_sum.1
  15.3 1.6 %collective-permute-start = (f32[68,128]{1,0:T(8,128)S(1)}, f32[68,128]{1,0:T(8,128)S(1)}, u32[]{:S(2)}, u32[]{:S(2)}) collective-permute-start(f32[68,128]{1,0:T(8,128)S(1)} %get-tuple-element.11), channel_id=1, source_target_pairs={{0,1},{1,3},{2,10},{3,0},{4,5},{5,7},{6,14},{7,4},{8,9},{9,11},{10... | collective-permute-start | bytes 104456 | tf_op jit(solution)/shard_map/ppermute | solution.py:382
  17.0 1.3 %collective-permute-start.1 = (f32[68,128]{1,0:T(8,128)S(1)}, f32[68,128]{1,0:T(8,128)S(1)}, u32[]{:S(2)}, u32[]{:S(2)}) collective-permute-start(f32[68,128]{1,0:T(8,128)S(1)} %get-tuple-element.12), channel_id=1, source_target_pairs={{0,2},{1,9},{2,0},{3,11},{4,6},{5,13},{6,4},{7,15},{8,10},{9,1},{1... | collective-permute-start | bytes 104456 | tf_op jit(solution)/shard_map/ppermute | solution.py:382
  18.2 1.1 %collective-permute-start.2 = (f32[68,128]{1,0:T(8,128)S(1)}, f32[68,128]{1,0:T(8,128)S(1)}, u32[]{:S(2)}, u32[]{:S(2)}) collective-permute-start(f32[68,128]{1,0:T(8,128)S(1)} %get-tuple-element.13), channel_id=1, source_target_pairs={{0,3},{1,0},{2,1},{3,2},{4,7},{5,4},{6,5},{7,6},{8,11},{9,8},{10,9... | collective-permute-start | bytes 104456 | tf_op jit(solution)/shard_map/ppermute | solution.py:382
  19.3 0.1 collective-permute-start.3
  19.5 0.0 copy-done.1
  19.5 0.1 cell_map.1.refs_5_
  19.6 1.5 %collective-permute-done.refs_1_ = f32[68,128]{1,0:T(8,128)S(1)} collective-permute-done((f32[68,128]{1,0:T(8,128)S(1)}, f32[68,128]{1,0:T(8,128)S(1)}, u32[]{:S(2)}, u32[]{:S(2)}) %collective-permute-start) | collective-permute-done | bytes 34848 | tf_op jit(solution)/shard_map/ppermute | solution.py:382
  21.2 0.7 %collective-permute-done.1.refs_2_ = f32[68,128]{1,0:T(8,128)S(1)} collective-permute-done((f32[68,128]{1,0:T(8,128)S(1)}, f32[68,128]{1,0:T(8,128)S(1)}, u32[]{:S(2)}, u32[]{:S(2)}) %collective-permute-start.1) | collective-permute-done | bytes 34848 | tf_op jit(solution)/shard_map/ppermute | solution.py:382
  21.9 0.6 %collective-permute-done.2.refs_3_ = f32[68,128]{1,0:T(8,128)S(1)} collective-permute-done((f32[68,128]{1,0:T(8,128)S(1)}, f32[68,128]{1,0:T(8,128)S(1)}, u32[]{:S(2)}, u32[]{:S(2)}) %collective-permute-start.2) | collective-permute-done | bytes 34848 | tf_op jit(solution)/shard_map/ppermute | solution.py:382
  22.5 0.0 collective-permute-done.3.refs_4_
  22.5 0.0 copy-done
  22.5 0.8 %cells.1 = f32[2,4096]{1,0:T(2,128)} custom-call(f32[68,128]{1,0:T(8,128)S(1)} %get-tuple-element.10.refs_0_, f32[68,128]{1,0:T(8,128)S(1)} %collective-permute-done.refs_1_, f32[68,128]{1,0:T(8,128)S(1)} %collective-permute-done.1.refs_2_, f32[68,128]{1,0:T(8,128)S(1)} %collective-permute-done.2.refs_3_, f32[68,128]{1,0:T(8,128)S(1)} %collective-permute-done.3.refs_4_, ...), custom_call_target="tpu_custom_call" | custom-call | tf_op jit(solution)/shard_map/cells/pallas_call | solution.py:394
Async XLA Ops:
  0.0 19.5 %copy-start.1 = (s32[2,256]{1,0:T(2,128)S(1)}, s32[2,256]{1,0:T(2,128)}, u32[]{:S(2)}) copy-start(s32[2,256]{1,0:T(2,128)} %cells_ref.1) | copy-start | bytes 6148
  0.0 22.5 %copy-start = (s32[2,256,8]{1,2,0:T(8,128)S(1)}, s32[2,256,8]{1,2,0:T(8,128)}, u32[]{:S(2)}) copy-start(s32[2,256,8]{1,2,0:T(8,128)} %param.17) | copy-start | bytes 49156
  15.3 5.8 %collective-permute-start = (f32[68,128]{1,0:T(8,128)S(1)}, f32[68,128]{1,0:T(8,128)S(1)}, u32[]{:S(2)}, u32[]{:S(2)}) collective-permute-start(f32[68,128]{1,0:T(8,128)S(1)} %get-tuple-element.11), channel_id=1, source_target_pairs={{0,1},{1,3},{2,10},{3,0},{4,5},{5,7},{6,14},{7,4},{8,9},{9,11},{10... | collective-permute-start | bytes 104456 | tf_op jit(solution)/shard_map/ppermute | solution.py:382
  17.0 4.9 %collective-permute-start.1 = (f32[68,128]{1,0:T(8,128)S(1)}, f32[68,128]{1,0:T(8,128)S(1)}, u32[]{:S(2)}, u32[]{:S(2)}) collective-permute-start(f32[68,128]{1,0:T(8,128)S(1)} %get-tuple-element.12), channel_id=1, source_target_pairs={{0,2},{1,9},{2,0},{3,11},{4,6},{5,13},{6,4},{7,15},{8,10},{9,1},{1... | collective-permute-start | bytes 104456 | tf_op jit(solution)/shard_map/ppermute | solution.py:382
  18.2 4.2 %collective-permute-start.2 = (f32[68,128]{1,0:T(8,128)S(1)}, f32[68,128]{1,0:T(8,128)S(1)}, u32[]{:S(2)}, u32[]{:S(2)}) collective-permute-start(f32[68,128]{1,0:T(8,128)S(1)} %get-tuple-element.13), channel_id=1, source_target_pairs={{0,3},{1,0},{2,1},{3,2},{4,7},{5,4},{6,5},{7,6},{8,11},{9,8},{10,9... | collective-permute-start | bytes 104456 | tf_op jit(solution)/shard_map/ppermute | solution.py:382
  19.3 3.1 %collective-permute-start.3 = (f32[68,128]{1,0:T(8,128)S(1)}, f32[68,128]{1,0:T(8,128)S(1)}, u32[]{:S(2)}, u32[]{:S(2)}) collective-permute-start(f32[68,128]{1,0:T(8,128)S(1)} %get-tuple-element.14), channel_id=1, source_target_pairs={{0,8},{1,2},{2,3},{3,1},{4,12},{5,6},{6,7},{7,5},{8,0},{9,10},{10,... | collective-permute-start | bytes 104456 | tf_op jit(solution)/shard_map/ppermute | solution.py:382
